TPU v7x, 32 devices: a whole 2x2x4 slice. The times are simulated.
32 devices in a mesh: batch: 16 (over z, x, core), seq: 2 (over y).
Axes of the slice: x: 2, y: 2, z: 4, core: 2. Of those that a mesh axis runs over, the one named last changes fastest.
Arguments:
- clips_in: bfloat16 [32, 16, 14, 14, 512], P('batch', 'seq'), may hold values from -28 to 28
- cotangent: bfloat16 [32, 16, 14, 14, 512], P('batch', 'seq'), may hold values from -6 to 6
- offset_index: int32 [392, 392], replicated, may hold values from 0 to 2534, as said below
- first_gain: bfloat16 [2, 512], P(None, ('batch', 'seq')), may hold values from 0.5 to 1.5
- first_shift: bfloat16 [2, 512], P(None, ('batch', 'seq')), may hold values from -1 to 1
- inner_weight: bfloat16 [2, 512, 1536], P(None, ('batch', 'seq')), may hold values from -0.25 to 0.25
- inner_bias: bfloat16 [2, 1024], P(None, ('batch', 'seq')), may hold values from -0.5 to 0.5
- outer_weight: bfloat16 [2, 512, 512], P(None, ('batch', 'seq')), may hold values from -3 to 3
- outer_bias: bfloat16 [2, 512], P(None, ('batch', 'seq')), may hold values from -1 to 1
- second_gain: bfloat16 [2, 512], P(None, ('batch', 'seq')), may hold values from 0.5 to 1.5
- second_shift: bfloat16 [2, 512], P(None, ('batch', 'seq')), may hold values from -1 to 1
- up_weight: bfloat16 [2, 512, 2048], P(None, ('batch', 'seq')), may hold values from -0.25 to 0.25
- up_bias: bfloat16 [2, 2048], P(None, ('batch', 'seq')), may hold values from -1 to 1
- down_weight: bfloat16 [2, 2048, 512], P(None, ('batch', 'seq')), may hold values from -0.125 to 0.125
- down_bias: bfloat16 [2, 512], P(None, ('batch', 'seq')), may hold values from -1 to 1
- bias_table: float32 [2, 2535, 16], replicated, may hold values from -3 to 3
Outputs:
- clips_out: bfloat16 [32, 16, 14, 14, 512], P('batch', 'seq')
- clips_grad: bfloat16 [32, 16, 14, 14, 512], P('batch', 'seq')
- grad_first_gain: float32 [2, 512], P(None, ('batch', 'seq'))
- grad_first_shift: float32 [2, 512], P(None, ('batch', 'seq'))
- grad_inner_weight: float32 [2, 512, 1536], P(None, ('batch', 'seq'))
- grad_inner_bias: float32 [2, 1024], P(None, ('batch', 'seq'))
- grad_outer_weight: float32 [2, 512, 512], P(None, ('batch', 'seq'))
- grad_outer_bias: float32 [2, 512], P(None, ('batch', 'seq'))
- grad_second_gain: float32 [2, 512], P(None, ('batch', 'seq'))
- grad_second_shift: float32 [2, 512], P(None, ('batch', 'seq'))
- grad_up_weight: float32 [2, 512, 2048], P(None, ('batch', 'seq'))
- grad_up_bias: float32 [2, 2048], P(None, ('batch', 'seq'))
- grad_down_weight: float32 [2, 2048, 512], P(None, ('batch', 'seq'))
- grad_down_bias: float32 [2, 512], P(None, ('batch', 'seq'))
- grad_bias_table: float32 [2, 2535, 16], replicated
Inputs may be any that keep to these rules, and one draw needn't show every extreme that they name: `offset_index`: entry (i, j) is the bias table row of the offset between window positions i and j; two pairs share a row exactly when their offsets are equal.
All inputs are finite; a program needn't handle non-finite values.
Results may differ from a plain program's by a relative error of at most 0.015.
Values may be sent and summed in bfloat16 or wider, within the bound.
A program may use at most 896 MiB of HBM per device.

v0:
```python
import jax
import jax.numpy as jnp
from jax import lax
from jax.sharding import PartitionSpec as P

D = 512
HEADS = 16
HD = 32
WT = 8
WH = 7
WW = 7
FRAMES = 16
HGT = 14
WID = 14
LAYERS = 2
SHIFT_T = 4
SHIFT_S = 3
WIN = 392
BIAS_ROWS = 2535


EPSILON = 1e-05
MASKED = -100.0


def norm_rows(values, gain, shift):
    average = jnp.mean(values, axis=-1, keepdims=True)
    centred = values - average
    spread = jnp.mean(centred * centred, axis=-1, keepdims=True)
    return centred * lax.rsqrt(spread + EPSILON) * gain + shift


def exact_gelu(values):
    return jax.nn.gelu(values, approximate=False)


def region_of(places, extent, window, offset):
    return (places >= extent - window).astype(jnp.int32) + (places >= extent - offset).astype(
        jnp.int32
    )


def region_grid():
    time_region = region_of(jnp.arange(FRAMES, dtype=jnp.int32), FRAMES, WT, SHIFT_T)
    row_region = region_of(jnp.arange(HGT, dtype=jnp.int32), HGT, WH, SHIFT_S)
    col_region = region_of(jnp.arange(WID, dtype=jnp.int32), WID, WW, SHIFT_S)
    return (time_region[:, None, None] * 3 + row_region[None, :, None]) * 3 + col_region[
        None, None, :
    ]


def weight_grad(inputs, grads):
    return lax.dot_general(
        inputs.reshape(-1, inputs.shape[-1]),
        grads.reshape(-1, grads.shape[-1]),
        (((0,), (0,)), ((), ())),
        preferred_element_type=jnp.float32,
    )


def input_grad(grads, matrix):
    return lax.dot_general(
        grads, matrix, (((grads.ndim - 1,), (1,)), ((), ())), preferred_element_type=jnp.float32
    )


def token_sum(values):
    return jnp.sum(values.astype(jnp.float32), axis=tuple(range(values.ndim - 1)))


def spatial_blocks(field):
    clip_count, frames_here, width = (field.shape[0], field.shape[1], field.shape[-1])
    shaped = field.reshape(clip_count, frames_here, HGT // WH, WH, WID // WW, WW, width)
    shaped = shaped.transpose(0, 2, 4, 1, 3, 5, 6)
    return shaped.reshape(clip_count * (HGT // WH) * (WID // WW), frames_here, WH * WW, width)


def frames_from(columns, clip_count, shifted):
    frames_here, width = (columns.shape[1], columns.shape[-1])
    shaped = columns.reshape(clip_count, HGT // WH, WID // WW, frames_here, WH, WW, width)
    shaped = shaped.transpose(0, 3, 1, 4, 2, 5, 6)
    field = shaped.reshape(clip_count, frames_here, HGT, WID, width)
    if shifted:
        field = jnp.roll(field, (SHIFT_S, SHIFT_S), axis=(2, 3))
    return field


def column_windows(columns, shifted):
    if shifted:
        columns = jnp.roll(columns, -SHIFT_T, axis=1)
    return columns.reshape(columns.shape[0] * (FRAMES // WT), WIN, columns.shape[-1])


def window_columns(windows, shifted):
    columns = windows.reshape(-1, FRAMES, WH * WW, windows.shape[-1])
    if shifted:
        columns = jnp.roll(columns, SHIFT_T, axis=1)
    return columns


def send_triple(triple, shifted):
    if shifted:
        triple = tuple((jnp.roll(member, (-SHIFT_S, -SHIFT_S), axis=(2, 3)) for member in triple))
    blocks = tuple((spatial_blocks(member) for member in triple))
    arrived = (
        lax.all_to_all(blocks[0], "seq", split_axis=0, concat_axis=1, tiled=True),
        lax.all_to_all(blocks[1], "seq", split_axis=0, concat_axis=1, tiled=True),
        lax.all_to_all(blocks[2], "seq", split_axis=0, concat_axis=1, tiled=True),
    )
    return tuple((column_windows(member, shifted) for member in arrived))


def return_output(windows, clip_count, shifted):
    arrived = lax.all_to_all(
        window_columns(windows, shifted), "seq", split_axis=1, concat_axis=0, tiled=True
    )
    return frames_from(arrived, clip_count, shifted)


def send_grad(field, shifted):
    if shifted:
        field = jnp.roll(field, (-SHIFT_S, -SHIFT_S), axis=(2, 3))
    arrived = lax.all_to_all(spatial_blocks(field), "seq", split_axis=0, concat_axis=1, tiled=True)
    return column_windows(arrived, shifted)


def return_grads(triple, clip_count, shifted):
    columns = tuple((window_columns(member, shifted) for member in triple))
    arrived = (
        lax.all_to_all(columns[0], "seq", split_axis=1, concat_axis=0, tiled=True),
        lax.all_to_all(columns[1], "seq", split_axis=1, concat_axis=0, tiled=True),
        lax.all_to_all(columns[2], "seq", split_axis=1, concat_axis=0, tiled=True),
    )
    return tuple((frames_from(member, clip_count, shifted) for member in arrived))


def window_extra(column_count):
    block_count = HGT // WH * (WID // WW)
    blocks = region_grid().reshape(FRAMES, HGT // WH, WH, WID // WW, WW).transpose(1, 3, 0, 2, 4)
    blocks = blocks.reshape(block_count, FRAMES, WH * WW)
    first_column = lax.axis_index("seq") * column_count
    which = (first_column + jnp.arange(column_count, dtype=jnp.int32)) % block_count
    chosen = jnp.take(blocks, which, axis=0).reshape(column_count * (FRAMES // WT), WIN)
    same = chosen[:, :, None] == chosen[:, None, :]
    return jnp.where(same, 0.0, MASKED).astype(jnp.float32)


def window_total(head_query, head_keys, bias_heads, extra):
    total = jnp.einsum("wqhd,wkhd->whqk", head_query, head_keys, preferred_element_type=jnp.float32)
    total = total + bias_heads[None]
    if extra is not None:
        total = total + extra[:, None]
    return total


def attend_forward(query, keys, values, bias_heads, extra):
    head_shape = (query.shape[0], WIN, HEADS, HD)
    total = window_total(query.reshape(head_shape), keys.reshape(head_shape), bias_heads, extra)
    peak = jnp.max(total, axis=-1, keepdims=True)
    exponent = jnp.exp(total - peak)
    summed = jnp.sum(exponent, axis=-1, keepdims=True)
    soft_low = (exponent / summed).astype(jnp.bfloat16)
    output = jnp.einsum(
        "whqk,wkhd->wqhd", soft_low, values.reshape(head_shape), preferred_element_type=jnp.float32
    )
    return (output.reshape(query.shape[0], WIN, D).astype(jnp.bfloat16), peak + jnp.log(summed))


def attend_backward(query, keys, values, log_total, bias_heads, extra, grad_output):
    head_shape = (query.shape[0], WIN, HEADS, HD)
    head_query = query.reshape(head_shape)
    head_keys = keys.reshape(head_shape)
    head_values = values.reshape(head_shape)
    grad_heads = grad_output.reshape(head_shape)
    soft = jnp.exp(window_total(head_query, head_keys, bias_heads, extra) - log_total)
    soft_grad = jnp.einsum(
        "wqhd,wkhd->whqk", grad_heads, head_values, preferred_element_type=jnp.float32
    )
    values_grad = jnp.einsum(
        "whqk,wqhd->wkhd", soft.astype(jnp.bfloat16), grad_heads, preferred_element_type=jnp.float32
    )
    inner = jnp.sum(soft * soft_grad, axis=-1, keepdims=True)
    total_grad = soft * (soft_grad - inner)
    total_low = total_grad.astype(jnp.bfloat16)
    query_grad = jnp.einsum(
        "whqk,wkhd->wqhd", total_low, head_keys, preferred_element_type=jnp.float32
    )
    keys_grad = jnp.einsum(
        "whqk,wqhd->wkhd", total_low, head_query, preferred_element_type=jnp.float32
    )
    flat_shape = (query.shape[0], WIN, D)
    return (
        query_grad.reshape(flat_shape).astype(jnp.bfloat16),
        keys_grad.reshape(flat_shape).astype(jnp.bfloat16),
        values_grad.reshape(flat_shape).astype(jnp.bfloat16),
        jnp.sum(total_grad, axis=0),
    )


def per_device(
    clips_in,
    cotangent,
    offset_index,
    first_gain,
    first_shift,
    inner_weight,
    inner_bias,
    outer_weight,
    outer_bias,
    second_gain,
    second_shift,
    up_weight,
    up_bias,
    down_weight,
    down_bias,
    bias_table,
):
    clip_count = clips_in.shape[0]
    column_count = clip_count * (HGT // WH) * (WID // WW) // lax.axis_size("seq")
    scale = HD ** (-0.5)
    column_scale = jnp.concatenate(
        [jnp.full((D,), scale, jnp.float32), jnp.ones((2 * D,), jnp.float32)]
    )
    bias_heads = [
        jnp.take(bias_table[layer], offset_index, axis=0).transpose(2, 0, 1)
        for layer in range(LAYERS)
    ]
    extras = [window_extra(column_count) if layer % 2 == 1 else None for layer in range(LAYERS)]

    def forward(field, weights, layer):
        shifted = layer % 2 == 1
        (
            gain_one,
            shift_one,
            in_matrix,
            in_offset,
            out_matrix,
            out_offset,
            gain_two,
            shift_two,
            up_matrix,
            up_offset,
            down_matrix,
            down_offset,
        ) = weights
        in_bias = in_offset.astype(jnp.float32)
        normed = norm_rows(
            field, gain_one.astype(jnp.float32), shift_one.astype(jnp.float32)
        ).astype(jnp.bfloat16)
        mixed = jnp.dot(normed, in_matrix, preferred_element_type=jnp.float32)
        query = ((mixed[..., :D] + in_bias[:D]) * scale).astype(jnp.bfloat16)
        keys = mixed[..., D : 2 * D].astype(jnp.bfloat16)
        values = (mixed[..., 2 * D :] + in_bias[D:]).astype(jnp.bfloat16)
        window_query, window_keys, window_values = send_triple((query, keys, values), shifted)
        window_output, log_total = attend_forward(
            window_query, window_keys, window_values, bias_heads[layer], extras[layer]
        )
        attended = return_output(window_output, clip_count, shifted)
        middle = (
            field
            + jnp.dot(attended, out_matrix, preferred_element_type=jnp.float32)
            + out_offset.astype(jnp.float32)
        )
        normed_two = norm_rows(
            middle, gain_two.astype(jnp.float32), shift_two.astype(jnp.float32)
        ).astype(jnp.bfloat16)
        hidden = jnp.dot(
            normed_two, up_matrix, preferred_element_type=jnp.float32
        ) + up_offset.astype(jnp.float32)
        active = exact_gelu(hidden).astype(jnp.bfloat16)
        result = (
            middle
            + jnp.dot(active, down_matrix, preferred_element_type=jnp.float32)
            + down_offset.astype(jnp.float32)
        )
        return (
            result,
            (
                normed,
                window_query,
                window_keys,
                window_values,
                log_total,
                attended,
                middle,
                normed_two,
                hidden,
                active,
            ),
        )

    field = clips_in.astype(jnp.float32)
    inputs_kept = []
    for layer in range(LAYERS):
        weights = (
            lax.all_gather(first_gain[layer], ("batch", "seq"), axis=0, tiled=True),
            lax.all_gather(first_shift[layer], ("batch", "seq"), axis=0, tiled=True),
            lax.all_gather(inner_weight[layer], ("batch", "seq"), axis=0, tiled=True),
            lax.all_gather(inner_bias[layer], ("batch", "seq"), axis=0, tiled=True),
            lax.all_gather(outer_weight[layer], ("batch", "seq"), axis=0, tiled=True),
            lax.all_gather(outer_bias[layer], ("batch", "seq"), axis=0, tiled=True),
            lax.all_gather(second_gain[layer], ("batch", "seq"), axis=0, tiled=True),
            lax.all_gather(second_shift[layer], ("batch", "seq"), axis=0, tiled=True),
            lax.all_gather(up_weight[layer], ("batch", "seq"), axis=0, tiled=True),
            lax.all_gather(up_bias[layer], ("batch", "seq"), axis=0, tiled=True),
            lax.all_gather(down_weight[layer], ("batch", "seq"), axis=0, tiled=True),
            lax.all_gather(down_bias[layer], ("batch", "seq"), axis=0, tiled=True),
        )
        inputs_kept.append(field)
        field, saved = forward(field, weights, layer)
    clips_out = field.astype(jnp.bfloat16)
    upstream = cotangent.astype(jnp.float32)
    grad_parts = [None] * LAYERS
    table_parts = [None] * LAYERS
    for layer in reversed(range(LAYERS)):
        weights = (
            lax.all_gather(first_gain[layer], ("batch", "seq"), axis=0, tiled=True),
            lax.all_gather(first_shift[layer], ("batch", "seq"), axis=0, tiled=True),
            lax.all_gather(inner_weight[layer], ("batch", "seq"), axis=0, tiled=True),
            lax.all_gather(inner_bias[layer], ("batch", "seq"), axis=0, tiled=True),
            lax.all_gather(outer_weight[layer], ("batch", "seq"), axis=0, tiled=True),
            lax.all_gather(outer_bias[layer], ("batch", "seq"), axis=0, tiled=True),
            lax.all_gather(second_gain[layer], ("batch", "seq"), axis=0, tiled=True),
            lax.all_gather(second_shift[layer], ("batch", "seq"), axis=0, tiled=True),
            lax.all_gather(up_weight[layer], ("batch", "seq"), axis=0, tiled=True),
            lax.all_gather(up_bias[layer], ("batch", "seq"), axis=0, tiled=True),
            lax.all_gather(down_weight[layer], ("batch", "seq"), axis=0, tiled=True),
            lax.all_gather(down_bias[layer], ("batch", "seq"), axis=0, tiled=True),
        )
        saved = forward(inputs_kept[layer], weights, layer)[1]
        backward_field = inputs_kept[layer]
        backward_shifted = layer % 2 == 1
        (
            backward_gain_one,
            backward_shift_one,
            backward_in_matrix,
            backward_in_offset,
            backward_out_matrix,
            backward_out_offset,
            backward_gain_two,
            backward_shift_two,
            backward_up_matrix,
            backward_up_offset,
            backward_down_matrix,
            backward_down_offset,
        ) = weights
        (
            backward_normed,
            backward_window_query,
            backward_window_keys,
            backward_window_values,
            backward_log_total,
            backward_attended,
            backward_middle,
            backward_normed_two,
            backward_hidden,
            backward_active,
        ) = saved
        down_bias_grad = token_sum(upstream)
        upstream_low = upstream.astype(jnp.bfloat16)
        down_grad = weight_grad(backward_active, upstream_low)
        active_grad = input_grad(upstream_low, backward_down_matrix)
        gelu_back = jax.vjp(exact_gelu, backward_hidden)[1]
        hidden_grad = gelu_back(active_grad)[0]
        up_bias_grad = token_sum(hidden_grad)
        hidden_low = hidden_grad.astype(jnp.bfloat16)
        up_grad = weight_grad(backward_normed_two, hidden_low)
        normed_two_grad = input_grad(hidden_low, backward_up_matrix)
        second_back = jax.vjp(
            norm_rows,
            backward_middle,
            backward_gain_two.astype(jnp.float32),
            backward_shift_two.astype(jnp.float32),
        )[1]
        middle_part, gain_two_grad, shift_two_grad = second_back(normed_two_grad)
        middle_grad = upstream + middle_part
        out_bias_grad = token_sum(middle_grad)
        middle_low = middle_grad.astype(jnp.bfloat16)
        out_grad = weight_grad(backward_attended, middle_low)
        attended_grad = input_grad(middle_low, backward_out_matrix).astype(jnp.bfloat16)
        window_grad = send_grad(attended_grad, backward_shifted)
        query_grad, keys_grad, values_grad, table_terms = attend_backward(
            backward_window_query,
            backward_window_keys,
            backward_window_values,
            backward_log_total,
            bias_heads[layer],
            extras[layer],
            window_grad,
        )
        place_query, place_keys, place_values = return_grads(
            (query_grad, keys_grad, values_grad), clip_count, backward_shifted
        )
        joined = jnp.concatenate([place_query, place_keys, place_values], axis=-1)
        in_grad = weight_grad(backward_normed, joined) * column_scale
        in_bias_grad = jnp.concatenate([token_sum(place_query) * scale, token_sum(place_values)])
        normed_grad = input_grad(place_query, backward_in_matrix[:, :D]) * scale + input_grad(
            joined[..., D:], backward_in_matrix[:, D:]
        )
        first_back = jax.vjp(
            norm_rows,
            backward_field,
            backward_gain_one.astype(jnp.float32),
            backward_shift_one.astype(jnp.float32),
        )[1]
        field_part, gain_one_grad, shift_one_grad = first_back(normed_grad)
        table_grad = jax.ops.segment_sum(
            table_terms.transpose(1, 2, 0).reshape(-1, HEADS),
            offset_index.reshape(-1),
            num_segments=BIAS_ROWS,
        )
        layer_grads = (
            gain_one_grad,
            shift_one_grad,
            in_grad,
            in_bias_grad,
            out_grad,
            out_bias_grad,
            gain_two_grad,
            shift_two_grad,
            up_grad,
            up_bias_grad,
            down_grad,
            down_bias_grad,
        )
        upstream, layer_grads, table_grad = (middle_grad + field_part, layer_grads, table_grad)
        grad_parts[layer] = (
            lax.psum_scatter(layer_grads[0], ("batch", "seq"), scatter_dimension=0, tiled=True),
            lax.psum_scatter(layer_grads[1], ("batch", "seq"), scatter_dimension=0, tiled=True),
            lax.psum_scatter(layer_grads[2], ("batch", "seq"), scatter_dimension=0, tiled=True),
            lax.psum_scatter(layer_grads[3], ("batch", "seq"), scatter_dimension=0, tiled=True),
            lax.psum_scatter(layer_grads[4], ("batch", "seq"), scatter_dimension=0, tiled=True),
            lax.psum_scatter(layer_grads[5], ("batch", "seq"), scatter_dimension=0, tiled=True),
            lax.psum_scatter(layer_grads[6], ("batch", "seq"), scatter_dimension=0, tiled=True),
            lax.psum_scatter(layer_grads[7], ("batch", "seq"), scatter_dimension=0, tiled=True),
            lax.psum_scatter(layer_grads[8], ("batch", "seq"), scatter_dimension=0, tiled=True),
            lax.psum_scatter(layer_grads[9], ("batch", "seq"), scatter_dimension=0, tiled=True),
            lax.psum_scatter(layer_grads[10], ("batch", "seq"), scatter_dimension=0, tiled=True),
            lax.psum_scatter(layer_grads[11], ("batch", "seq"), scatter_dimension=0, tiled=True),
        )
        table_parts[layer] = table_grad
    stacked = tuple(
        (jnp.stack([grad_parts[layer][index] for layer in range(LAYERS)]) for index in range(12))
    )
    table_total = lax.psum(jnp.stack(table_parts), ("batch", "seq"))
    return (clips_out, upstream.astype(jnp.bfloat16)) + stacked + (table_total,)


def solution(mesh):
    return jax.shard_map(
        per_device,
        mesh=mesh,
        in_specs=(
            P("batch", "seq", None, None, None),
            P("batch", "seq", None, None, None),
            P(),
            P(None, ("batch", "seq")),
            P(None, ("batch", "seq")),
            P(None, ("batch", "seq"), None),
            P(None, ("batch", "seq")),
            P(None, ("batch", "seq"), None),
            P(None, ("batch", "seq")),
            P(None, ("batch", "seq")),
            P(None, ("batch", "seq")),
            P(None, ("batch", "seq"), None),
            P(None, ("batch", "seq")),
            P(None, ("batch", "seq"), None),
            P(None, ("batch", "seq")),
            P(),
        ),
        out_specs=(
            P("batch", "seq", None, None, None),
            P("batch", "seq", None, None, None),
            P(None, ("batch", "seq")),
            P(None, ("batch", "seq")),
            P(None, ("batch", "seq"), None),
            P(None, ("batch", "seq")),
            P(None, ("batch", "seq"), None),
            P(None, ("batch", "seq")),
            P(None, ("batch", "seq")),
            P(None, ("batch", "seq")),
            P(None, ("batch", "seq"), None),
            P(None, ("batch", "seq")),
            P(None, ("batch", "seq"), None),
            P(None, ("batch", "seq")),
            P(),
        ),
        check_vma=False,
    )
```

profile of v0, /device:TPU:25, one launch (start us, length us, event | category | flops | bytes accessed | tf_op | source)
XLA Modules:
  0.0 5115.1 jit_solution(9874248529269179150)
XLA Ops:
  19.9 40.9 all-reduce.33
  159.2 283.0 %gather_fusion.1 = f32[153664,16]{1,0:T(8,128)} fusion(f32[2535,16]{1,0:T(8,128)S(1)} %bitcast.493, s32[154624]{0:T(1024)S(1)} %pad_clamp_fusion), kind=kCustom, calls=%fused_computation.clone | custom fusion | bytes 20283648 | tf_op jit(solution)/shard_map/jit(_take)/gather | solution.py:225
  442.2 54.5 %copy.617 = f32[392,392,16]{0,1,2:T(8,128)} copy(f32[392,392,16]{2,1,0:T(8,128)} %bitcast.25) | data formatting | bytes 19668992 | tf_op jit(solution)/shard_map/jit(_take)/gather | solution.py:225
  496.7 282.6 %gather_fusion.2 = f32[153664,16]{1,0:T(8,128)} fusion(f32[2535,16]{1,0:T(8,128)S(1)} %bitcast.492, s32[154624]{0:T(1024)S(1)} %pad_clamp_fusion), kind=kCustom, calls=%fused_computation.1.clone | custom fusion | bytes 20283648 | tf_op jit(solution)/shard_map/jit(_take)/gather | solution.py:225
  779.3 54.5 %copy.645 = f32[392,392,16]{0,1,2:T(8,128)} copy(f32[392,392,16]{2,1,0:T(8,128)} %bitcast.79) | data formatting | bytes 19668992 | tf_op jit(solution)/shard_map/jit(_take)/gather | solution.py:225
  922.8 42.5 add_reduce_fusion
  965.3 43.0 fusion
  1008.2 40.0 convert_bitcast_fusion.7
  1085.6 92.5 %all-gather.4 = bf16[1,512,512]{2,1,0:T(8,128)(2,1)} all-gather(bf16[1,16,512]{2,1,0:T(8,128)(2,1)S(1)} %get-tuple-element.200), channel_id=6, replica_groups=mesh['batch'=16,'seq'=2] {'batch','seq'}, dimensions={1}, use_global_device_ids=true | all-gather | bytes 540672 | tf_op jit(solution)/shard_map/all_gather | solution.py:300
  1211.6 69.2 %multiply_convert_fusion.1 = (bf16[2,8,14,14,2048]{4,3,2,1,0:T(8,128)(2,1)}, f32[2,8,14,14,2048]{4,3,2,1,0:T(8,128)}) fusion(f32[2,8,14,14,2048]{4,3,2,1,0:T(8,128)} %get-tuple-element.225, f32[2048]{0:T(1024)S(1)} %convert_element_type.397, u16[2,8,14,2048]{3,2,1,0:T(8,128)(2,1)S(1)} %get-tuple-element.109, u16[2,8,14,2048]{3,2,1,0:T(8,128)(2,1)S(1)} %get-tuple-element.108), kind=kLoop, calls=%fused_computation.54 | loop fusion | flops 455999488 | bytes 66068480 | tf_op jit(solution)/shard_map/convert_element_type | solution.py:270
  1572.1 49.3 fusion.214
  1621.4 42.3 fusion.1
  1745.1 99.7 %all-gather.16 = bf16[1,512,512]{2,1,0:T(8,128)(2,1)} all-gather(bf16[1,16,512]{2,1,0:T(8,128)(2,1)S(1)} %copy-done.93), channel_id=18, replica_groups=mesh['batch'=16,'seq'=2] {'batch','seq'}, dimensions={1}, use_global_device_ids=true | all-gather | bytes 540672 | tf_op jit(solution)/shard_map/all_gather | solution.py:300
  1879.6 69.4 %multiply_convert_fusion = (bf16[2,8,14,14,2048]{4,3,2,1,0:T(8,128)(2,1)}, f32[2,8,14,14,2048]{4,3,2,1,0:T(8,128)}) fusion(f32[2,8,14,14,2048]{4,3,2,1,0:T(8,128)} %get-tuple-element.232, f32[2048]{0:T(1024)S(1)} %convert_element_type.405, u16[2,8,14,2048]{3,2,1,0:T(8,128)(2,1)S(1)} %get-tuple-element.107, u16[2,8,14,2048]{3,2,1,0:T(8,128)(2,1)S(1)} %get-tuple-element.106), kind=kLoop, calls=%fused_computation.41 | loop fusion | flops 455999488 | bytes 66068480 | tf_op jit(solution)/shard_map/convert_element_type | solution.py:270
  2152.8 76.1 %multiply_reduce_fusion.1 = (f32[8,16,392]{2,1,0:T(8,128)}, f32[8,16,392,392]{2,3,1,0:T(8,128)}) fusion(f32[8,16,392,392]{2,3,1,0:T(8,128)} %get-tuple-element.229, f32[8,16,392]{2,1,0:T(8,128)S(1)} %log_add_fusion.1, bf16[8,392,16,32]{1,0,3,2:T(8,128)(2,1)} %reshape_reshape.42, bf16[8,392,16,32]{1,0,3,2:T(8,128)(2,1)} %reshape_reshape.45), kind=kOutput, calls=%fused_computation.9 | convolution fusion | flops 1317772288 | bytes 164175872 | tf_op jit(solution)/shard_map/wqhd,wkhd->whqk/dot_general | solution.py:176
  2278.4 93.8 %fusion.23 = (f32[16,392,392]{1,2,0:T(8,128)}, bf16[8,16,392,392]{2,3,1,0:T(8,128)(2,1)}) fusion(f32[8,16,392,392]{2,3,1,0:T(8,128)} %get-tuple-element.235, f32[8,16,392]{2,1,0:T(8,128)} %get-tuple-element.234, f32[8,16,392,392]{2,3,1,0:T(8,128)} %get-tuple-element.229, f32[8,16,392]{2,1,0:T(8,128)S(1)} %log_add_fusion.1), kind=kLoop, calls=%fused_computation.67 | loop fusion | flops 95886336 | bytes 206925824 | tf_op jit(solution)/shard_map/reduce_sum | solution.py:196
  2749.7 41.1 convert_bitcast_fusion
  2790.8 73.0 %multiply_reduce_fusion = (f32[8,16,392]{2,1,0:T(8,128)}, f32[8,16,392,392]{2,3,1,0:T(8,128)}) fusion(f32[8,16,392,392]{2,3,1,0:T(8,128)} %get-tuple-element.222, f32[8,16,392]{2,1,0:T(8,128)S(1)} %copy-done.48, f32[16,392,392]{1,2,0:T(8,128)} %get-tuple-element.192, bf16[8,392,16,32]{1,3,2,0:T(8,128)(2,1)} %reshape_reshape.46, ...), kind=kOutput, calls=%fused_computation.6 | convolution fusion | flops 1337441280 | bytes 174010368 | tf_op jit(solution)/shard_map/wqhd,wkhd->whqk/dot_general | solution.py:176
  2900.5 96.7 %fusion.194 = (f32[16,392,392]{1,2,0:T(8,128)}, bf16[8,16,392,392]{2,3,1,0:T(8,128)(2,1)}) fusion(f32[8,16,392,392]{2,3,1,0:T(8,128)} %get-tuple-element.239, f32[8,16,392]{2,1,0:T(8,128)} %get-tuple-element.238, f32[8,16,392]{2,1,0:T(8,128)S(1)} %copy-done.48, f32[8,16,392,392]{2,3,1,0:T(8,128)} %get-tuple-element.222, f32[16,392,392]{1,2,0:T(8,128)} %get-tuple-element.192), kind=kLoop, calls=%fused_computation.376 | loop fusion | flops 115555328 | bytes 216760320 | tf_op jit(solution)/shard_map/reduce_sum | solution.py:196
  3240.3 46.5 copy.804
  3286.8 819.6 %scatter_custom_fusion.1 = f32[2535,16]{1,0:T(8,128)S(1)} fusion(s32[153664]{0:T(1024)S(1)} %reshape.593, f32[153664,16]{1,0:T(8,128)} %bitcast.238, f32[]{:T(128)} %constant.55.clone.1), kind=kCustom, calls=%fused_computation.264 | custom fusion | flops 2458624 | bytes 162752 | tf_op jit(solution)/shard_map/scatter-add | solution.py:407
  4110.6 46.2 copy.803
  4156.8 819.4 %scatter_custom_fusion = f32[2535,16]{1,0:T(8,128)S(1)} fusion(s32[153664]{0:T(1024)S(1)} %reshape.593, f32[153664,16]{1,0:T(8,128)} %bitcast.235, f32[]{:T(128)} %constant.55.clone.1), kind=kCustom, calls=%fused_computation.266 | custom fusion | flops 2458624 | bytes 162752 | tf_op jit(solution)/shard_map/scatter-add | solution.py:407
  5006.0 41.2 all-reduce.32
  (718 shorter events, 1681.3 us)
Async XLA Ops:
  7.2 61.3 %all-gather.31.cloned.1.call-start = ((), (), s32[]{:S(2)}) async-start(), calls=%async_computation.33 | async-start | bytes 1622016 | tf_op jit(solution)/shard_map/all_gather | solution.py:298
  8.9 1180.9 %all-gather.33.cloned.1.call-start = ((), (), s32[]{:S(2)}) async-start(), calls=%async_computation.34 | async-start | bytes 2162688 | tf_op jit(solution)/shard_map/all_gather | solution.py:304
  117.4 1163.5 %all-gather.35.cloned.1.call-start = ((), (), s32[]{:S(2)}) async-start(), calls=%async_computation.35 | async-start | bytes 2162688 | tf_op jit(solution)/shard_map/all_gather | solution.py:306
  153.8 682.0 %all-to-all-start.2 = ((bf16[8,8,49,512]{3,1,2,0:T(8,128)(2,1)}), bf16[8,8,49,512]{3,1,2,0:T(8,128)(2,1)}, u32[]{:S(2)}, u32[]{:S(2)}) async-start(bf16[8,8,49,512]{3,1,2,0:T(8,128)(2,1)} %bitcast.539), calls=%async_computation.2 | async-start | bytes 6422528 | tf_op jit(solution)/shard_map/all_to_all | solution.py:107
  835.8 66.3 %all-to-all-start = ((bf16[8,8,49,512]{3,1,2,0:T(8,128)(2,1)}), bf16[8,8,49,512]{3,1,2,0:T(8,128)(2,1)S(1)}, u32[]{:S(2)}, u32[]{:S(2)}) async-start(bf16[8,8,49,512]{3,1,2,0:T(8,128)(2,1)} %bitcast.10), calls=%async_computation | async-start | bytes 6422528 | tf_op jit(solution)/shard_map/all_to_all | solution.py:108
  1079.0 99.1 %all-to-all-start.3 = ((bf16[4,16,49,512]{3,0,2,1:T(4,128)(2,1)}), bf16[4,16,49,512]{3,0,2,1:T(4,128)(2,1)}, u32[]{:S(2)}, u32[]{:S(2)}) async-start(bf16[4,16,49,512]{3,0,2,1:T(4,128)(2,1)} %copy.620), calls=%async_computation.3 | async-start | bytes 6422528 | tf_op jit(solution)/shard_map/all_to_all | solution.py:114
  1084.2 222.6 %all-gather.37.cloned.1.call-start = ((), (), s32[]{:S(2)}) async-start(), calls=%async_computation.36 | async-start | bytes 1622016 | tf_op jit(solution)/shard_map/all_gather | solution.py:298
  1392.1 465.6 %all-gather.39.cloned.1.call-start = ((), (), s32[]{:S(2)}) async-start(), calls=%async_computation.37 | async-start | bytes 2162688 | tf_op jit(solution)/shard_map/all_gather | solution.py:304
  1740.4 104.4 %all-to-all-start.7 = ((bf16[4,16,49,512]{3,0,2,1:T(4,128)(2,1)}), bf16[4,16,49,512]{3,0,2,1:T(4,128)(2,1)S(1)}, u32[]{:S(2)}, u32[]{:S(2)}) async-start(bf16[4,16,49,512]{3,0,2,1:T(4,128)(2,1)} %copy.651), calls=%async_computation.7 | async-start | bytes 6422528 | tf_op jit(solution)/shard_map/all_to_all | solution.py:114
  1744.4 204.6 %all-gather.41.cloned.1.call-start = ((), (), s32[]{:S(2)}) async-start(), calls=%async_computation.38 | async-start | bytes 2162688 | tf_op jit(solution)/shard_map/all_gather | solution.py:306
  2274.2 166.5 %all-to-all-start.11 = ((bf16[4,16,49,512]{3,0,2,1:T(4,128)(2,1)}), bf16[4,16,49,512]{3,0,2,1:T(4,128)(2,1)S(1)}, u32[]{:S(2)}, u32[]{:S(2)}) async-start(bf16[4,16,49,512]{3,0,2,1:T(4,128)(2,1)} %copy.691), calls=%async_computation.11 | async-start | bytes 6422528 | tf_op jit(solution)/shard_map/all_to_all | solution.py:132
  2440.7 68.1 %all-to-all-start.10 = ((bf16[4,16,49,512]{3,0,2,1:T(4,128)(2,1)}), bf16[4,16,49,512]{3,0,2,1:T(4,128)(2,1)}, u32[]{:S(2)}, u32[]{:S(2)}) async-start(bf16[4,16,49,512]{3,0,2,1:T(4,128)(2,1)} %copy.682), calls=%async_computation.10 | async-start | bytes 6422528 | tf_op jit(solution)/shard_map/all_to_all | solution.py:131
  2514.1 2463.3 %reduce-scatter.15.cloned.1.call-start = ((), (), s32[]{:S(2)}) async-start(), calls=%async_computation.27 | async-start | bytes 1081344 | tf_op jit(solution)/shard_map/reduce_scatter | solution.py:432
  2681.0 46.0 all-to-all-start.12
  2686.6 2290.8 %reduce-scatter.13.cloned.1.call-start = ((), (), s32[]{:S(2)}) async-start(), calls=%async_computation.26 | async-start | bytes 1081344 | tf_op jit(solution)/shard_map/reduce_scatter | solution.py:432
  2896.6 156.7 %all-to-all-start.15 = ((bf16[4,16,49,512]{3,0,2,1:T(4,128)(2,1)}), bf16[4,16,49,512]{3,0,2,1:T(4,128)(2,1)S(1)}, u32[]{:S(2)}, u32[]{:S(2)}) async-start(bf16[4,16,49,512]{3,0,2,1:T(4,128)(2,1)} %copy.720), calls=%async_computation.15 | async-start | bytes 6422528 | tf_op jit(solution)/shard_map/all_to_all | solution.py:132
  3053.2 55.8 %all-to-all-start.14 = ((bf16[4,16,49,512]{3,0,2,1:T(4,128)(2,1)}), bf16[4,16,49,512]{3,0,2,1:T(4,128)(2,1)}, u32[]{:S(2)}, u32[]{:S(2)}) async-start(bf16[4,16,49,512]{3,0,2,1:T(4,128)(2,1)} %copy.714), calls=%async_computation.14 | async-start | bytes 6422528 | tf_op jit(solution)/shard_map/all_to_all | solution.py:131
  3114.3 1953.3 %reduce-scatter.11.cloned.1.call-start = ((), (), s32[]{:S(2)}) async-start(), calls=%async_computation.25 | async-start | bytes 3244032 | tf_op jit(solution)/shard_map/reduce_scatter | solution.py:430
  3127.1 1940.5 %reduce-scatter.9.cloned.1.call-start = ((), (), s32[]{:S(2)}) async-start(), calls=%async_computation.24 | async-start | bytes 3244032 | tf_op jit(solution)/shard_map/reduce_scatter | solution.py:430
  3178.1 1891.1 %reduce-scatter.19.cloned.1.call-start = ((), (), s32[]{:S(2)}) async-start(), calls=%async_computation.29 | async-start | bytes 4325376 | tf_op jit(solution)/shard_map/reduce_scatter | solution.py:436
  3194.8 1874.4 %reduce-scatter.17.cloned.1.call-start = ((), (), s32[]{:S(2)}) async-start(), calls=%async_computation.28 | async-start | bytes 4325376 | tf_op jit(solution)/shard_map/reduce_scatter | solution.py:436
  3212.5 1858.4 %reduce-scatter.23.cloned.1.call-start = ((), (), s32[]{:S(2)}) async-start(), calls=%async_computation.31 | async-start | bytes 4325376 | tf_op jit(solution)/shard_map/reduce_scatter | solution.py:438
  3225.7 1845.2 %reduce-scatter.21.cloned.1.call-start = ((), (), s32[]{:S(2)}) async-start(), calls=%async_computation.30 | async-start | bytes 4325376 | tf_op jit(solution)/shard_map/reduce_scatter | solution.py:438
  3239.4 1867.2 %all-reduce.36.cloned.1.call-start = ((), (), s32[]{:S(2)}) async-start(), calls=%async_computation.32 | async-start | bytes 655360 | tf_op jit(solution)/shard_map/psum | solution.py:445
  (150 other events, 3991.1 us)
Sparse Core Ops, SparseCore 0:
  11.5 55.5 all-gather.30
  70.8 55.5 all-gather.32
  130.0 58.1 all-gather.34
  1087.6 56.7 all-gather.36
  1396.3 66.2 all-gather.38
  1748.0 66.0 all-gather.40
  2521.0 133.9 reduce-scatter.14
  2697.8 131.3 reduce-scatter.12
  3127.2 104.1 reduce-scatter.10
  3236.7 100.3 reduce-scatter.8
  3339.4 134.5 reduce-scatter.18
  3476.1 138.2 reduce-scatter.16
  3616.7 138.6 reduce-scatter.22
  3757.6 138.5 reduce-scatter.20
  4977.5 129.1 all-reduce.35
where the time goes:
time: 5140 us; the launch traced here: 5120 us
  other arithmetic  2320 us (45%)
  local copies, waits for them, and re-layouts  1410 us (27%)
  matrix products  797 us (16%)
  blocking collectives  274 us (5%)
  waiting for transfers between devices  214 us (4%)
  starting transfers between devices  79.3 us (2%)
    scatter-add x2, other arithmetic, per_device(): jax.ops.segment_sum(table_terms.transpose(1, 2, 0).reshape(-1, HEADS), of...  1640 us
    gather x4, local copies, waits for them, and re-layouts, per_device(): jnp.take(bias_table[layer], offset_index, axis=0).transpose(2, 0, 1)  675 us
    all_gather x2, blocking collectives, per_device(): lax.all_gather(outer_weight[layer], ('batch', 'seq'), axis=0, tiled=True)  192 us
    reduce_sum x2, other arithmetic, attend_backward(): jnp.sum(total_grad, axis=0)  191 us
    dot_general x2, matrix products, attend_backward(): jnp.einsum('wqhd,wkhd->whqk', grad_heads, head_values, preferred_element_...  149 us
    convert_element_type x2, other arithmetic, forward(): active = exact_gelu(hidden).astype(jnp.bfloat16)  139 us
    dot_general x10, matrix products, input_grad(): lax.dot_general(grads, matrix, (((grads.ndim - 1,), (1,)), ((), ())), pre...  116 us
  transfers between devices with their start and end apart: 31, of which 9 were waited for; matrix products, arithmetic and copies ran while one was open for 82% of the time, Pallas kernels for 0%

commit v1 on v0

v1 whole, which is shorter than its diff:
```python
import functools

import jax
import jax.numpy as jnp
import numpy as np
from jax import lax
from jax.experimental import pallas as pl
from jax.experimental.pallas import tpu as pltpu
from jax.sharding import PartitionSpec as P

D = 512
HEADS = 16
HD = 32
FF = 2048
WT = 8
WH = 7
WW = 7
FRAMES = 16
HGT = 14
WID = 14
LAYERS = 2
SHIFT_T = 4
SHIFT_S = 3
WIN = 392
BIAS_ROWS = 2535
ROWS = 16
PACKS = D // ROWS
CELLS = (2 * WH - 1) * (2 * WW - 1)

EPSILON = 1e-05
MASKED = -100.0
LOG2E = 1.4426950408889634
LN2 = 0.6931471805599453
SCALE = HD**-0.5

BF16 = jnp.bfloat16
F32 = jnp.float32
AXES = ("batch", "seq")

NT = (((1,), (1,)), ((), ()))
TN = (((0,), (0,)), ((), ()))


def params():
    return pltpu.CompilerParams(
        vmem_limit_bytes=61 * 1024 * 1024, dimension_semantics=("arbitrary",)
    )


def dot(left, right, dims=(((1,), (0,)), ((), ()))):
    return lax.dot_general(left, right, dims, preferred_element_type=F32)


def normalize(values):
    average = jnp.mean(values, axis=-1, keepdims=True)
    centred = values - average
    rate = lax.rsqrt(jnp.mean(centred * centred, axis=-1, keepdims=True) + EPSILON)
    return centred * rate, rate


def row_sum(values):
    return jnp.sum(values, axis=0, keepdims=True)


def split_three(values):
    high = values.astype(BF16)
    rest = values - high.astype(F32)
    middle = rest.astype(BF16)
    low = (rest - middle.astype(F32)).astype(BF16)
    return high, middle, low


def square(ref, first):
    return ref[:, first : first + ROWS, :].reshape(D, D)


def grid_spec(shape):
    row_blocks, col_blocks = shape[1] // WH, shape[2] // WW
    per_clip = row_blocks * col_blocks
    return pl.BlockSpec(
        (1, WH, WW, WT, D),
        lambda i: (i // per_clip, (i % per_clip) // col_blocks, i % col_blocks, 0, 0),
    )


def window_spec(*tail):
    return pl.BlockSpec((1,) + tail, lambda i: (i,) + (0,) * len(tail))


def whole_spec(*shape):
    return pl.BlockSpec(shape, lambda i: (0,) * len(shape), pipeline_mode=pl.Buffered(1))


def pack_spec(rows, index):
    return pl.BlockSpec(
        (PACKS, rows, D), lambda i: (0, index, 0), pipeline_mode=pl.Buffered(1)
    )


def head_lanes(which):
    lane = lax.broadcasted_iota(jnp.int32, (1, 128), 1)
    return (lane // HD) == which


def lane_slice(group, base=0):
    return pl.ds(pl.multiple_of(base + group * 128, 128), 128)


def attention_forward(masked, *refs):
    if masked:
        x_ref, w_ref, vec_ref, bias_ref, augq_ref, augk_ref = refs[:6]
        qkv_ref, soft_ref, rate_ref, att_ref, mid_ref, vt_s, ot_s = refs[6:]
    else:
        x_ref, w_ref, vec_ref, bias_ref = refs[:4]
        qkv_ref, soft_ref, rate_ref, att_ref, mid_ref, vt_s, ot_s = refs[4:]
    x = x_ref[0].astype(F32).reshape(WIN, D)
    normed = (normalize(x)[0] * vec_ref[0:1] + vec_ref[1:2]).astype(BF16)
    query = (dot(normed, square(w_ref, 0)) + vec_ref[2:3]) * (SCALE * LOG2E)
    qkv_ref[0, :, 0:D] = query.astype(BF16)
    qkv_ref[0, :, D : 2 * D] = dot(normed, square(w_ref, ROWS)).astype(BF16)
    values = dot(normed, square(w_ref, 2 * ROWS)) + vec_ref[3:4]
    qkv_ref[0, :, 2 * D :] = values.astype(BF16)
    vt_s[...] = jnp.transpose(values).astype(BF16)

    def group(g, carry):
        query4 = qkv_ref[0, :, lane_slice(g)]
        keys4 = qkv_ref[0, :, lane_slice(g, D)]
        if masked:
            query4 = jnp.concatenate([query4, augq_ref[0]], axis=1)
        for which in range(4):
            head = g * 4 + which
            keys = jnp.where(head_lanes(which), keys4, jnp.zeros_like(keys4))
            if masked:
                keys = jnp.concatenate([keys, augk_ref[0]], axis=1)
            total = dot(keys, query4, NT) + bias_ref[head]
            peak = jnp.max(total, axis=0, keepdims=True)
            soft = jnp.exp2(total - peak).astype(BF16)
            soft_ref[0, head] = soft
            rows = pl.ds(pl.multiple_of(head * HD, HD), HD)
            left = jnp.concatenate([vt_s[rows, :], jnp.ones((16, WIN), BF16)], axis=0)
            joined = dot(left, soft)
            rate = 1.0 / joined[HD : HD + 1]
            rate_ref[0, pl.ds(head, 1), :] = rate
            ot_s[rows, :] = joined[:HD] * rate
        return carry

    lax.fori_loop(0, 4, group, 0)
    attended = jnp.transpose(ot_s[...]).astype(BF16)
    att_ref[0] = attended
    mid_ref[0] = x + dot(attended, square(w_ref, 3 * ROWS)) + vec_ref[4:5]


def run_attention_forward(x, pack, vec, bias, aug):
    windows = x.shape[0] * (x.shape[1] // WH) * (x.shape[2] // WW)
    masked = aug is not None
    extra = list(aug) if masked else []
    return pl.pallas_call(
        functools.partial(attention_forward, masked),
        grid=(windows,),
        in_specs=[
            grid_spec(x.shape),
            pack_spec(64, 0),
            whole_spec(12, D),
            whole_spec(HEADS, WIN, WIN),
        ]
        + [window_spec(WIN, 128)] * len(extra),
        out_specs=[
            window_spec(WIN, 3 * D),
            window_spec(HEADS, WIN, WIN),
            window_spec(HEADS, WIN),
            window_spec(WIN, D),
            window_spec(WIN, D),
        ],
        out_shape=[
            jax.ShapeDtypeStruct((windows, WIN, 3 * D), BF16),
            jax.ShapeDtypeStruct((windows, HEADS, WIN, WIN), BF16),
            jax.ShapeDtypeStruct((windows, HEADS, WIN), F32),
            jax.ShapeDtypeStruct((windows, WIN, D), BF16),
            jax.ShapeDtypeStruct((windows, WIN, D), F32),
        ],
        scratch_shapes=[pltpu.VMEM((D, WIN), BF16), pltpu.VMEM((D, WIN), F32)],
        compiler_params=params(),
    )(x, pack, vec, bias, *extra)


def gelu_parts(hidden):
    cumulative = 0.5 + 0.5 * lax.erf(hidden * (0.5**0.5))
    density = jnp.exp(-0.5 * hidden * hidden) * 0.3989422804014327
    return hidden * cumulative, cumulative + hidden * density


def feed_forward(mid_ref, up_ref, down_ref, vec_ref, act_ref, slope_ref, out_ref):
    middle = mid_ref[0]
    normed = (normalize(middle)[0] * vec_ref[5:6] + vec_ref[6:7]).astype(BF16)
    total = middle + vec_ref[7:8]
    for part in range(4):
        lanes = slice(part * D, (part + 1) * D)
        hidden = dot(normed, square(up_ref, part * ROWS)) + vec_ref[8 + part : 9 + part]
        active, slope = gelu_parts(hidden)
        active = active.astype(BF16)
        act_ref[0, :, lanes] = active
        slope_ref[0, :, lanes] = slope.astype(BF16)
        down = down_ref[part * 8 : part * 8 + 8].reshape(D, D)
        total = total + dot(active, down)
    out_ref[0] = total.reshape(WH, WW, WT, D).astype(out_ref.dtype)


def run_feed_forward(middle, pack, vec, grid_shape, dtype):
    windows = middle.shape[0]
    return pl.pallas_call(
        feed_forward,
        grid=(windows,),
        in_specs=[
            window_spec(WIN, D),
            pack_spec(64, 1),
            pack_spec(64, 2),
            whole_spec(12, D),
        ],
        out_specs=[window_spec(WIN, FF), window_spec(WIN, FF), grid_spec(grid_shape)],
        out_shape=[
            jax.ShapeDtypeStruct((windows, WIN, FF), BF16),
            jax.ShapeDtypeStruct((windows, WIN, FF), BF16),
            jax.ShapeDtypeStruct(grid_shape, dtype),
        ],
        compiler_params=params(),
    )(middle, pack, pack, vec)


def norm_back(normal, rate, gained):
    first = jnp.mean(gained, axis=-1, keepdims=True)
    second = jnp.mean(gained * normal, axis=-1, keepdims=True)
    return (gained - first - normal * second) * rate


def feed_backward(
    grad_ref, act_ref, slope_ref, mid_ref, att_ref, in_ref, up_ref, down_ref, vec_ref,
    gmid_ref, gatt_ref, pack_ref, gvec_ref,
):
    @pl.when(pl.program_id(0) == 0)
    def _():
        pack_ref[...] = jnp.zeros_like(pack_ref)
        gvec_ref[...] = jnp.zeros_like(gvec_ref)

    grad = grad_ref[0].astype(F32).reshape(WIN, D)
    gvec_ref[3:4] += row_sum(grad)
    grad_low = grad.astype(BF16)
    normal, rate = normalize(mid_ref[0])
    normed = (normal * vec_ref[5:6] + vec_ref[6:7]).astype(BF16)
    gnormed = jnp.zeros((WIN, D), F32)
    for part in range(4):
        lanes = slice(part * D, (part + 1) * D)
        active = act_ref[0, :, lanes]
        pack_ref[part * 8 : part * 8 + 8, 80:144, :] += dot(active, grad_low, TN).reshape(8, 64, D)
        down = down_ref[part * 8 : part * 8 + 8].reshape(D, D)
        ghidden = dot(grad_low, down, NT) * slope_ref[0, :, lanes].astype(F32)
        gvec_ref[4 + part : 5 + part] += row_sum(ghidden)
        ghidden = ghidden.astype(BF16)
        first = ROWS * (1 + part)
        pack_ref[:, first : first + ROWS, :] += dot(normed, ghidden, TN).reshape(PACKS, ROWS, D)
        gnormed = gnormed + dot(ghidden, square(up_ref, part * ROWS), NT)
    gvec_ref[1:2] += row_sum(gnormed * normal)
    gvec_ref[2:3] += row_sum(gnormed)
    gmid = grad + norm_back(normal, rate, gnormed * vec_ref[5:6])
    gmid_ref[0] = gmid
    gvec_ref[0:1] += row_sum(gmid)
    gmid_low = gmid.astype(BF16)
    pack_ref[:, 0:ROWS, :] += dot(att_ref[0], gmid_low, TN).reshape(PACKS, ROWS, D)
    gatt_ref[0] = dot(gmid_low, square(in_ref, 3 * ROWS), NT).astype(BF16)


def run_feed_backward(grad, active, slope, middle, attended, pack, vec):
    windows = middle.shape[0]
    return pl.pallas_call(
        feed_backward,
        grid=(windows,),
        in_specs=[
            grid_spec(grad.shape),
            window_spec(WIN, FF),
            window_spec(WIN, FF),
            window_spec(WIN, D),
            window_spec(WIN, D),
            pack_spec(64, 0),
            pack_spec(64, 1),
            pack_spec(64, 2),
            whole_spec(12, D),
        ],
        out_specs=[
            window_spec(WIN, D),
            window_spec(WIN, D),
            pl.BlockSpec((PACKS, 144, D), lambda i: (0, 0, 0)),
            pl.BlockSpec((8, D), lambda i: (0, 0)),
        ],
        out_shape=[
            jax.ShapeDtypeStruct((windows, WIN, D), F32),
            jax.ShapeDtypeStruct((windows, WIN, D), BF16),
            jax.ShapeDtypeStruct((PACKS, 144, D), F32),
            jax.ShapeDtypeStruct((8, D), F32),
        ],
        compiler_params=params(),
    )(grad, active, slope, middle, attended, pack, pack, pack, vec)


def attention_backward(
    x_ref, gatt_ref, att_ref, rate_ref, soft_ref, qkv_ref, gmid_ref, in_ref, vec_ref,
    out_ref, pack_ref, gvec_ref, table_ref,
    sum_s, kt_s, qt_s, do_s, gk_s, gv_s, wide_s,
):
    step = pl.program_id(0)

    @pl.when(step == 0)
    def _():
        sum_s[...] = jnp.zeros_like(sum_s)
        pack_ref[...] = jnp.zeros_like(pack_ref)
        gvec_ref[...] = jnp.zeros_like(gvec_ref)

    lane = lax.broadcasted_iota(jnp.int32, (1, 128), 1)
    head_row = lax.broadcasted_iota(jnp.int32, (3 * HEADS, D), 0) % HEADS
    head_col = lax.broadcasted_iota(jnp.int32, (3 * HEADS, D), 1) // HD
    spread = jnp.where(head_row == head_col, 1.0, 0.0).astype(BF16)
    rates = jnp.concatenate(split_three(rate_ref[0]), axis=0)
    scaled = (gatt_ref[0].astype(F32) * dot(rates, spread, TN)).astype(BF16)
    do_s[...] = scaled
    product = scaled.astype(F32) * att_ref[0].astype(F32)
    gather_row = lax.broadcasted_iota(jnp.int32, (D, 128), 0) // HD
    gather_col = lax.broadcasted_iota(jnp.int32, (D, 128), 1)
    gather = jnp.where(
        (gather_row == gather_col % HEADS) & (gather_col < 3 * HEADS), 1.0, 0.0
    ).astype(BF16)
    high = product.astype(BF16)
    low = (product - high.astype(F32)).astype(BF16)
    inner = dot(high, gather) + dot(low, gather)
    first, second, third = split_three(inner)
    inner = jnp.where(lane < HEADS, first, jnp.where(lane < 2 * HEADS, second, third))
    kt_s[...] = jnp.transpose(qkv_ref[0, :, D : 2 * D].astype(F32)).astype(BF16)

    def group(g, carry):
        query4 = qkv_ref[0, :, lane_slice(g)]
        values4 = qkv_ref[0, :, lane_slice(g, 2 * D)]
        grad4 = do_s[:, lane_slice(g)]
        right = jnp.concatenate([grad4, inner], axis=1)
        zero = jnp.zeros_like(grad4)
        gvalues = jnp.zeros((WIN, 128), F32)
        gkeys = jnp.zeros((WIN, 128), F32)
        for which in range(4):
            head = g * 4 + which
            mine = head_lanes(which)
            minus = jnp.where((lane % HEADS == head) & (lane < 3 * HEADS), -1.0, 0.0)
            minus = jnp.broadcast_to(minus, (WIN, 128)).astype(BF16)
            left = jnp.concatenate([jnp.where(mine, values4, zero), minus], axis=1)
            soft = soft_ref[0, head]
            gtotal = soft.astype(F32) * dot(left, right, NT)
            sum_s[head] += gtotal
            gtotal = gtotal.astype(BF16)
            gvalues = gvalues + dot(soft, jnp.where(mine, grad4, zero))
            gkeys = gkeys + dot(gtotal, jnp.where(mine, query4, zero))
            rows = pl.ds(pl.multiple_of(head * HD, HD), HD)
            qt_s[rows, :] = dot(kt_s[rows, :], gtotal)
        gv_s[:, lane_slice(g)] = gvalues.astype(BF16)
        gk_s[:, lane_slice(g)] = (gkeys * LN2).astype(BF16)
        return carry

    lax.fori_loop(0, 4, group, 0)
    gquery = jnp.transpose(qt_s[...]).astype(BF16)
    gkeys = gk_s[...]
    gvalues = gv_s[...]
    normal, rate = normalize(x_ref[0].astype(F32).reshape(WIN, D))
    normed = (normal * vec_ref[0:1] + vec_ref[1:2]).astype(BF16)
    pack_ref[:, 0:ROWS, :] += (dot(normed, gquery, TN) * SCALE).reshape(PACKS, ROWS, D)
    pack_ref[:, ROWS : 2 * ROWS, :] += dot(normed, gkeys, TN).reshape(PACKS, ROWS, D)
    pack_ref[:, 2 * ROWS :, :] += dot(normed, gvalues, TN).reshape(PACKS, ROWS, D)
    gvec_ref[2:3] += row_sum(gquery.astype(F32)) * SCALE
    gvec_ref[3:4] += row_sum(gvalues.astype(F32))
    gnormed = (
        dot(gquery, square(in_ref, 0), NT) * SCALE
        + dot(gkeys, square(in_ref, ROWS), NT)
        + dot(gvalues, square(in_ref, 2 * ROWS), NT)
    )
    gvec_ref[0:1] += row_sum(gnormed * normal)
    gvec_ref[1:2] += row_sum(gnormed)
    grad = gmid_ref[0] + norm_back(normal, rate, gnormed * vec_ref[0:1])
    out_ref[0] = grad.reshape(WH, WW, WT, D).astype(out_ref.dtype)

    @pl.when(step == pl.num_programs(0) - 1)
    def _():
        table_ref[...] = jnp.zeros_like(table_ref)
        for col in range(WW):
            wide_s[...] = jnp.zeros_like(wide_s)
            for row in range(WH):
                place = (row * WW + col) * WT
                low_lane = (WH - 1 - row) * WW * WT
                wide_s[:, low_lane : low_lane + WIN] += sum_s[:, place : place + WT, :].reshape(
                    HEADS * WT, WIN
                )
            for shift in range(2 * WH - 1):
                low_lane = (shift * (2 * WW - 1) + WW - 1 - col) * WT
                table_ref[:, low_lane : low_lane + WW * WT] += wide_s[
                    :, shift * WW * WT : (shift + 1) * WW * WT
                ]


def run_attention_backward(x, gattended, attended, rates, soft, qkv, gmiddle, pack, vec, dtype):
    windows = gmiddle.shape[0]
    return pl.pallas_call(
        attention_backward,
        grid=(windows,),
        in_specs=[
            grid_spec(x.shape),
            window_spec(WIN, D),
            window_spec(WIN, D),
            window_spec(HEADS, WIN),
            window_spec(HEADS, WIN, WIN),
            window_spec(WIN, 3 * D),
            window_spec(WIN, D),
            pack_spec(64, 0),
            whole_spec(12, D),
        ],
        out_specs=[
            grid_spec(x.shape),
            pl.BlockSpec((PACKS, 48, D), lambda i: (0, 0, 0)),
            pl.BlockSpec((4, D), lambda i: (0, 0)),
            pl.BlockSpec((HEADS * WT, CELLS * WT), lambda i: (0, 0)),
        ],
        out_shape=[
            jax.ShapeDtypeStruct(x.shape, dtype),
            jax.ShapeDtypeStruct((PACKS, 48, D), F32),
            jax.ShapeDtypeStruct((4, D), F32),
            jax.ShapeDtypeStruct((HEADS * WT, CELLS * WT), F32),
        ],
        scratch_shapes=[
            pltpu.VMEM((HEADS, WIN, WIN), F32),
            pltpu.VMEM((D, WIN), BF16),
            pltpu.VMEM((D, WIN), F32),
            pltpu.VMEM((WIN, D), BF16),
            pltpu.VMEM((WIN, D), BF16),
            pltpu.VMEM((WIN, D), BF16),
            pltpu.VMEM((HEADS * WT, (2 * WH - 1) * WW * WT), F32),
        ],
        compiler_params=params(),
    )(x, gattended, attended, rates, soft, qkv, gmiddle, pack, vec)


def expand_bias(cells_ref, out_ref, wide_s):
    for col in range(WW):
        for shift in range(2 * WH - 1):
            low_lane = (shift * (2 * WW - 1) + WW - 1 - col) * WT
            wide_s[:, shift * WW * WT : (shift + 1) * WW * WT] = cells_ref[
                0, :, low_lane : low_lane + WW * WT
            ]
        for row in range(WH):
            place = (row * WW + col) * WT
            low_lane = (WH - 1 - row) * WW * WT
            out_ref[0, :, place : place + WT, :] = wide_s[:, low_lane : low_lane + WIN].reshape(
                HEADS, WT, WIN
            )


def run_expand_bias(cells):
    return pl.pallas_call(
        expand_bias,
        grid=(LAYERS,),
        in_specs=[pl.BlockSpec((1, HEADS * WT, CELLS * WT), lambda i: (i, 0, 0))],
        out_specs=pl.BlockSpec((1, HEADS, WIN, WIN), lambda i: (i, 0, 0, 0)),
        out_shape=jax.ShapeDtypeStruct((LAYERS, HEADS, WIN, WIN), F32),
        scratch_shapes=[pltpu.VMEM((HEADS * WT, (2 * WH - 1) * WW * WT), F32)],
        compiler_params=params(),
    )(cells)


def offset_places():
    frame, row, col = np.meshgrid(
        np.arange(1 - WT, WT), np.arange(1 - WH, WH), np.arange(1 - WW, WW), indexing="ij"
    )

    def place(f, r, c):
        return (np.maximum(f, 0) * WH + np.maximum(r, 0)) * WW + np.maximum(c, 0)

    return (place(frame, row, col) * WIN + place(-frame, -row, -col)).reshape(-1)


def select_rows(tables, chosen, dims):
    flat = tables.transpose(1, 0, 2).reshape(BIAS_ROWS, LAYERS * HEADS)
    pieces = dot(chosen, jnp.concatenate(split_three(flat), axis=1), dims)
    width = LAYERS * HEADS
    total = pieces[:, :width] + pieces[:, width : 2 * width] + pieces[:, 2 * width :]
    return total.reshape(BIAS_ROWS, LAYERS, HEADS).transpose(1, 0, 2)


def bias_cells(tables, chosen):
    taken = select_rows(tables, chosen, (((1,), (0,)), ((), ())))
    taken = taken.transpose(1, 0, 2).reshape(BIAS_ROWS, LAYERS * HEADS)
    taken = (taken * LOG2E).reshape(2 * WT - 1, CELLS, LAYERS * HEADS).transpose(2, 1, 0)
    placed = jnp.stack([taken[:, :, WT - 1 - t : 2 * WT - 1 - t] for t in range(WT)], axis=1)
    return placed.reshape(LAYERS, HEADS * WT, CELLS * WT)


def cells_to_rows(cells):
    shaped = cells.reshape(LAYERS, HEADS, WT, CELLS, WT)
    parts = [
        jnp.pad(shaped[:, :, t], ((0, 0), (0, 0), (0, 0), (WT - 1 - t, t))) for t in range(WT)
    ]
    total = functools.reduce(jnp.add, parts)
    return total.transpose(0, 3, 2, 1).reshape(LAYERS, BIAS_ROWS, HEADS)


def spatial_blocks(field):
    clip_count, frames_here, width = (field.shape[0], field.shape[1], field.shape[-1])
    shaped = field.reshape(clip_count, frames_here, HGT // WH, WH, WID // WW, WW, width)
    shaped = shaped.transpose(0, 2, 4, 1, 3, 5, 6)
    return shaped.reshape(clip_count * (HGT // WH) * (WID // WW), frames_here, WH * WW, width)


def roll_space(field, amount, first):
    return jnp.roll(field, (amount, amount), axis=(first, first + 1))


def swap_halves(part):
    return lax.ppermute(part, "seq", [(0, 1), (1, 0)])


class Placement:
    def __init__(self, clip_count, frames_here):
        self.clips = clip_count
        self.frames = frames_here
        self.parts = lax.axis_size("seq")
        self.near = self.parts == 2 and frames_here == WT

    def grid_shape(self):
        if self.near:
            return (self.clips, HGT, WID, WT, D)
        columns = self.clips * 4 // self.parts
        return (columns * 2, WH, WW, WT, D)

    def enter(self, field, shifted):
        if self.near:
            if shifted:
                arrived = swap_halves(field[:, :SHIFT_T])
                field = jnp.concatenate([field[:, SHIFT_T:], arrived], axis=1)
                field = roll_space(field, -SHIFT_S, 2)
            return field.transpose(0, 2, 3, 1, 4)
        if shifted:
            field = roll_space(field, -SHIFT_S, 2)
        columns = lax.all_to_all(
            spatial_blocks(field), "seq", split_axis=0, concat_axis=1, tiled=True
        )
        if shifted:
            columns = jnp.roll(columns, -SHIFT_T, axis=1)
        windows = columns.reshape(-1, WT, WH, WW, D)
        return windows.transpose(0, 2, 3, 1, 4)

    def leave(self, grid, shifted):
        if self.near:
            field = grid.transpose(0, 3, 1, 2, 4)
            if shifted:
                field = roll_space(field, SHIFT_S, 2)
                arrived = swap_halves(field[:, SHIFT_T:])
                field = jnp.concatenate([arrived, field[:, :SHIFT_T]], axis=1)
            return field
        columns = grid.transpose(0, 3, 1, 2, 4).reshape(-1, FRAMES, WH * WW, D)
        if shifted:
            columns = jnp.roll(columns, SHIFT_T, axis=1)
        columns = lax.all_to_all(columns, "seq", split_axis=1, concat_axis=0, tiled=True)
        shaped = columns.reshape(self.clips, HGT // WH, WID // WW, self.frames, WH, WW, D)
        shaped = shaped.transpose(0, 3, 1, 4, 2, 5, 6)
        field = shaped.reshape(self.clips, self.frames, HGT, WID, D)
        return roll_space(field, SHIFT_S, 2) if shifted else field

    def forth(self, grid):
        if self.near:
            arrived = swap_halves(grid[..., :SHIFT_T, :])
            grid = jnp.concatenate([grid[..., SHIFT_T:, :], arrived], axis=3)
            return roll_space(grid, -SHIFT_S, 1)
        return self.enter(self.leave(grid, False), True)

    def back(self, grid):
        if self.near:
            grid = roll_space(grid, SHIFT_S, 1)
            arrived = swap_halves(grid[..., SHIFT_T:, :])
            return jnp.concatenate([arrived, grid[..., :SHIFT_T, :]], axis=3)
        return self.enter(self.leave(grid, True), False)

    def mask_lanes(self):
        if self.near:
            index = jnp.arange(self.clips * 4, dtype=jnp.int32)
            late = jnp.full(index.shape, lax.axis_index("seq"), jnp.int32)
            block = index % 4
        else:
            columns = self.clips * 4 // self.parts
            index = jnp.arange(columns * 2, dtype=jnp.int32)
            late = index % 2
            block = (lax.axis_index("seq") * columns + index // 2) % 4
        place = np.arange(WIN)
        frame_late = jnp.asarray(place % WT >= WT - SHIFT_T).astype(jnp.int32)
        row_late = jnp.asarray(place // (WT * WW) >= WH - SHIFT_S).astype(jnp.int32)
        col_late = jnp.asarray(place // WT % WW >= WW - SHIFT_S).astype(jnp.int32)
        region = (
            late[:, None] * frame_late * 4
            + (block // 2)[:, None] * row_late * 2
            + (block % 2)[:, None] * col_late
        )
        lane = np.arange(128)
        same = (region[:, :, None] == lane % 8) & (lane < 24)
        pieces = []
        rest = np.float32(MASKED * LOG2E)
        for _ in range(3):
            piece = np.float32(np.asarray(rest).astype(BF16))
            pieces.append(piece)
            rest = np.float32(rest - piece)
        piece_of = np.zeros((128,), np.float32)
        for number, piece in enumerate(pieces):
            piece_of[8 * number : 8 * number + 8] = -piece
            piece_of[24 + number] = piece
        always = (lane >= 24) & (lane < 27)
        on_keys = jnp.where(same | always, 1.0, 0.0)
        return (on_keys * piece_of).astype(BF16), on_keys.astype(BF16)


def pack_layer(inner, outer, up, down):
    parts = [inner[:, i * D : (i + 1) * D] for i in range(3)] + [outer]
    parts = parts + [up[:, i * D : (i + 1) * D] for i in range(4)] + [down]
    return jnp.concatenate(parts, axis=0)


def per_device(
    clips_in,
    cotangent,
    offset_index,
    first_gain,
    first_shift,
    inner_weight,
    inner_bias,
    outer_weight,
    outer_bias,
    second_gain,
    second_shift,
    up_weight,
    up_bias,
    down_weight,
    down_bias,
    bias_table,
):
    place = Placement(clips_in.shape[0], clips_in.shape[1])
    rows = inner_weight.shape[1]
    devices = D // rows
    vectors = [
        first_gain, first_shift, inner_bias, outer_bias, second_gain, second_shift,
        down_bias, up_bias,
    ]
    vec_pack = jnp.concatenate(vectors, axis=1)
    width = vec_pack.shape[1]
    vec_rows = jnp.pad(vec_pack, ((0, 0), (0, D - width)))[:, None]
    vec_rows = jnp.pad(vec_rows, ((0, 0), (0, 7), (0, 0)))

    def gathered(layer):
        local = pack_layer(
            inner_weight[layer], outer_weight[layer], up_weight[layer], down_weight[layer]
        )
        local = jnp.concatenate([local, vec_rows[layer]], axis=0)
        full = lax.all_gather(local, AXES, axis=0)
        held = full[:, 12 * rows, :width].astype(F32)
        pieces = []
        start = 0
        for vector in vectors:
            size = vector.shape[1]
            pieces.append(held[:, start : start + size].reshape(-1, D))
            start += size
        vec = jnp.concatenate(pieces, axis=0)
        if rows != ROWS:
            parts = [
                full[:, i * rows : (i + 1) * rows].reshape(PACKS, ROWS, D) for i in range(8)
            ]
            parts.append(full[:, 8 * rows : 12 * rows].reshape(PACKS, 4 * ROWS, D))
            full = jnp.concatenate(parts, axis=1)
        return full, vec

    weights = [gathered(layer) for layer in range(LAYERS)]
    taken_rows = jnp.take(offset_index.reshape(-1), offset_places())
    order = jnp.arange(BIAS_ROWS, dtype=jnp.int32)
    chosen = (taken_rows[:, None] == order[None, :]).astype(BF16)
    bias = run_expand_bias(bias_cells(bias_table, chosen))
    shape = place.grid_shape()
    aug = place.mask_lanes()

    x_zero = place.enter(clips_in, False)
    upstream = place.enter(cotangent, True)
    saved = []
    x = x_zero
    for layer in range(LAYERS):
        pack, vec = weights[layer]
        qkv, soft, rates, attended, middle = run_attention_forward(
            x, pack, vec, bias[layer], aug if layer == 1 else None
        )
        active, slope, result = run_feed_forward(
            middle, pack, vec, shape, F32 if layer == 0 else BF16
        )
        saved.append((x, qkv, soft, rates, attended, middle, active, slope))
        x = place.forth(result) if layer == 0 else result
    clips_out = place.leave(x, True)

    scattered = [None] * LAYERS
    vec_parts = [None] * LAYERS
    cell_parts = [None] * LAYERS

    def scatter(value, blocks):
        if rows != ROWS:
            per = ROWS // rows
            parts = []
            start = 0
            for size in blocks:
                part = value[:, start : start + size].reshape(PACKS * per, size // per, D)
                parts.append(part)
                start += size
            value = jnp.concatenate(parts, axis=1)
        return lax.psum_scatter(value, AXES, scatter_dimension=0, tiled=False)

    for layer in reversed(range(LAYERS)):
        pack, vec = weights[layer]
        x, qkv, soft, rates, attended, middle, active, slope = saved[layer]
        gmiddle, gattended, big, gvec_two = run_feed_backward(
            upstream, active, slope, middle, attended, pack, vec
        )
        upstream, small, gvec_one, cells = run_attention_backward(
            x, gattended, attended, rates, soft, qkv, gmiddle, pack, vec,
            F32 if layer == 1 else BF16,
        )
        scattered[layer] = (
            scatter(big, [ROWS] * 5 + [4 * ROWS]),
            scatter(small, [ROWS] * 3),
        )
        vec_parts[layer] = jnp.concatenate([gvec_one, gvec_two], axis=0)
        cell_parts[layer] = cells
        if layer == 1:
            upstream = place.back(upstream)
    clips_grad = place.leave(upstream, False)

    table_rows = cells_to_rows(jnp.stack(cell_parts))
    vec_total, table_total = lax.psum((jnp.stack(vec_parts), table_rows), AXES)
    table_total = select_rows(table_total, chosen, TN)

    device = lax.axis_index(AXES)

    def own(first, count):
        whole = vec_total[:, first : first + count].reshape(LAYERS, count * D)
        size = count * D // devices
        return lax.dynamic_slice_in_dim(whole, device * size, size, axis=1)

    def both(which, first, count):
        parts = []
        for layer in range(LAYERS):
            value = scattered[layer][which]
            columns = [
                value[first + i * rows : first + (i + 1) * rows] for i in range(count)
            ]
            parts.append(jnp.concatenate(columns, axis=1))
        return jnp.stack(parts)

    down = jnp.stack([scattered[layer][0][5 * rows : 9 * rows] for layer in range(LAYERS)])
    return (
        clips_out,
        clips_grad,
        own(0, 1),
        own(1, 1),
        both(1, 0, 3),
        own(2, 2),
        both(0, 0, 1),
        own(4, 1),
        own(5, 1),
        own(6, 1),
        both(0, rows, 4),
        own(8, 4),
        down,
        own(7, 1),
        table_total,
    )


def solution(mesh):
    clips = P("batch", "seq", None, None, None)
    vector = P(None, AXES)
    matrix = P(None, AXES, None)
    return jax.shard_map(
        per_device,
        mesh=mesh,
        in_specs=(
            clips, clips, P(), vector, vector, matrix, vector, matrix, vector, vector, vector,
            matrix, vector, matrix, vector, P(),
        ),
        out_specs=(
            clips, clips, vector, vector, matrix, vector, matrix, vector, vector, vector,
            matrix, vector, matrix, vector, P(),
        ),
        check_vma=False,
    )
```

time: 5140 us -> 1500 us (0.29)
  other arithmetic: 2320 us -> 37.5 us
  local copies, waits for them, and re-layouts: 1410 us -> 137 us
  matrix products: 797 us -> 10.2 us
  Pallas kernels: 0 us -> 535 us
  waiting for transfers between devices: 214 us -> 708 us
  blocking collectives: 274 us -> 40.6 us
  starting transfers between devices: 79.3 us -> 4.51 us
    scatter-add x2 -> x0, other arithmetic: 1640 us -> none  [per_device(): jax.ops.segment_sum(table_terms.transpose(1, 2, 0).reshape(-1, HEADS), of...]
    dot_general x38 -> x2, matrix products: 797 us -> 10.2 us  [dot(): return lax.dot_general(left, right, dims, preferred_element_type=F32)]
    gather x5 -> x1, local copies, waits for them, and re-layouts: 675 us -> 13.6 us  [per_device(): taken_rows = jnp.take(offset_index.reshape(-1), offset_places())]
    pallas_call x0 -> x9, Pallas kernels: none -> 535 us  [the longest x2 200 us: run_attention_backward(): pl.pallas_call(attention_backward, grid=(windows,), in_specs=[grid_spec(x...]
    reduce_scatter x8 -> x4, waiting for transfers between devices: 0.05 us -> 484 us  [scatter(): return lax.psum_scatter(value, AXES, scatter_dimension=0, tiled=False)]
    reduce_sum x22 -> x0, other arithmetic: 358 us -> none  [the longest x2 191 us: attend_backward(): jnp.sum(total_grad, axis=0)]
    convert_element_type x22 -> x0, local copies, waits for them, and re-layouts: 209 us -> none  [the longest x5 53.2 us: attend_backward(): values_grad.reshape(flat_shape).astype(jnp.bfloat16)]
    all_gather x2 -> x0, blocking collectives: 192 us -> none  [per_device(): lax.all_gather(outer_weight[layer], ('batch', 'seq'), axis=0, tiled=True)]
  transfers between devices with their start and end apart: 31 -> 11, of which waited for: 9 -> 8; matrix products, arithmetic and copies ran while one was open for 82% -> 9% of each run, Pallas kernels for 0% -> 8%
where the time goes in v1:
time: 1500 us; the launch traced here: 1490 us
  waiting for transfers between devices  708 us (47%)
  Pallas kernels  535 us (36%)
  local copies, waits for them, and re-layouts  137 us (9%)
  blocking collectives  40.6 us (3%)
  other arithmetic  37.5 us (2%)
  between operations  15.3 us (1%)
    reduce_scatter x4, waiting for transfers between devices, scatter(): return lax.psum_scatter(value, AXES, scatter_dimension=0, tiled=False)  484 us
    pallas_call x2, Pallas kernels, run_attention_backward(): pl.pallas_call(attention_backward, grid=(windows,), in_specs=[grid_spec(x...  200 us
    ppermute x4, waiting for transfers between devices, swap_halves(): return lax.ppermute(part, 'seq', [(0, 1), (1, 0)])  186 us
    pallas_call x2, Pallas kernels, run_attention_forward(): pl.pallas_call(functools.partial(attention_forward, masked), grid=(window...  156 us
    pallas_call x2, Pallas kernels, run_feed_backward(): pl.pallas_call(feed_backward, grid=(windows,), in_specs=[grid_spec(grad.s...  105 us
    pallas_call x2, Pallas kernels, run_feed_forward(): pl.pallas_call(feed_forward, grid=(windows,), in_specs=[window_spec(WIN,...  57.3 us
    psum x1, blocking collectives, per_device(): vec_total, table_total = lax.psum((jnp.stack(vec_parts), table_rows), AXES)  40.6 us
    psum x1, waiting for transfers between devices, per_device(): vec_total, table_total = lax.psum((jnp.stack(vec_parts), table_rows), AXES)  36.2 us
  transfers between devices with their start and end apart: 11, of which 8 were waited for; matrix products, arithmetic and copies ran while one was open for 9% of the time, Pallas kernels for 8%

profile of v1, /device:TPU:25, one launch (start us, length us, event | category | flops | bytes accessed | tf_op | source)
XLA Modules:
  0.0 1488.1 jit_solution(17354349521367873018)
XLA Ops:
  15.0 13.6 gather_fusion
  34.8 10.9 copy.196
  45.7 16.8 %reshape.298.cells_ref = f32[2,128,1352]{2,1,0:T(8,128)} reshape(f32[32,8,169,8]{3,2,1,0:T(8,128)} %copy.196) | data formatting | bytes 2768896 | tf_op jit(solution)/shard_map/reshape | solution.py:493
  62.5 17.4 %shard_map.343 = f32[2,16,392,392]{3,2,1,0:T(8,128)} custom-call(f32[2,128,1352]{2,1,0:T(8,128)} %reshape.298.cells_ref), custom_call_target="tpu_custom_call" | custom-call | tf_op jit(solution)/shard_map/pallas_call | solution.py:458
  79.9 17.0 %slice_bitcast_fusion = (f32[16,392,392]{2,1,0:T(8,128)}, f32[16,392,392]{2,1,0:T(8,128)}) fusion(f32[2,16,392,392]{3,2,1,0:T(8,128)} %shard_map.343), kind=kLoop, calls=%fused_computation.6 | loop fusion | bytes 39337984 | tf_op jit(solution)/shard_map/squeeze | solution.py:690
  99.9 76.3 %shard_map.344 = (bf16[8,392,1536]{2,1,0:T(8,128)(2,1)}, bf16[8,16,392,392]{3,2,1,0:T(8,128)(2,1)}, f32[8,16,392]{2,1,0:T(8,128)}, bf16[8,392,512]{2,1,0:T(8,128)(2,1)}, f32[8,392,512]{2,1,0:T(8,128)}) custom-call(bf16[2,14,14,8,512]{4,3,2,1,0:T(8,128)(2,1)} %bitcast.191, bf16[32,200,512]{2,1,0:T(8,128)(2,1)} %bitcast.176, ...), custom_call_target="tpu_custom_call" | custom-call | tf_op jit(solution)/shard_map/pallas_call | solution.py:157
  176.2 28.6 %shard_map.345 = (bf16[8,392,2048]{2,1,0:T(8,128)(2,1)}, bf16[8,392,2048]{2,1,0:T(8,128)(2,1)}, f32[2,14,14,8,512]{4,3,2,1,0:T(8,128)}) custom-call(f32[8,392,512]{2,1,0:T(8,128)} %get-tuple-element.47.mid_ref, bf16[32,200,512]{2,1,0:T(8,128)(2,1)} %bitcast.177, bf16[32,200,512]{2,1,0:T(8,128)(2,1)} %bitcast.178, f32[12,512]{1,0:T(8,128)} %concatenate.86.refs_2_.vec_ref), custom_call_target="tpu_custom_call" | custom-call | tf_op jit(solution)/shard_map/pallas_call | solution.py:210
  219.2 99.3 %collective-permute-done.2 = bf16[2,4,14,14,512]{4,1,3,2,0:T(4,128)(2,1)} collective-permute-done((bf16[2,4,14,14,512]{4,1,3,2,0:T(4,128)(2,1)}, bf16[2,4,14,14,512]{4,1,3,2,0:T(4,128)(2,1)}, u32[]{:S(2)}, u32[]{:S(2)}) %collective-permute-start.2) | collective-permute-done | bytes 1605664 | tf_op jit(solution)/shard_map/ppermute | solution.py:517
  338.9 79.3 %shard_map.346 = (bf16[8,392,1536]{2,1,0:T(8,128)(2,1)}, bf16[8,16,392,392]{3,2,1,0:T(8,128)(2,1)}, f32[8,16,392]{2,1,0:T(8,128)}, bf16[8,392,512]{2,1,0:T(8,128)(2,1)}, f32[8,392,512]{2,1,0:T(8,128)}) custom-call(f32[2,14,14,8,512]{4,3,2,1,0:T(8,128)} %fusion.5.refs_0_.x_ref, bf16[32,200,512]{2,1,0:T(8,128)(2,1)} %bitcast.168, ...), custom_call_target="tpu_custom_call" | custom-call | tf_op jit(solution)/shard_map/pallas_call | solution.py:157
  418.1 28.6 %shard_map.347 = (bf16[8,392,2048]{2,1,0:T(8,128)(2,1)}, bf16[8,392,2048]{2,1,0:T(8,128)(2,1)}, bf16[2,14,14,8,512]{4,3,2,1,0:T(8,128)(2,1)}) custom-call(f32[8,392,512]{2,1,0:T(8,128)} %get-tuple-element.49.mid_ref, bf16[32,200,512]{2,1,0:T(8,128)(2,1)} %bitcast.169, bf16[32,200,512]{2,1,0:T(8,128)(2,1)} %bitcast.170, f32[12,512]{1,0:T(8,128)} %concatenate.92.refs_2_.vec_ref), custom_call_target="tpu_custom_call" | custom-call | tf_op jit(solution)/shard_map/pallas_call | solution.py:210
  446.8 52.6 %shard_map.348 = (f32[8,392,512]{2,1,0:T(8,128)}, bf16[8,392,512]{2,1,0:T(8,128)(2,1)}, f32[32,144,512]{2,1,0:T(8,128)}, f32[8,512]{1,0:T(8,128)}) custom-call(bf16[2,14,14,8,512]{4,3,2,1,0:T(8,128)(2,1)} %fusion.9.grad_ref, bf16[8,392,2048]{2,1,0:T(8,128)(2,1)} %get-tuple-element.51.act_ref, bf16[8,392,2048]{2,1,0:T(8,128)(2,1)} %get-tuple-element.52.slope_ref, ...), custom_call_target="tpu_custom_call" | custom-call | tf_op jit(solution)/shard_map/pallas_call | solution.py:273
  499.3 99.9 %shard_map.349 = (f32[2,14,14,8,512]{4,3,2,1,0:T(8,128)}, f32[32,48,512]{2,1,0:T(8,128)}, f32[4,512]{1,0:T(4,128)}, f32[128,1352]{1,0:T(8,128)}) custom-call(f32[2,14,14,8,512]{4,3,2,1,0:T(8,128)} %fusion.5.refs_0_.x_ref, bf16[8,392,512]{2,1,0:T(8,128)(2,1)} %get-tuple-element.54.gatt_ref, bf16[8,392,512]{2,1,0:T(8,128)(2,1)} %get-tuple-element.53.att_ref, ...), custom_call_target="tpu_custom_call" | custom-call | tf_op jit(solution)/shard_map/pallas_call | solution.py:403
  609.5 8.7 reshape.300
  626.1 52.0 %collective-permute-done.3 = f32[2,14,14,4,512]{4,3,2,1,0:T(4,128)} collective-permute-done((f32[2,14,14,4,512]{4,3,2,1,0:T(4,128)}, f32[2,14,14,4,512]{4,3,2,1,0:T(4,128)}, u32[]{:S(2)}, u32[]{:S(2)}) %collective-permute-start.3) | collective-permute-done | bytes 3211296 | tf_op jit(solution)/shard_map/ppermute | solution.py:517
  684.1 52.5 %shard_map.350 = (f32[8,392,512]{2,1,0:T(8,128)}, bf16[8,392,512]{2,1,0:T(8,128)(2,1)}, f32[32,144,512]{2,1,0:T(8,128)}, f32[8,512]{1,0:T(8,128)}) custom-call(f32[2,14,14,8,512]{4,3,2,1,0:T(8,128)} %pad_maximum_fusion.5.grad_ref, bf16[8,392,2048]{2,1,0:T(8,128)(2,1)} %get-tuple-element.60.act_ref, bf16[8,392,2048]{2,1,0:T(8,128)(2,1)} %get-tuple-element.61.slope_ref, ...), custom_call_target="tpu_custom_call" | custom-call | tf_op jit(solution)/shard_map/pallas_call | solution.py:273
  736.6 99.8 %shard_map.351 = (bf16[2,14,14,8,512]{4,3,2,1,0:T(8,128)(2,1)}, f32[32,48,512]{2,1,0:T(8,128)}, f32[4,512]{1,0:T(4,128)}, f32[128,1352]{1,0:T(8,128)}) custom-call(bf16[2,14,14,8,512]{4,3,2,1,0:T(8,128)(2,1)} %bitcast.192, bf16[8,392,512]{2,1,0:T(8,128)(2,1)} %get-tuple-element.63.gatt_ref, bf16[8,392,512]{2,1,0:T(8,128)(2,1)} %get-tuple-element.62.att_ref, ...), custom_call_target="tpu_custom_call" | custom-call | tf_op jit(solution)/shard_map/pallas_call | solution.py:403
  836.4 8.6 reshape.299
  860.8 34.3 %collective-permute-done.1 = bf16[2,4,14,14,512]{4,1,3,2,0:T(4,128)(2,1)} collective-permute-done((bf16[2,4,14,14,512]{4,1,3,2,0:T(4,128)(2,1)S(1)}, bf16[2,4,14,14,512]{4,1,3,2,0:T(4,128)(2,1)}, u32[]{:S(2)}, u32[]{:S(2)}) %collective-permute-start.1) | collective-permute-done | bytes 1605664 | tf_op jit(solution)/shard_map/ppermute | solution.py:517
  899.9 40.6 %psum.14 = f32[2,12,512]{2,1,0:T(8,128)S(1)} all-reduce(f32[2,12,512]{2,1,0:T(8,128)S(1)} %pad_maximum_fusion.16), channel_id=1, replica_groups=mesh['batch'=16,'seq'=2] {'batch','seq'}, use_global_device_ids=true, to_apply=%region_0.1 | all-reduce | flops 12288 | bytes 98304 | tf_op jit(solution)/shard_map/psum | solution.py:736
  945.6 36.2 %all-reduce.12.cloned.1.call-done = f32[2535,32]{0,1:T(8,128)} async-done(((f32[2535,32]{0,1:T(8,128)}), f32[2535,32]{0,1:T(8,128)}) %all-reduce.12.cloned.1.call-update) | async-done | bytes 324496 | tf_op jit(solution)/shard_map/psum | solution.py:736
  988.9 99.6 %reduce-scatter.7.cloned.1.call-done = f32[1,48,512]{2,1,0:T(8,128)} async-done(((f32[32,48,512]{2,1,0:T(8,128)}), f32[1,48,512]{2,1,0:T(8,128)}) %reduce-scatter.7.cloned.1.call-update) | async-done | bytes 98320 | tf_op jit(solution)/shard_map/reduce_scatter | solution.py:713
  1089.4 105.9 %reduce-scatter.5.cloned.1.call-done = f32[1,48,512]{2,1,0:T(8,128)} async-done(((f32[32,48,512]{2,1,0:T(8,128)}), f32[1,48,512]{2,1,0:T(8,128)}) %reduce-scatter.5.cloned.1.call-update) | async-done | bytes 98320 | tf_op jit(solution)/shard_map/reduce_scatter | solution.py:713
  1196.7 139.7 %reduce-scatter.11.cloned.1.call-done = f32[1,144,512]{2,1,0:T(8,128)} async-done(((f32[32,144,512]{2,1,0:T(8,128)}), f32[1,144,512]{2,1,0:T(8,128)}) %reduce-scatter.11.cloned.1.call-update) | async-done | bytes 294928 | tf_op jit(solution)/shard_map/reduce_scatter | solution.py:713
  1338.2 138.8 %reduce-scatter.9.cloned.1.call-done = f32[1,144,512]{2,1,0:T(8,128)} async-done(((f32[32,144,512]{2,1,0:T(8,128)}), f32[1,144,512]{2,1,0:T(8,128)}) %reduce-scatter.9.cloned.1.call-update) | async-done | bytes 294928 | tf_op jit(solution)/shard_map/reduce_scatter | solution.py:713
  (190 shorter events, 116.1 us)
Async XLA Ops:
  7.2 7.8 copy-start.9
  7.2 89.7 %all-gather.5.cloned.1.call-start = ((), (), s32[]{:S(2)}) async-start(), calls=%async_computation.9 | async-start | bytes 6758400 | tf_op jit(solution)/shard_map/all_gather | solution.py:658
  12.3 313.9 %all-gather.7.cloned.1.call-start = ((), (), s32[]{:S(2)}) async-start(), calls=%async_computation.10 | async-start | bytes 6758400 | tf_op jit(solution)/shard_map/all_gather | solution.py:658
  13.1 968.7 %all-reduce.12.cloned.1.call-start = ((), (), s32[]{:S(2)}) async-start(), calls=%async_computation.8 | async-start | bytes 655360 | tf_op jit(solution)/shard_map/psum | solution.py:736
  15.0 13.6 copy-start.4
  28.7 5.1 copy-start.10
  204.8 9.7 copy-start.3
  213.1 4.4 copy-start.16
  213.2 4.4 copy-start.17
  213.2 4.4 copy-start.18
  213.2 4.4 copy-start.19
  213.2 116.1 %collective-permute-start = (f32[2,14,14,4,512]{4,3,2,1,0:T(4,128)}, f32[2,14,14,4,512]{4,3,2,1,0:T(4,128)}, u32[]{:S(2)}, u32[]{:S(2)}) collective-permute-start(f32[2,14,14,4,512]{4,3,2,1,0:T(4,128)} %get-tuple-element.83), channel_id=1, source_target_pairs={{0,1},{1,0},{2,3},{3,2},{4,5},{5,4},{6,7},{7,6},{8,9},{9,8},{10,11... | collective-permute-start | bytes 9633800 | tf_op jit(solution)/shard_map/ppermute | solution.py:517
  217.2 101.2 %collective-permute-start.2 = (bf16[2,4,14,14,512]{4,1,3,2,0:T(4,128)(2,1)}, bf16[2,4,14,14,512]{4,1,3,2,0:T(4,128)(2,1)}, u32[]{:S(2)}, u32[]{:S(2)}) collective-permute-start(bf16[2,4,14,14,512]{4,1,3,2,0:T(4,128)(2,1)} %get-tuple-element.85), channel_id=1, source_target_pairs={{0,1},{1,0},{2,3},{3,2},{4,5},{5,4},{6,7},{7,6},{8,9},{9,8},{10,11... | collective-permute-start | bytes 4816904 | tf_op jit(solution)/shard_map/ppermute | solution.py:517
  219.2 102.2 %copy-start = (bf16[2,4,14,14,512]{4,1,3,2,0:T(4,128)(2,1)S(1)}, bf16[2,4,14,14,512]{4,1,3,2,0:T(4,128)(2,1)}, u32[]{:S(2)}) copy-start(bf16[2,4,14,14,512]{4,1,3,2,0:T(4,128)(2,1)} %get-tuple-element.86) | copy-start | bytes 4816900
  608.2 69.9 %collective-permute-start.3 = (f32[2,14,14,4,512]{4,3,2,1,0:T(4,128)}, f32[2,14,14,4,512]{4,3,2,1,0:T(4,128)}, u32[]{:S(2)}, u32[]{:S(2)}) collective-permute-start(f32[2,14,14,4,512]{4,3,2,1,0:T(4,128)} %get-tuple-element.81), channel_id=1, source_target_pairs={{0,1},{1,0},{2,3},{3,2},{4,5},{5,4},{6,7},{7,6},{8,9},{9,8},{10,11... | collective-permute-start | bytes 9633800 | tf_op jit(solution)/shard_map/ppermute | solution.py:517
  844.9 7.5 copy-start.1
  854.1 234.5 %reduce-scatter.7.cloned.1.call-start = ((), (), s32[]{:S(2)}) async-start(), calls=%async_computation.5 | async-start | bytes 3244032 | tf_op jit(solution)/shard_map/reduce_scatter | solution.py:713
  854.7 340.6 %reduce-scatter.5.cloned.1.call-start = ((), (), s32[]{:S(2)}) async-start(), calls=%async_computation.4 | async-start | bytes 3244032 | tf_op jit(solution)/shard_map/reduce_scatter | solution.py:713
  855.2 481.2 %reduce-scatter.11.cloned.1.call-start = ((), (), s32[]{:S(2)}) async-start(), calls=%async_computation.7 | async-start | bytes 9732096 | tf_op jit(solution)/shard_map/reduce_scatter | solution.py:713
  855.8 621.2 %reduce-scatter.9.cloned.1.call-start = ((), (), s32[]{:S(2)}) async-start(), calls=%async_computation.6 | async-start | bytes 9732096 | tf_op jit(solution)/shard_map/reduce_scatter | solution.py:713
  859.4 35.7 %collective-permute-start.1 = (bf16[2,4,14,14,512]{4,1,3,2,0:T(4,128)(2,1)S(1)}, bf16[2,4,14,14,512]{4,1,3,2,0:T(4,128)(2,1)}, u32[]{:S(2)}, u32[]{:S(2)}) collective-permute-start(bf16[2,4,14,14,512]{4,1,3,2,0:T(4,128)(2,1)S(1)} %get-tuple-element.87), channel_id=1, source_target_pairs={{0,1},{1,0},{2,3},{3,2},{4,5},{5,4},{6,7},{7,6},{8,9},{9,8},{10,11... | collective-permute-start | bytes 4816904 | tf_op jit(solution)/shard_map/ppermute | solution.py:517
  895.1 4.7 copy-start.8
  895.1 4.7 copy-start.13
  895.1 87.8 %copy-start.11 = (s32[2535]{0:T(1024)S(1)}, s32[2535]{0:T(1024)}, u32[]{:S(2)}) copy-start(s32[2535]{0:T(1024)} %copy-done.10) | copy-start | bytes 30424
  (8 other events, 21.3 us)
Sparse Core Ops, SparseCore 0:
  12.5 70.6 all-gather.4
  86.6 69.2 all-gather.6
  854.2 127.5 all-reduce.11
  988.0 100.5 reduce-scatter.6
  1094.7 100.4 reduce-scatter.4
  1202.0 134.3 reduce-scatter.10
  1342.3 134.5 reduce-scatter.8

commit v2 on v1

--- a/solution.py
+++ b/solution.py
@@ -44,6 +44,12 @@
 def params():
     return pltpu.CompilerParams(
         vmem_limit_bytes=61 * 1024 * 1024, dimension_semantics=("arbitrary",)
+    )
+
+
+def cost(windows, microseconds):
+    return pl.CostEstimate(
+        flops=int(windows * microseconds * 1e9), bytes_accessed=0, transcendentals=0
     )
 
 
@@ -179,6 +185,7 @@
             jax.ShapeDtypeStruct((windows, WIN, D), F32),
         ],
         scratch_shapes=[pltpu.VMEM((D, WIN), BF16), pltpu.VMEM((D, WIN), F32)],
+        cost_estimate=cost(windows, 10),
         compiler_params=params(),
     )(x, pack, vec, bias, *extra)
 
@@ -222,6 +229,7 @@
             jax.ShapeDtypeStruct((windows, WIN, FF), BF16),
             jax.ShapeDtypeStruct(grid_shape, dtype),
         ],
+        cost_estimate=cost(windows, 4),
         compiler_params=params(),
     )(middle, pack, pack, vec)
 
@@ -234,7 +242,7 @@
 
 def feed_backward(
     grad_ref, act_ref, slope_ref, mid_ref, att_ref, in_ref, up_ref, down_ref, vec_ref,
-    gmid_ref, gatt_ref, pack_ref, gvec_ref,
+    gmid_ref, gatt_ref, result_ref, gvec_ref, pack_ref,
 ):
     @pl.when(pl.program_id(0) == 0)
     def _():
@@ -267,8 +275,12 @@
     pack_ref[:, 0:ROWS, :] += dot(att_ref[0], gmid_low, TN).reshape(PACKS, ROWS, D)
     gatt_ref[0] = dot(gmid_low, square(in_ref, 3 * ROWS), NT).astype(BF16)
 
-
-def run_feed_backward(grad, active, slope, middle, attended, pack, vec):
+    @pl.when(pl.program_id(0) == pl.num_programs(0) - 1)
+    def _():
+        result_ref[...] = pack_ref[...].astype(result_ref.dtype)
+
+
+def run_feed_backward(grad, active, slope, middle, attended, pack, vec, dtype):
     windows = middle.shape[0]
     return pl.pallas_call(
         feed_backward,
@@ -287,23 +299,25 @@
         out_specs=[
             window_spec(WIN, D),
             window_spec(WIN, D),
-            pl.BlockSpec((PACKS, 144, D), lambda i: (0, 0, 0)),
+            whole_spec(PACKS, 144, D),
             pl.BlockSpec((8, D), lambda i: (0, 0)),
         ],
         out_shape=[
             jax.ShapeDtypeStruct((windows, WIN, D), F32),
             jax.ShapeDtypeStruct((windows, WIN, D), BF16),
-            jax.ShapeDtypeStruct((PACKS, 144, D), F32),
+            jax.ShapeDtypeStruct((PACKS, 144, D), dtype),
             jax.ShapeDtypeStruct((8, D), F32),
         ],
+        scratch_shapes=[pltpu.VMEM((PACKS, 144, D), F32)],
+        cost_estimate=cost(windows, 7),
         compiler_params=params(),
     )(grad, active, slope, middle, attended, pack, pack, pack, vec)
 
 
 def attention_backward(
     x_ref, gatt_ref, att_ref, rate_ref, soft_ref, qkv_ref, gmid_ref, in_ref, vec_ref,
-    out_ref, pack_ref, gvec_ref, table_ref,
-    sum_s, kt_s, qt_s, do_s, gk_s, gv_s, wide_s,
+    out_ref, result_ref, gvec_ref, table_ref,
+    pack_ref, sum_s, kt_s, qt_s, do_s, gk_s, gv_s, wide_s,
 ):
     step = pl.program_id(0)
 
@@ -382,6 +396,7 @@
 
     @pl.when(step == pl.num_programs(0) - 1)
     def _():
+        result_ref[...] = pack_ref[...].astype(result_ref.dtype)
         table_ref[...] = jnp.zeros_like(table_ref)
         for col in range(WW):
             wide_s[...] = jnp.zeros_like(wide_s)
@@ -398,7 +413,9 @@
                 ]
 
 
-def run_attention_backward(x, gattended, attended, rates, soft, qkv, gmiddle, pack, vec, dtype):
+def run_attention_backward(
+    x, gattended, attended, rates, soft, qkv, gmiddle, pack, vec, dtype, pack_dtype
+):
     windows = gmiddle.shape[0]
     return pl.pallas_call(
         attention_backward,
@@ -416,17 +433,18 @@
         ],
         out_specs=[
             grid_spec(x.shape),
-            pl.BlockSpec((PACKS, 48, D), lambda i: (0, 0, 0)),
+            whole_spec(PACKS, 48, D),
             pl.BlockSpec((4, D), lambda i: (0, 0)),
             pl.BlockSpec((HEADS * WT, CELLS * WT), lambda i: (0, 0)),
         ],
         out_shape=[
             jax.ShapeDtypeStruct(x.shape, dtype),
-            jax.ShapeDtypeStruct((PACKS, 48, D), F32),
+            jax.ShapeDtypeStruct((PACKS, 48, D), pack_dtype),
             jax.ShapeDtypeStruct((4, D), F32),
             jax.ShapeDtypeStruct((HEADS * WT, CELLS * WT), F32),
         ],
         scratch_shapes=[
+            pltpu.VMEM((PACKS, 48, D), F32),
             pltpu.VMEM((HEADS, WIN, WIN), F32),
             pltpu.VMEM((D, WIN), BF16),
             pltpu.VMEM((D, WIN), F32),
@@ -435,6 +453,7 @@
             pltpu.VMEM((WIN, D), BF16),
             pltpu.VMEM((HEADS * WT, (2 * WH - 1) * WW * WT), F32),
         ],
+        cost_estimate=cost(windows, 12),
         compiler_params=params(),
     )(x, gattended, attended, rates, soft, qkv, gmiddle, pack, vec)
 
@@ -444,12 +463,12 @@
         for shift in range(2 * WH - 1):
             low_lane = (shift * (2 * WW - 1) + WW - 1 - col) * WT
             wide_s[:, shift * WW * WT : (shift + 1) * WW * WT] = cells_ref[
-                0, :, low_lane : low_lane + WW * WT
+                :, low_lane : low_lane + WW * WT
             ]
         for row in range(WH):
             place = (row * WW + col) * WT
             low_lane = (WH - 1 - row) * WW * WT
-            out_ref[0, :, place : place + WT, :] = wide_s[:, low_lane : low_lane + WIN].reshape(
+            out_ref[:, place : place + WT, :] = wide_s[:, low_lane : low_lane + WIN].reshape(
                 HEADS, WT, WIN
             )
 
@@ -457,13 +476,168 @@
 def run_expand_bias(cells):
     return pl.pallas_call(
         expand_bias,
-        grid=(LAYERS,),
-        in_specs=[pl.BlockSpec((1, HEADS * WT, CELLS * WT), lambda i: (i, 0, 0))],
-        out_specs=pl.BlockSpec((1, HEADS, WIN, WIN), lambda i: (i, 0, 0, 0)),
-        out_shape=jax.ShapeDtypeStruct((LAYERS, HEADS, WIN, WIN), F32),
+        out_shape=jax.ShapeDtypeStruct((HEADS, WIN, WIN), F32),
         scratch_shapes=[pltpu.VMEM((HEADS * WT, (2 * WH - 1) * WW * WT), F32)],
-        compiler_params=params(),
+        compiler_params=pltpu.CompilerParams(vmem_limit_bytes=61 * 1024 * 1024),
     )(cells)
+
+
+AUX_ROWS = 8
+SHARES = ((0, 0, 96, 0), (0, 96, 48, 1), (1, 0, 48, 1), (2, 0, AUX_ROWS, 0))
+
+
+def fold_gradients(*refs):
+    operands = refs[:3]
+    big_out, small_out, aux_out = refs[3:6]
+    buffers = refs[6:18]
+    send_sem, recv_sem, wide_send, wide_recv = refs[18:]
+    batch = lax.axis_index("batch")
+    y = lax.axis_index("seq")
+    z, x, core = batch // 4, (batch // 2) % 2, batch % 2
+    count = len(SHARES)
+
+    def device(z_to, x_to, core_to, y_to):
+        return ((z_to * 2 + x_to) * 2 + core_to, y_to)
+
+    barrier = pltpu.get_barrier_semaphore()
+
+    def greet(k, carry):
+        other = lax.rem(batch * 2 + y + k, 32)
+        pl.semaphore_signal(
+            barrier, inc=1, device_id=(other // 2, other % 2), device_id_type=pl.DeviceIdType.MESH
+        )
+        return carry
+
+    lax.fori_loop(1, 32, greet, 0)
+    pl.semaphore_wait(barrier, 31)
+
+    def send(number, source, target, to):
+        copy = pltpu.make_async_remote_copy(
+            src_ref=source,
+            dst_ref=target,
+            send_sem=send_sem.at[number],
+            recv_sem=recv_sem.at[number],
+            device_id=to,
+            device_id_type=pl.DeviceIdType.MESH,
+        )
+        copy.start()
+        return copy
+
+    copies = []
+    for k, (which, first, size, order) in enumerate(SHARES):
+        source = operands[which].at[:, :, 1 - core, :, pl.ds(first, size), :]
+        copies.append(send(k, source, buffers[3 * k], device(z, x, 1 - core, y)))
+    for k, (which, first, size, order) in enumerate(SHARES):
+        copies[k].wait()
+        held = buffers[3 * k]
+
+        def add_core(i, carry, which=which, first=first, size=size, held=held):
+            a, b = i // 2, i % 2
+            mine = operands[which][a, b, core, :, first : first + size, :].astype(F32)
+            held[a, b] = (held[a, b].astype(F32) + mine).astype(held.dtype)
+            return carry
+
+        lax.fori_loop(0, 8, add_core, 0)
+        if order == 0:
+            copies.append(send(count + k, held.at[:, 1 - x], buffers[3 * k + 1], device(z, 1 - x, core, y)))
+        else:
+            copies.append(send(count + k, held.at[:, :, 1 - y], buffers[3 * k + 1], device(z, x, core, 1 - y)))
+    for k, (which, first, size, order) in enumerate(SHARES):
+        copies[count + k].wait()
+        before, held = buffers[3 * k], buffers[3 * k + 1]
+
+        def add_next(i, carry, order=order, before=before, held=held):
+            a, b = i // 2, i % 2
+            mine = before[a, x, b] if order == 0 else before[a, b, y]
+            held[a, b] = (held[a, b].astype(F32) + mine.astype(F32)).astype(held.dtype)
+            return carry
+
+        lax.fori_loop(0, 8, add_next, 0)
+        if order == 0:
+            copies.append(send(2 * count + k, held.at[:, 1 - y], buffers[3 * k + 2].at[pl.ds(0, 4)], device(z, x, core, 1 - y)))
+        else:
+            copies.append(send(2 * count + k, held.at[:, 1 - x], buffers[3 * k + 2].at[pl.ds(0, 4)], device(z, 1 - x, core, y)))
+    far = []
+    for k, (which, first, size, order) in enumerate(SHARES):
+        copies[2 * count + k].wait()
+        before, held = buffers[3 * k + 1], buffers[3 * k + 2]
+
+        def add_last(a, carry, order=order, before=before, held=held):
+            mine = before[a, y] if order == 0 else before[a, x]
+            held[a] = (held[a].astype(F32) + mine.astype(F32)).astype(held.dtype)
+            return carry
+
+        lax.fori_loop(0, 4, add_last, 0)
+        for step in range(1, 4):
+            other = lax.rem(z + step, 4)
+            far.append(
+                send(
+                    3 * count + 3 * k + step - 1,
+                    held.at[other],
+                    held.at[3 + step],
+                    device(other, x, core, y),
+                )
+            )
+    for k, (which, first, size, order) in enumerate(SHARES):
+        for step in range(1, 4):
+            far[3 * k + step - 1].wait()
+        held = buffers[3 * k + 2]
+        total = held[z].astype(F32) + held[4].astype(F32)
+        total = total + held[5].astype(F32) + held[6].astype(F32)
+        if which == 0:
+            big_out[first : first + size, :] = total
+        elif which == 1:
+            small_out[...] = total
+        else:
+            aux_out[batch * 2 + y] = total
+
+    def spread(k, carry):
+        other = lax.rem(batch * 2 + y + k, 32)
+        pltpu.make_async_remote_copy(
+            src_ref=aux_out.at[batch * 2 + y],
+            dst_ref=aux_out.at[batch * 2 + y],
+            send_sem=wide_send,
+            recv_sem=wide_recv,
+            device_id=(other // 2, other % 2),
+            device_id_type=pl.DeviceIdType.MESH,
+        ).start()
+        return carry
+
+    lax.fori_loop(1, 32, spread, 0)
+    others = aux_out.at[pl.ds(0, 31)]
+    pltpu.make_async_copy(others, others, wide_send).wait()
+    pltpu.make_async_copy(others, others, wide_recv).wait()
+
+
+def run_fold_gradients(big, small, aux):
+    operands = [value.reshape((4, 2, 2, 2) + value.shape[1:]) for value in (big, small, aux)]
+    scratch = []
+    for which, first, size, order in SHARES:
+        dtype = operands[which].dtype
+        scratch.append(pltpu.VMEM((4, 2, 2, size, D), dtype))
+        scratch.append(pltpu.VMEM((4, 2, size, D), dtype))
+        scratch.append(pltpu.VMEM((7, size, D), dtype))
+    semaphores = 6 * len(SHARES)
+    return pl.pallas_call(
+        fold_gradients,
+        in_specs=[pl.BlockSpec(memory_space=pltpu.VMEM)] * 3,
+        out_specs=[pl.BlockSpec(memory_space=pltpu.VMEM)] * 3,
+        out_shape=[
+            jax.ShapeDtypeStruct((144, D), F32),
+            jax.ShapeDtypeStruct((48, D), F32),
+            jax.ShapeDtypeStruct((32, AUX_ROWS, D), F32),
+        ],
+        scratch_shapes=scratch
+        + [
+            pltpu.SemaphoreType.DMA((semaphores,)),
+            pltpu.SemaphoreType.DMA((semaphores,)),
+            pltpu.SemaphoreType.DMA,
+            pltpu.SemaphoreType.DMA,
+        ],
+        compiler_params=pltpu.CompilerParams(
+            vmem_limit_bytes=61 * 1024 * 1024, collective_id=1, has_side_effects=True
+        ),
+    )(*operands)
 
 
 def offset_places():
@@ -477,29 +651,42 @@
     return (place(frame, row, col) * WIN + place(-frame, -row, -col)).reshape(-1)
 
 
-def select_rows(tables, chosen, dims):
-    flat = tables.transpose(1, 0, 2).reshape(BIAS_ROWS, LAYERS * HEADS)
-    pieces = dot(chosen, jnp.concatenate(split_three(flat), axis=1), dims)
-    width = LAYERS * HEADS
-    total = pieces[:, :width] + pieces[:, width : 2 * width] + pieces[:, 2 * width :]
-    return total.reshape(BIAS_ROWS, LAYERS, HEADS).transpose(1, 0, 2)
-
-
-def bias_cells(tables, chosen):
-    taken = select_rows(tables, chosen, (((1,), (0,)), ((), ())))
-    taken = taken.transpose(1, 0, 2).reshape(BIAS_ROWS, LAYERS * HEADS)
-    taken = (taken * LOG2E).reshape(2 * WT - 1, CELLS, LAYERS * HEADS).transpose(2, 1, 0)
-    placed = jnp.stack([taken[:, :, WT - 1 - t : 2 * WT - 1 - t] for t in range(WT)], axis=1)
-    return placed.reshape(LAYERS, HEADS * WT, CELLS * WT)
-
-
-def cells_to_rows(cells):
-    shaped = cells.reshape(LAYERS, HEADS, WT, CELLS, WT)
+def interleave():
+    cell = np.arange(CELLS * WT)
+    source = jnp.asarray((cell % WT) * CELLS + cell // WT, jnp.int32)
+    order = jnp.arange(CELLS * WT, dtype=jnp.int32)
+    return (order[:, None] == source[None, :]).astype(BF16)
+
+
+def join_three(values, axis):
+    first, second, third = jnp.split(values, 3, axis=axis)
+    return first + second + third
+
+
+def bias_cells(tables, chosen, order):
+    flat = jnp.concatenate([tables[layer] for layer in range(LAYERS)], axis=1) * LOG2E
+    pieces = jnp.concatenate(split_three(flat), axis=1)
+    taken = dot(pieces, chosen, (((0,), (1,)), ((), ()))).astype(BF16)
+    placed = jnp.stack(
+        [taken[:, (WT - 1 - t) * CELLS : (2 * WT - 1 - t) * CELLS] for t in range(WT)], axis=1
+    )
+    cells = dot(placed.reshape(-1, WT * CELLS), order)
+    return join_three(cells, 0).reshape(LAYERS, HEADS * WT, CELLS * WT)
+
+
+def cells_to_rows(cells, order):
+    pieces = jnp.concatenate(split_three(cells.reshape(-1, CELLS * WT)), axis=0)
+    placed = join_three(dot(pieces, order, NT), 0).reshape(LAYERS * HEADS, WT, CELLS * WT)
     parts = [
-        jnp.pad(shaped[:, :, t], ((0, 0), (0, 0), (0, 0), (WT - 1 - t, t))) for t in range(WT)
+        jnp.pad(placed[:, t], ((0, 0), ((WT - 1 - t) * CELLS, t * CELLS))) for t in range(WT)
     ]
-    total = functools.reduce(jnp.add, parts)
-    return total.transpose(0, 3, 2, 1).reshape(LAYERS, BIAS_ROWS, HEADS)
+    return functools.reduce(jnp.add, parts)
+
+
+def rows_to_table(rows, chosen):
+    pieces = jnp.concatenate(split_three(rows), axis=0)
+    total = join_three(dot(chosen, pieces, (((0,), (1,)), ((), ()))), 1)
+    return jnp.stack([total[:, i * HEADS : (i + 1) * HEADS] for i in range(LAYERS)])
 
 
 def spatial_blocks(field):
@@ -676,7 +863,9 @@
     taken_rows = jnp.take(offset_index.reshape(-1), offset_places())
     order = jnp.arange(BIAS_ROWS, dtype=jnp.int32)
     chosen = (taken_rows[:, None] == order[None, :]).astype(BF16)
-    bias = run_expand_bias(bias_cells(bias_table, chosen))
+    interleaved = interleave()
+    cells_in = bias_cells(bias_table, chosen, interleaved)
+    bias = [run_expand_bias(cells_in[layer]) for layer in range(LAYERS)]
     shape = place.grid_shape()
     aug = place.mask_lanes()
 
@@ -712,29 +901,42 @@
             value = jnp.concatenate(parts, axis=1)
         return lax.psum_scatter(value, AXES, scatter_dimension=0, tiled=False)
 
+    folded = lax.axis_size("batch") == 16 and lax.axis_size("seq") == 2
     for layer in reversed(range(LAYERS)):
         pack, vec = weights[layer]
         x, qkv, soft, rates, attended, middle, active, slope = saved[layer]
         gmiddle, gattended, big, gvec_two = run_feed_backward(
-            upstream, active, slope, middle, attended, pack, vec
+            upstream, active, slope, middle, attended, pack, vec, F32 if layer == 1 or not folded else BF16
         )
         upstream, small, gvec_one, cells = run_attention_backward(
             x, gattended, attended, rates, soft, qkv, gmiddle, pack, vec,
-            F32 if layer == 1 else BF16,
+            F32 if layer == 1 else BF16, F32 if layer == 1 or not folded else BF16,
         )
-        scattered[layer] = (
-            scatter(big, [ROWS] * 5 + [4 * ROWS]),
-            scatter(small, [ROWS] * 3),
-        )
+        if layer == 1 or not folded:
+            scattered[layer] = (
+                scatter(big, [ROWS] * 5 + [4 * ROWS]),
+                scatter(small, [ROWS] * 3),
+            )
         vec_parts[layer] = jnp.concatenate([gvec_one, gvec_two], axis=0)
         cell_parts[layer] = cells
         if layer == 1:
             upstream = place.back(upstream)
     clips_grad = place.leave(upstream, False)
 
-    table_rows = cells_to_rows(jnp.stack(cell_parts))
-    vec_total, table_total = lax.psum((jnp.stack(vec_parts), table_rows), AXES)
-    table_total = select_rows(table_total, chosen, TN)
+    table_rows = cells_to_rows(jnp.stack(cell_parts), interleaved)
+    vec_stack = jnp.stack(vec_parts)
+    if folded:
+        aux = jnp.concatenate([table_rows.reshape(-1), vec_stack.reshape(-1)])
+        used = aux.shape[0]
+        aux = jnp.pad(aux, (0, PACKS * AUX_ROWS * D - used)).reshape(PACKS, AUX_ROWS, D)
+        big_own, small_own, aux = run_fold_gradients(big, small, aux)
+        scattered[0] = (big_own, small_own)
+        aux = aux.reshape(-1)[:used]
+        table_total = aux[: table_rows.size].reshape(table_rows.shape)
+        vec_total = aux[table_rows.size :].reshape(vec_stack.shape)
+    else:
+        vec_total, table_total = lax.psum((vec_stack, table_rows), AXES)
+    table_total = rows_to_table(table_total, chosen)
 
     device = lax.axis_index(AXES)
 

time: 1500 us -> 996 us (0.66)
  waiting for transfers between devices: 708 us -> 225 us
  Pallas kernels: 535 us -> 614 us
  local copies, waits for them, and re-layouts: 137 us -> 68.9 us
  blocking collectives: 40.6 us -> 0 us
    reduce_scatter x4 -> x2, waiting for transfers between devices: 484 us -> 0.01 us  [scatter(): return lax.psum_scatter(value, AXES, scatter_dimension=0, tiled=False)]
    pallas_call x1 -> x3, Pallas kernels: 17.4 us -> 95.5 us  [the longest x1 72.4 us: run_fold_gradients(): pl.pallas_call(fold_gradients, in_specs=[pl.BlockSpec(memory_space=pltpu....]
    psum x1 -> x0, blocking collectives: 40.6 us -> none  [per_device(): vec_total, table_total = lax.psum((jnp.stack(vec_parts), table_rows), AXES)]
    psum x1 -> x0, waiting for transfers between devices: 36.2 us -> none  [per_device(): vec_total, table_total = lax.psum((jnp.stack(vec_parts), table_rows), AXES)]
    another operation x5 -> x4, local copies, waits for them, and re-layouts: 32.7 us -> 0.96 us  [the longest x1 0.9 us: run_fold_gradients(): value.reshape((4, 2, 2, 2) + value.shape[1:])]
    all_gather x2, waiting for transfers between devices: 0.01 us -> 31.4 us  [gathered(): full = lax.all_gather(local, AXES, axis=0)]
    reshape x4, local copies, waits for them, and re-layouts: 29.4 us -> 0.43 us  [the longest x1 0.22 us: per_device(): table_total = aux[:table_rows.size].reshape(table_rows.shape)]
    squeeze x1, local copies, waits for them, and re-layouts: 17 us -> 0.02 us  [bias_cells(): tables[layer]]
  transfers between devices with their start and end apart: 11 -> 8, of which waited for: 8 -> 3; matrix products, arithmetic and copies ran while one was open for 9% -> 11% of each run, Pallas kernels for 8% -> 36%
where the time goes in v2:
time: 996 us; the launch traced here: 985 us
  Pallas kernels  614 us (62%)
  waiting for transfers between devices  225 us (23%)
  local copies, waits for them, and re-layouts  68.9 us (7%)
  other arithmetic  40.5 us (4%)
  matrix products  17.7 us (2%)
  between operations  15.1 us (2%)
    pallas_call x2, Pallas kernels, run_attention_backward(): pl.pallas_call(attention_backward, grid=(windows,), in_specs=[grid_spec(x...  200 us
    ppermute x4, waiting for transfers between devices, swap_halves(): return lax.ppermute(part, 'seq', [(0, 1), (1, 0)])  193 us
    pallas_call x2, Pallas kernels, run_attention_forward(): pl.pallas_call(functools.partial(attention_forward, masked), grid=(window...  155 us
    pallas_call x2, Pallas kernels, run_feed_backward(): pl.pallas_call(feed_backward, grid=(windows,), in_specs=[grid_spec(grad.s...  106 us
    pallas_call x1, Pallas kernels, run_fold_gradients(): pl.pallas_call(fold_gradients, in_specs=[pl.BlockSpec(memory_space=pltpu....  72.4 us
    pallas_call x2, Pallas kernels, run_feed_forward(): pl.pallas_call(feed_forward, grid=(windows,), in_specs=[window_spec(WIN,...  57.3 us
    all_gather x2, waiting for transfers between devices, gathered(): full = lax.all_gather(local, AXES, axis=0)  31.4 us
    pallas_call x2, Pallas kernels, run_expand_bias(): pl.pallas_call(expand_bias, out_shape=jax.ShapeDtypeStruct((HEADS, WIN, W...  23.2 us
  transfers between devices with their start and end apart: 8, of which 3 were waited for; matrix products, arithmetic and copies ran while one was open for 11% of the time, Pallas kernels for 36%

profile of v2, /device:TPU:25, one launch (start us, length us, event | category | flops | bytes accessed | tf_op | source)
XLA Modules:
  0.0 984.6 jit_solution(17679388073073645896)
XLA Ops:
  15.1 13.6 %gather_fusion = s32[2535]{0:T(1024)S(1)} fusion(s32[153664]{0:T(1024)S(1)} %reshape.271, s32[3072]{0:T(1024)S(1)} %pad_clamp_fusion), kind=kCustom, calls=%fused_computation | custom fusion | bytes 30420 | tf_op jit(solution)/shard_map/jit(_take)/gather | solution.py:863
  28.8 5.0 fusion.12
  34.9 3.8 fusion.5
  40.1 11.6 %shard_map.352.refs_3_ = f32[16,392,392]{2,1,0:T(8,128)} custom-call(f32[128,1352]{1,0:T(8,128)} %get-tuple-element.104.cells_ref), custom_call_target="tpu_custom_call" | custom-call | tf_op jit(solution)/shard_map/pallas_call | solution.py:477
  51.7 31.4 %all-gather.5.cloned.1.call-done = bf16[6400,512]{1,0:T(8,128)(2,1)} async-done(((bf16[200,512]{1,0:T(8,128)(2,1)}), bf16[6400,512]{1,0:T(8,128)(2,1)}) %all-gather.5.cloned.1.call-update) | async-done | bytes 6553616 | tf_op jit(solution)/shard_map/all_gather | solution.py:845
  86.1 76.2 %shard_map.353 = (bf16[8,392,1536]{2,1,0:T(8,128)(2,1)}, bf16[8,16,392,392]{3,2,1,0:T(8,128)(2,1)}, f32[8,16,392]{2,1,0:T(8,128)}, bf16[8,392,512]{2,1,0:T(8,128)(2,1)}, f32[8,392,512]{2,1,0:T(8,128)}) custom-call(bf16[2,14,14,8,512]{4,3,2,1,0:T(8,128)(2,1)} %bitcast.212, bf16[32,200,512]{2,1,0:T(8,128)(2,1)} %bitcast.197, ...), custom_call_target="tpu_custom_call" | custom-call | flops 80000000000 | tf_op jit(solution)/shard_map/pallas_call | solution.py:163
  162.4 28.9 %shard_map.354 = (bf16[8,392,2048]{2,1,0:T(8,128)(2,1)}, bf16[8,392,2048]{2,1,0:T(8,128)(2,1)}, f32[2,14,14,8,512]{4,3,2,1,0:T(8,128)}) custom-call(f32[8,392,512]{2,1,0:T(8,128)} %get-tuple-element.50.mid_ref, bf16[32,200,512]{2,1,0:T(8,128)(2,1)} %bitcast.198, bf16[32,200,512]{2,1,0:T(8,128)(2,1)} %bitcast.199, f32[12,512]{1,0:T(8,128)} %concatenate.94.refs_2_.vec_ref), custom_call_target="tpu_custom_call" | custom-call | flops 32000000000 | tf_op jit(solution)/shard_map/pallas_call | solution.py:217
  191.2 9.4 fusion.52
  204.4 11.6 %shard_map.355.refs_3_ = f32[16,392,392]{2,1,0:T(8,128)} custom-call(f32[128,1352]{1,0:T(8,128)} %get-tuple-element.103.cells_ref), custom_call_target="tpu_custom_call" | custom-call | tf_op jit(solution)/shard_map/pallas_call | solution.py:477
  217.7 88.5 %collective-permute-done.2 = bf16[2,4,14,14,512]{4,1,3,2,0:T(4,128)(2,1)} collective-permute-done((bf16[2,4,14,14,512]{4,1,3,2,0:T(4,128)(2,1)}, bf16[2,4,14,14,512]{4,1,3,2,0:T(4,128)(2,1)}, u32[]{:S(2)}, u32[]{:S(2)}) %collective-permute-start.2) | collective-permute-done | bytes 1605664 | tf_op jit(solution)/shard_map/ppermute | solution.py:704
  323.9 3.9 fusion.7.refs_0_.x_ref
  327.8 79.3 %shard_map.356 = (bf16[8,392,1536]{2,1,0:T(8,128)(2,1)}, bf16[8,16,392,392]{3,2,1,0:T(8,128)(2,1)}, f32[8,16,392]{2,1,0:T(8,128)}, bf16[8,392,512]{2,1,0:T(8,128)(2,1)}, f32[8,392,512]{2,1,0:T(8,128)}) custom-call(f32[2,14,14,8,512]{4,3,2,1,0:T(8,128)} %fusion.7.refs_0_.x_ref, bf16[32,200,512]{2,1,0:T(8,128)(2,1)} %bitcast.205, ...), custom_call_target="tpu_custom_call" | custom-call | flops 80000000000 | tf_op jit(solution)/shard_map/pallas_call | solution.py:163
  407.1 28.4 %shard_map.357 = (bf16[8,392,2048]{2,1,0:T(8,128)(2,1)}, bf16[8,392,2048]{2,1,0:T(8,128)(2,1)}, bf16[2,14,14,8,512]{4,3,2,1,0:T(8,128)(2,1)}) custom-call(f32[8,392,512]{2,1,0:T(8,128)} %get-tuple-element.52.mid_ref, bf16[32,200,512]{2,1,0:T(8,128)(2,1)} %bitcast.206, bf16[32,200,512]{2,1,0:T(8,128)(2,1)} %bitcast.207, f32[12,512]{1,0:T(8,128)} %concatenate.101.refs_2_.vec_ref), custom_call_target="tpu_custom_call" | custom-call | flops 32000000000 | tf_op jit(solution)/shard_map/pallas_call | solution.py:217
  435.5 53.8 %shard_map.358 = (f32[8,392,512]{2,1,0:T(8,128)}, bf16[8,392,512]{2,1,0:T(8,128)(2,1)}, f32[32,144,512]{2,1,0:T(8,128)}, f32[8,512]{1,0:T(8,128)}) custom-call(bf16[2,14,14,8,512]{4,3,2,1,0:T(8,128)(2,1)} %fusion.14.grad_ref, bf16[8,392,2048]{2,1,0:T(8,128)(2,1)} %get-tuple-element.54.act_ref, bf16[8,392,2048]{2,1,0:T(8,128)(2,1)} %get-tuple-element.55.slope_ref, ...), custom_call_target="tpu_custom_call" | custom-call | flops 56000000000 | tf_op jit(solution)/shard_map/pallas_call | solution.py:285
  489.3 99.9 %shard_map.359 = (f32[2,14,14,8,512]{4,3,2,1,0:T(8,128)}, f32[32,48,512]{2,1,0:T(8,128)}, f32[4,512]{1,0:T(4,128)}, f32[128,1352]{1,0:T(8,128)}) custom-call(f32[2,14,14,8,512]{4,3,2,1,0:T(8,128)} %fusion.7.refs_0_.x_ref, bf16[8,392,512]{2,1,0:T(8,128)(2,1)} %get-tuple-element.57.gatt_ref, bf16[8,392,512]{2,1,0:T(8,128)(2,1)} %get-tuple-element.56.att_ref, ...), custom_call_target="tpu_custom_call" | custom-call | flops 96000000000 | tf_op jit(solution)/shard_map/pallas_call | solution.py:420
  595.2 3.4 fusion.51
  607.6 104.8 %collective-permute-done.1 = bf16[2,4,14,14,512]{4,1,3,2,0:T(4,128)(2,1)} collective-permute-done((bf16[2,4,14,14,512]{4,1,3,2,0:T(4,128)(2,1)}, bf16[2,4,14,14,512]{4,1,3,2,0:T(4,128)(2,1)}, u32[]{:S(2)}, u32[]{:S(2)}) %collective-permute-start.1) | collective-permute-done | bytes 1605664 | tf_op jit(solution)/shard_map/ppermute | solution.py:704
  712.4 5.3 pad_maximum_fusion.11
  717.7 6.2 pad_maximum_fusion.5.grad_ref
  723.8 52.5 %shard_map.360 = (f32[8,392,512]{2,1,0:T(8,128)}, bf16[8,392,512]{2,1,0:T(8,128)(2,1)}, bf16[32,144,512]{2,1,0:T(8,128)(2,1)}, f32[8,512]{1,0:T(8,128)}) custom-call(f32[2,14,14,8,512]{4,3,2,1,0:T(8,128)} %pad_maximum_fusion.5.grad_ref, bf16[8,392,2048]{2,1,0:T(8,128)(2,1)} %get-tuple-element.63.act_ref, bf16[8,392,2048]{2,1,0:T(8,128)(2,1)} %get-tuple-element.64.slope_ref, ...), custom_call_target="tpu_custom_call" | custom-call | flops 56000000000 | tf_op jit(solution)/shard_map/pallas_call | solution.py:285
  776.4 99.9 %shard_map.361 = (bf16[2,14,14,8,512]{4,3,2,1,0:T(8,128)(2,1)}, bf16[32,48,512]{2,1,0:T(8,128)(2,1)}, f32[4,512]{1,0:T(4,128)}, f32[128,1352]{1,0:T(8,128)}) custom-call(bf16[2,14,14,8,512]{4,3,2,1,0:T(8,128)(2,1)} %bitcast.213, bf16[8,392,512]{2,1,0:T(8,128)(2,1)} %get-tuple-element.66.gatt_ref, bf16[8,392,512]{2,1,0:T(8,128)(2,1)} %get-tuple-element.65.att_ref, ...), custom_call_target="tpu_custom_call" | custom-call | flops 96000000000 | tf_op jit(solution)/shard_map/pallas_call | solution.py:420
  878.9 3.7 fusion.4
  886.1 72.4 %shard_map.362 = (f32[144,512]{1,0:T(8,128)}, f32[48,512]{1,0:T(8,128)}, f32[32,8,512]{2,1,0:T(8,128)}) custom-call(bf16[4,2,2,2,144,512]{5,4,3,2,1,0:T(8,128)(2,1)} %bitcast.165, bf16[4,2,2,2,48,512]{5,4,3,2,1,0:T(8,128)(2,1)} %bitcast.168, f32[4,2,2,2,8,512]{5,4,3,2,1,0:T(8,128)} %reshape_reshape.3.refs_2_), custom_call_target="tpu_custom_call" | custom-call | tf_op jit(solution)/shard_map/pallas_call | solution.py:621
  966.2 5.2 fusion
  (208 shorter events, 70.8 us)
Async XLA Ops:
  7.2 7.9 copy-start.12
  7.2 7.9 copy-start.5
  7.2 75.9 %all-gather.5.cloned.1.call-start = ((), (), s32[]{:S(2)}) async-start(), calls=%async_computation.4 | async-start | bytes 6758400 | tf_op jit(solution)/shard_map/all_gather | solution.py:845
  12.4 302.7 %all-gather.7.cloned.1.call-start = ((), (), s32[]{:S(2)}) async-start(), calls=%async_computation.5 | async-start | bytes 6758400 | tf_op jit(solution)/shard_map/all_gather | solution.py:845
  13.2 959.1 %reduce-scatter.3.cloned.1.call-start = ((), (), s32[]{:S(2)}) async-start(), calls=%async_computation.2 | async-start | bytes 3244032 | tf_op jit(solution)/shard_map/reduce_scatter | solution.py:902
  191.2 10.6 %copy-start.3 = (bf16[2,8,14,14,512]{4,1,3,2,0:T(8,128)(2,1)S(1)}, bf16[2,8,14,14,512]{4,1,3,2,0:T(8,128)(2,1)}, u32[]{:S(2)}) copy-start(bf16[2,8,14,14,512]{4,1,3,2,0:T(8,128)(2,1)} %param.26) | copy-start | bytes 9633796
  200.6 117.4 %collective-permute-start = (f32[2,14,14,4,512]{4,3,2,1,0:T(4,128)}, f32[2,14,14,4,512]{4,3,2,1,0:T(4,128)}, u32[]{:S(2)}, u32[]{:S(2)}) collective-permute-start(f32[2,14,14,4,512]{4,3,2,1,0:T(4,128)} %get-tuple-element.87), channel_id=1, source_target_pairs={{0,1},{1,0},{2,3},{3,2},{4,5},{5,4},{6,7},{7,6},{8,9},{9,8},{10,11... | collective-permute-start | bytes 9633800 | tf_op jit(solution)/shard_map/ppermute | solution.py:704
  204.1 104.7 %copy-start.1 = (bf16[2,4,14,14,512]{4,1,3,2,0:T(4,128)(2,1)}, bf16[2,4,14,14,512]{4,1,3,2,0:T(4,128)(2,1)S(1)}, u32[]{:S(2)}) copy-start(bf16[2,4,14,14,512]{4,1,3,2,0:T(4,128)(2,1)S(1)} %get-tuple-element.90) | copy-start | bytes 4816900
  204.1 102.1 %collective-permute-start.2 = (bf16[2,4,14,14,512]{4,1,3,2,0:T(4,128)(2,1)}, bf16[2,4,14,14,512]{4,1,3,2,0:T(4,128)(2,1)}, u32[]{:S(2)}, u32[]{:S(2)}) collective-permute-start(bf16[2,4,14,14,512]{4,1,3,2,0:T(4,128)(2,1)} %get-tuple-element.89), channel_id=1, source_target_pairs={{0,1},{1,0},{2,3},{3,2},{4,5},{5,4},{6,7},{7,6},{8,9},{9,8},{10,11... | collective-permute-start | bytes 4816904 | tf_op jit(solution)/shard_map/ppermute | solution.py:704
  204.4 11.6 %copy-start.22 = (pred[392]{0:T(512)(128)(4,1)S(1)}, pred[392]{0:T(512)(128)(4,1)}, u32[]{:S(2)}) copy-start(pred[392]{0:T(512)(128)(4,1)} %constant.112.clone) | copy-start | bytes 1180
  204.4 11.7 %copy-start.16 = (s32[392]{0:T(512)S(1)}, s32[392]{0:T(512)}, u32[]{:S(2)}) copy-start(s32[392]{0:T(512)} %constant.160) | copy-start | bytes 4708
  204.4 11.7 %copy-start.17 = (s32[392]{0:T(512)S(1)}, s32[392]{0:T(512)}, u32[]{:S(2)}) copy-start(s32[392]{0:T(512)} %constant.159) | copy-start | bytes 4708
  204.4 11.8 %copy-start.18 = (s32[128]{0:T(128)S(1)}, s32[128]{0:T(128)}, u32[]{:S(2)}) copy-start(s32[128]{0:T(128)} %constant.115.clone) | copy-start | bytes 1540
  204.4 11.8 %copy-start.19 = (pred[128]{0:T(512)(128)(4,1)S(1)}, pred[128]{0:T(512)(128)(4,1)}, u32[]{:S(2)}) copy-start(pred[128]{0:T(512)(128)(4,1)} %constant.117.clone) | copy-start | bytes 388
  204.4 11.7 %copy-start.20 = (pred[128]{0:T(512)(128)(4,1)S(1)}, pred[128]{0:T(512)(128)(4,1)}, u32[]{:S(2)}) copy-start(pred[128]{0:T(512)(128)(4,1)} %constant.116.clone) | copy-start | bytes 388
  204.4 11.7 %copy-start.21 = (f32[128]{0:T(128)S(1)}, f32[128]{0:T(128)}, u32[]{:S(2)}) copy-start(f32[128]{0:T(128)} %constant.118.clone) | copy-start | bytes 1540
  589.3 384.5 %reduce-scatter.5.cloned.1.call-start = ((), (), s32[]{:S(2)}) async-start(), calls=%async_computation.3 | async-start | bytes 9732096 | tf_op jit(solution)/shard_map/reduce_scatter | solution.py:902
  598.6 119.1 %collective-permute-start.3 = (f32[2,14,14,4,512]{4,3,2,1,0:T(4,128)}, f32[2,14,14,4,512]{4,3,2,1,0:T(4,128)}, u32[]{:S(2)}, u32[]{:S(2)}) collective-permute-start(f32[2,14,14,4,512]{4,3,2,1,0:T(4,128)} %get-tuple-element.85), channel_id=1, source_target_pairs={{0,1},{1,0},{2,3},{3,2},{4,5},{5,4},{6,7},{7,6},{8,9},{9,8},{10,11... | collective-permute-start | bytes 9633800 | tf_op jit(solution)/shard_map/ppermute | solution.py:704
  606.0 106.4 %collective-permute-start.1 = (bf16[2,4,14,14,512]{4,1,3,2,0:T(4,128)(2,1)}, bf16[2,4,14,14,512]{4,1,3,2,0:T(4,128)(2,1)}, u32[]{:S(2)}, u32[]{:S(2)}) collective-permute-start(bf16[2,4,14,14,512]{4,1,3,2,0:T(4,128)(2,1)} %get-tuple-element.91), channel_id=1, source_target_pairs={{0,1},{1,0},{2,3},{3,2},{4,5},{5,4},{6,7},{7,6},{8,9},{9,8},{10,11... | collective-permute-start | bytes 4816904 | tf_op jit(solution)/shard_map/ppermute | solution.py:704
  776.4 99.9 %copy-start.11 = (f32[8,512]{1,0:T(8,128)S(1)}, f32[8,512]{1,0:T(8,128)}, u32[]{:S(2)}) copy-start(f32[8,512]{1,0:T(8,128)} %get-tuple-element.77) | copy-start | bytes 49156
  776.4 100.6 %copy-start.9 = (f32[1,12,512]{2,1,0:T(8,128)S(1)}, f32[1,12,512]{2,1,0:T(8,128)}, u32[]{:S(2)}) copy-start(f32[1,12,512]{2,1,0:T(8,128)} %maximum_bitcast_fusion.5) | copy-start | bytes 73732
  776.4 100.6 %copy-start.4 = (f32[128,1352]{1,0:T(8,128)S(1)}, f32[128,1352]{1,0:T(8,128)}, u32[]{:S(2)}) copy-start(f32[128,1352]{1,0:T(8,128)} %get-tuple-element.75) | copy-start | bytes 2076676
  958.5 7.6 copy-start.6
  958.6 7.7 copy-start.14
  (9 other events, 17.1 us)
Sparse Core Ops, SparseCore 0:
  12.5 70.5 all-gather.4
  86.6 69.2 all-gather.6
  589.4 107.9 reduce-scatter.2
  703.1 134.2 reduce-scatter.4

commit v3 on v2

--- a/solution.py
+++ b/solution.py
@@ -41,9 +41,12 @@
 TN = (((0,), (0,)), ((), ()))
 
 
-def params():
+def params(collective=None):
     return pltpu.CompilerParams(
-        vmem_limit_bytes=61 * 1024 * 1024, dimension_semantics=("arbitrary",)
+        vmem_limit_bytes=61 * 1024 * 1024,
+        dimension_semantics=("arbitrary",),
+        collective_id=collective,
+        has_side_effects=collective is not None,
     )
 
 
@@ -112,13 +115,116 @@
     return pl.ds(pl.multiple_of(base + group * 128, 128), 128)
 
 
-def attention_forward(masked, *refs):
+def neighbour():
+    return (lax.axis_index("batch"), 1 - lax.axis_index("seq"))
+
+
+def piece_places(forth, block):
+    if forth:
+        return ((0, 3, lax.rem(7 * block + 11, 14)), (3, 4, 7 * block))
+    return ((0, 4, 7 * block + 3), (4, 3, lax.rem(7 * block + 7, 14)))
+
+
+def window_copies(forth, step, slot, stage, out_ref, own_sem, send_sem, recv_sem):
+    clip, row_block, col_block = step // 4, (step // 2) % 2, step % 2
+    kept, kept_to, sent, sent_to = (4, 0, 0, 4) if forth else (0, 4, 4, 0)
+    copies = []
+    number = 0
+    for row, rows, row_to in piece_places(forth, row_block):
+        for col, cols, col_to in piece_places(forth, col_block):
+
+            def place(frame, row_to=row_to, rows=rows, col_to=col_to, cols=cols):
+                return out_ref.at[
+                    clip, pl.ds(row_to, rows), pl.ds(col_to, cols), pl.ds(frame, 4), :
+                ]
+
+            def held(frame, row=row, rows=rows, col=col, cols=cols):
+                return stage.at[
+                    slot, pl.ds(row, rows), pl.ds(col, cols), pl.ds(frame, 4), :
+                ]
+
+            copies.append(
+                pltpu.make_async_copy(held(kept), place(kept_to), own_sem.at[slot, number])
+            )
+            copies.append(
+                pltpu.make_async_remote_copy(
+                    src_ref=held(sent),
+                    dst_ref=place(sent_to),
+                    send_sem=send_sem.at[slot, number],
+                    recv_sem=recv_sem,
+                    device_id=neighbour(),
+                    device_id_type=pl.DeviceIdType.MESH,
+                )
+            )
+            number += 1
+    return copies
+
+
+def wait_left(copies):
+    for number, copy in enumerate(copies):
+        if number % 2 == 0:
+            copy.wait()
+        else:
+            copy.wait_send()
+
+
+def push_begin():
+    @pl.when(pl.program_id(0) == 0)
+    def _():
+        barrier = pltpu.get_barrier_semaphore()
+        pl.semaphore_signal(
+            barrier, inc=1, device_id=neighbour(), device_id_type=pl.DeviceIdType.MESH
+        )
+        pl.semaphore_wait(barrier, 1)
+
+
+def push_window(forth, value, out_ref, stage, own_sem, send_sem, recv_sem):
+    step = pl.program_id(0)
+    slot = lax.rem(step, 2)
+    rest = (stage, out_ref, own_sem, send_sem, recv_sem)
+
+    @pl.when(step >= 2)
+    def _():
+        wait_left(window_copies(forth, step - 2, slot, *rest))
+
+    stage[slot] = value.reshape(WH, WW, WT, D)
+    for copy in window_copies(forth, step, slot, *rest):
+        copy.start()
+
+    @pl.when(step == pl.num_programs(0) - 1)
+    def _():
+        wait_left(window_copies(forth, step - 1, 1 - slot, *rest))
+        wait_left(window_copies(forth, step, slot, *rest))
+        half = out_ref.at[:, :, :, pl.ds(4 if forth else 0, 4), :]
+        pltpu.make_async_copy(half, half, recv_sem).wait()
+
+
+def push_scratch():
+    return [
+        pltpu.VMEM((2, WH, WW, WT, D), F32),
+        pltpu.SemaphoreType.DMA((2, 4)),
+        pltpu.SemaphoreType.DMA((2, 4)),
+        pltpu.SemaphoreType.DMA,
+    ]
+
+
+def gelu_parts(hidden):
+    cumulative = 0.5 + 0.5 * lax.erf(hidden * (0.5**0.5))
+    density = jnp.exp(-0.5 * hidden * hidden) * 0.3989422804014327
+    return hidden * cumulative, cumulative + hidden * density
+
+
+def block_forward(masked, pushed, forth, *refs):
+    x_ref, w_ref, up_ref, down_ref, vec_ref, bias_ref = refs[:6]
+    refs = refs[6:]
     if masked:
-        x_ref, w_ref, vec_ref, bias_ref, augq_ref, augk_ref = refs[:6]
-        qkv_ref, soft_ref, rate_ref, att_ref, mid_ref, vt_s, ot_s = refs[6:]
-    else:
-        x_ref, w_ref, vec_ref, bias_ref = refs[:4]
-        qkv_ref, soft_ref, rate_ref, att_ref, mid_ref, vt_s, ot_s = refs[4:]
+        augq_ref, augk_ref = refs[:2]
+        refs = refs[2:]
+    qkv_ref, soft_ref, rate_ref, att_ref, mid_ref, act_ref, slope_ref, out_ref = refs[:8]
+    vt_s, ot_s = refs[8:10]
+    push = refs[10:]
+    if pushed:
+        push_begin()
     x = x_ref[0].astype(F32).reshape(WIN, D)
     normed = (normalize(x)[0] * vec_ref[0:1] + vec_ref[1:2]).astype(BF16)
     query = (dot(normed, square(w_ref, 0)) + vec_ref[2:3]) * (SCALE * LOG2E)
@@ -153,51 +259,9 @@
     lax.fori_loop(0, 4, group, 0)
     attended = jnp.transpose(ot_s[...]).astype(BF16)
     att_ref[0] = attended
-    mid_ref[0] = x + dot(attended, square(w_ref, 3 * ROWS)) + vec_ref[4:5]
-
-
-def run_attention_forward(x, pack, vec, bias, aug):
-    windows = x.shape[0] * (x.shape[1] // WH) * (x.shape[2] // WW)
-    masked = aug is not None
-    extra = list(aug) if masked else []
-    return pl.pallas_call(
-        functools.partial(attention_forward, masked),
-        grid=(windows,),
-        in_specs=[
-            grid_spec(x.shape),
-            pack_spec(64, 0),
-            whole_spec(12, D),
-            whole_spec(HEADS, WIN, WIN),
-        ]
-        + [window_spec(WIN, 128)] * len(extra),
-        out_specs=[
-            window_spec(WIN, 3 * D),
-            window_spec(HEADS, WIN, WIN),
-            window_spec(HEADS, WIN),
-            window_spec(WIN, D),
-            window_spec(WIN, D),
-        ],
-        out_shape=[
-            jax.ShapeDtypeStruct((windows, WIN, 3 * D), BF16),
-            jax.ShapeDtypeStruct((windows, HEADS, WIN, WIN), BF16),
-            jax.ShapeDtypeStruct((windows, HEADS, WIN), F32),
-            jax.ShapeDtypeStruct((windows, WIN, D), BF16),
-            jax.ShapeDtypeStruct((windows, WIN, D), F32),
-        ],
-        scratch_shapes=[pltpu.VMEM((D, WIN), BF16), pltpu.VMEM((D, WIN), F32)],
-        cost_estimate=cost(windows, 10),
-        compiler_params=params(),
-    )(x, pack, vec, bias, *extra)
-
-
-def gelu_parts(hidden):
-    cumulative = 0.5 + 0.5 * lax.erf(hidden * (0.5**0.5))
-    density = jnp.exp(-0.5 * hidden * hidden) * 0.3989422804014327
-    return hidden * cumulative, cumulative + hidden * density
-
-
-def feed_forward(mid_ref, up_ref, down_ref, vec_ref, act_ref, slope_ref, out_ref):
-    middle = mid_ref[0]
+    middle = x_ref[0].astype(F32).reshape(WIN, D)
+    middle = middle + dot(attended, square(w_ref, 3 * ROWS)) + vec_ref[4:5]
+    mid_ref[0] = middle
     normed = (normalize(middle)[0] * vec_ref[5:6] + vec_ref[6:7]).astype(BF16)
     total = middle + vec_ref[7:8]
     for part in range(4):
@@ -209,29 +273,53 @@
         slope_ref[0, :, lanes] = slope.astype(BF16)
         down = down_ref[part * 8 : part * 8 + 8].reshape(D, D)
         total = total + dot(active, down)
-    out_ref[0] = total.reshape(WH, WW, WT, D).astype(out_ref.dtype)
-
-
-def run_feed_forward(middle, pack, vec, grid_shape, dtype):
-    windows = middle.shape[0]
+    if pushed:
+        push_window(forth, total, out_ref, *push)
+    else:
+        out_ref[0] = total.reshape(WH, WW, WT, D).astype(out_ref.dtype)
+
+
+def run_block_forward(layer, x, pack, vec, bias, aug, dtype, pushed):
+    windows = x.shape[0] * (x.shape[1] // WH) * (x.shape[2] // WW)
+    masked = aug is not None
+    extra = list(aug) if masked else []
     return pl.pallas_call(
-        feed_forward,
+        functools.partial(block_forward, masked, pushed, layer == 0),
         grid=(windows,),
         in_specs=[
+            grid_spec(x.shape),
+            pack_spec(64, 3 * layer),
+            pack_spec(64, 3 * layer + 1),
+            pack_spec(64, 3 * layer + 2),
+            whole_spec(12, D),
+            whole_spec(HEADS, WIN, WIN),
+        ]
+        + [window_spec(WIN, 128)] * len(extra),
+        out_specs=[
+            window_spec(WIN, 3 * D),
+            window_spec(HEADS, WIN, WIN),
+            window_spec(HEADS, WIN),
             window_spec(WIN, D),
-            pack_spec(64, 1),
-            pack_spec(64, 2),
-            whole_spec(12, D),
+            window_spec(WIN, D),
+            window_spec(WIN, FF),
+            window_spec(WIN, FF),
+            pl.BlockSpec(memory_space=pl.ANY) if pushed else grid_spec(x.shape),
         ],
-        out_specs=[window_spec(WIN, FF), window_spec(WIN, FF), grid_spec(grid_shape)],
         out_shape=[
+            jax.ShapeDtypeStruct((windows, WIN, 3 * D), BF16),
+            jax.ShapeDtypeStruct((windows, HEADS, WIN, WIN), BF16),
+            jax.ShapeDtypeStruct((windows, HEADS, WIN), F32),
+            jax.ShapeDtypeStruct((windows, WIN, D), BF16),
+            jax.ShapeDtypeStruct((windows, WIN, D), F32),
             jax.ShapeDtypeStruct((windows, WIN, FF), BF16),
             jax.ShapeDtypeStruct((windows, WIN, FF), BF16),
-            jax.ShapeDtypeStruct(grid_shape, dtype),
+            jax.ShapeDtypeStruct(x.shape, dtype),
         ],
-        cost_estimate=cost(windows, 4),
-        compiler_params=params(),
-    )(middle, pack, pack, vec)
+        scratch_shapes=[pltpu.VMEM((D, WIN), BF16), pltpu.VMEM((D, WIN), F32)]
+        + (push_scratch() if pushed else []),
+        cost_estimate=cost(windows, 13),
+        compiler_params=params(2 + layer if pushed else None),
+    )(x, pack, pack, pack, vec, bias, *extra)
 
 
 def norm_back(normal, rate, gained):
@@ -280,7 +368,7 @@
         result_ref[...] = pack_ref[...].astype(result_ref.dtype)
 
 
-def run_feed_backward(grad, active, slope, middle, attended, pack, vec, dtype):
+def run_feed_backward(layer, grad, active, slope, middle, attended, pack, vec, dtype):
     windows = middle.shape[0]
     return pl.pallas_call(
         feed_backward,
@@ -291,9 +379,9 @@
             window_spec(WIN, FF),
             window_spec(WIN, D),
             window_spec(WIN, D),
-            pack_spec(64, 0),
-            pack_spec(64, 1),
-            pack_spec(64, 2),
+            pack_spec(64, 3 * layer),
+            pack_spec(64, 3 * layer + 1),
+            pack_spec(64, 3 * layer + 2),
             whole_spec(12, D),
         ],
         out_specs=[
@@ -305,7 +393,7 @@
         out_shape=[
             jax.ShapeDtypeStruct((windows, WIN, D), F32),
             jax.ShapeDtypeStruct((windows, WIN, D), BF16),
-            jax.ShapeDtypeStruct((PACKS, 144, D), dtype),
+            jax.ShapeDtypeStruct((PACKS, 192, D), dtype),
             jax.ShapeDtypeStruct((8, D), F32),
         ],
         scratch_shapes=[pltpu.VMEM((PACKS, 144, D), F32)],
@@ -315,11 +403,14 @@
 
 
 def attention_backward(
-    x_ref, gatt_ref, att_ref, rate_ref, soft_ref, qkv_ref, gmid_ref, in_ref, vec_ref,
+    pushed,
+    whole_ref, x_ref, gatt_ref, att_ref, rate_ref, soft_ref, qkv_ref, gmid_ref, in_ref, vec_ref,
     out_ref, result_ref, gvec_ref, table_ref,
-    pack_ref, sum_s, kt_s, qt_s, do_s, gk_s, gv_s, wide_s,
+    pack_ref, sum_s, kt_s, qt_s, do_s, gk_s, gv_s, wide_s, *push,
 ):
     step = pl.program_id(0)
+    if pushed:
+        push_begin()
 
     @pl.when(step == 0)
     def _():
@@ -392,7 +483,10 @@
     gvec_ref[0:1] += row_sum(gnormed * normal)
     gvec_ref[1:2] += row_sum(gnormed)
     grad = gmid_ref[0] + norm_back(normal, rate, gnormed * vec_ref[0:1])
-    out_ref[0] = grad.reshape(WH, WW, WT, D).astype(out_ref.dtype)
+    if pushed:
+        push_window(False, grad, out_ref, *push)
+    else:
+        out_ref[0] = grad.reshape(WH, WW, WT, D).astype(out_ref.dtype)
 
     @pl.when(step == pl.num_programs(0) - 1)
     def _():
@@ -414,13 +508,14 @@
 
 
 def run_attention_backward(
-    x, gattended, attended, rates, soft, qkv, gmiddle, pack, vec, dtype, pack_dtype
+    layer, whole, x, gattended, attended, rates, soft, qkv, gmiddle, pack, vec, dtype, pack_dtype, pushed
 ):
     windows = gmiddle.shape[0]
     return pl.pallas_call(
-        attention_backward,
+        functools.partial(attention_backward, pushed),
         grid=(windows,),
         in_specs=[
+            pl.BlockSpec(memory_space=pl.ANY),
             grid_spec(x.shape),
             window_spec(WIN, D),
             window_spec(WIN, D),
@@ -428,18 +523,18 @@
             window_spec(HEADS, WIN, WIN),
             window_spec(WIN, 3 * D),
             window_spec(WIN, D),
-            pack_spec(64, 0),
+            pack_spec(64, 3 * layer),
             whole_spec(12, D),
         ],
         out_specs=[
-            grid_spec(x.shape),
-            whole_spec(PACKS, 48, D),
+            pl.BlockSpec(memory_space=pl.ANY) if pushed else grid_spec(x.shape),
+            pack_spec(48, 3),
             pl.BlockSpec((4, D), lambda i: (0, 0)),
             pl.BlockSpec((HEADS * WT, CELLS * WT), lambda i: (0, 0)),
         ],
         out_shape=[
             jax.ShapeDtypeStruct(x.shape, dtype),
-            jax.ShapeDtypeStruct((PACKS, 48, D), pack_dtype),
+            jax.ShapeDtypeStruct((PACKS, 192, D), pack_dtype),
             jax.ShapeDtypeStruct((4, D), F32),
             jax.ShapeDtypeStruct((HEADS * WT, CELLS * WT), F32),
         ],
@@ -452,10 +547,12 @@
             pltpu.VMEM((WIN, D), BF16),
             pltpu.VMEM((WIN, D), BF16),
             pltpu.VMEM((HEADS * WT, (2 * WH - 1) * WW * WT), F32),
-        ],
+        ]
+        + (push_scratch() if pushed else []),
         cost_estimate=cost(windows, 12),
-        compiler_params=params(),
-    )(x, gattended, attended, rates, soft, qkv, gmiddle, pack, vec)
+        compiler_params=params(4 if pushed else None),
+        input_output_aliases={0: 1},
+    )(whole, x, gattended, attended, rates, soft, qkv, gmiddle, pack, vec)
 
 
 def expand_bias(cells_ref, out_ref, wide_s):
@@ -483,14 +580,14 @@
 
 
 AUX_ROWS = 8
-SHARES = ((0, 0, 96, 0), (0, 96, 48, 1), (1, 0, 48, 1), (2, 0, AUX_ROWS, 0))
+SHARES = ((0, 0, 96, 0), (0, 96, 96, 1), (1, 0, AUX_ROWS, 0))
 
 
 def fold_gradients(*refs):
-    operands = refs[:3]
-    big_out, small_out, aux_out = refs[3:6]
-    buffers = refs[6:18]
-    send_sem, recv_sem, wide_send, wide_recv = refs[18:]
+    operands = refs[:2]
+    pack_out, aux_out = refs[2:4]
+    buffers = refs[4:13]
+    send_sem, recv_sem, wide_send, wide_recv = refs[13:]
     batch = lax.axis_index("batch")
     y = lax.axis_index("seq")
     z, x, core = batch // 4, (batch // 2) % 2, batch % 2
@@ -585,9 +682,7 @@
         total = held[z].astype(F32) + held[4].astype(F32)
         total = total + held[5].astype(F32) + held[6].astype(F32)
         if which == 0:
-            big_out[first : first + size, :] = total
-        elif which == 1:
-            small_out[...] = total
+            pack_out[first : first + size, :] = total
         else:
             aux_out[batch * 2 + y] = total
 
@@ -609,8 +704,8 @@
     pltpu.make_async_copy(others, others, wide_recv).wait()
 
 
-def run_fold_gradients(big, small, aux):
-    operands = [value.reshape((4, 2, 2, 2) + value.shape[1:]) for value in (big, small, aux)]
+def run_fold_gradients(big, aux):
+    operands = [value.reshape((4, 2, 2, 2) + value.shape[1:]) for value in (big, aux)]
     scratch = []
     for which, first, size, order in SHARES:
         dtype = operands[which].dtype
@@ -620,11 +715,10 @@
     semaphores = 6 * len(SHARES)
     return pl.pallas_call(
         fold_gradients,
-        in_specs=[pl.BlockSpec(memory_space=pltpu.VMEM)] * 3,
-        out_specs=[pl.BlockSpec(memory_space=pltpu.VMEM)] * 3,
+        in_specs=[pl.BlockSpec(memory_space=pltpu.VMEM)] * 2,
+        out_specs=[pl.BlockSpec(memory_space=pltpu.VMEM)] * 2,
         out_shape=[
-            jax.ShapeDtypeStruct((144, D), F32),
-            jax.ShapeDtypeStruct((48, D), F32),
+            jax.ShapeDtypeStruct((192, D), F32),
             jax.ShapeDtypeStruct((32, AUX_ROWS, D), F32),
         ],
         scratch_shapes=scratch
@@ -752,17 +846,9 @@
         return roll_space(field, SHIFT_S, 2) if shifted else field
 
     def forth(self, grid):
-        if self.near:
-            arrived = swap_halves(grid[..., :SHIFT_T, :])
-            grid = jnp.concatenate([grid[..., SHIFT_T:, :], arrived], axis=3)
-            return roll_space(grid, -SHIFT_S, 1)
         return self.enter(self.leave(grid, False), True)
 
     def back(self, grid):
-        if self.near:
-            grid = roll_space(grid, SHIFT_S, 1)
-            arrived = swap_halves(grid[..., SHIFT_T:, :])
-            return jnp.concatenate([arrived, grid[..., :SHIFT_T, :]], axis=3)
         return self.enter(self.leave(grid, True), False)
 
     def mask_lanes(self):
@@ -834,32 +920,32 @@
     ]
     vec_pack = jnp.concatenate(vectors, axis=1)
     width = vec_pack.shape[1]
-    vec_rows = jnp.pad(vec_pack, ((0, 0), (0, D - width)))[:, None]
-    vec_rows = jnp.pad(vec_rows, ((0, 0), (0, 7), (0, 0)))
-
-    def gathered(layer):
-        local = pack_layer(
-            inner_weight[layer], outer_weight[layer], up_weight[layer], down_weight[layer]
-        )
-        local = jnp.concatenate([local, vec_rows[layer]], axis=0)
-        full = lax.all_gather(local, AXES, axis=0)
-        held = full[:, 12 * rows, :width].astype(F32)
+    vec_rows = jnp.pad(vec_pack, ((0, 14), (0, D - width)))
+    local = [
+        pack_layer(inner_weight[layer], outer_weight[layer], up_weight[layer], down_weight[layer])
+        for layer in range(LAYERS)
+    ]
+    full = lax.all_gather(jnp.concatenate(local + [vec_rows], axis=0), AXES, axis=0)
+    vecs = []
+    for layer in range(LAYERS):
+        held = full[:, 24 * rows + layer, :width].astype(F32)
         pieces = []
         start = 0
         for vector in vectors:
             size = vector.shape[1]
             pieces.append(held[:, start : start + size].reshape(-1, D))
             start += size
-        vec = jnp.concatenate(pieces, axis=0)
-        if rows != ROWS:
-            parts = [
-                full[:, i * rows : (i + 1) * rows].reshape(PACKS, ROWS, D) for i in range(8)
-            ]
-            parts.append(full[:, 8 * rows : 12 * rows].reshape(PACKS, 4 * ROWS, D))
-            full = jnp.concatenate(parts, axis=1)
-        return full, vec
-
-    weights = [gathered(layer) for layer in range(LAYERS)]
+        vecs.append(jnp.concatenate(pieces, axis=0))
+    if rows != ROWS:
+        parts = []
+        for first in (0, 12 * rows):
+            for i in range(8):
+                part = full[:, first + i * rows : first + (i + 1) * rows]
+                parts.append(part.reshape(PACKS, ROWS, D))
+            part = full[:, first + 8 * rows : first + 12 * rows]
+            parts.append(part.reshape(PACKS, 4 * ROWS, D))
+        full = jnp.concatenate(parts, axis=1)
+    weights = [(full, vec) for vec in vecs]
     taken_rows = jnp.take(offset_index.reshape(-1), offset_places())
     order = jnp.arange(BIAS_ROWS, dtype=jnp.int32)
     chosen = (taken_rows[:, None] == order[None, :]).astype(BF16)
@@ -875,15 +961,13 @@
     x = x_zero
     for layer in range(LAYERS):
         pack, vec = weights[layer]
-        qkv, soft, rates, attended, middle = run_attention_forward(
-            x, pack, vec, bias[layer], aug if layer == 1 else None
-        )
-        active, slope, result = run_feed_forward(
-            middle, pack, vec, shape, F32 if layer == 0 else BF16
+        qkv, soft, rates, attended, middle, active, slope, result = run_block_forward(
+            layer, x, pack, vec, bias[layer], aug if layer == 1 else None,
+            F32 if layer == 0 or place.near else BF16, place.near,
         )
         saved.append((x, qkv, soft, rates, attended, middle, active, slope))
-        x = place.forth(result) if layer == 0 else result
-    clips_out = place.leave(x, True)
+        x = place.forth(result) if layer == 0 and not place.near else result
+    clips_out = place.leave(x, not place.near).astype(BF16)
 
     scattered = [None] * LAYERS
     vec_parts = [None] * LAYERS
@@ -906,20 +990,18 @@
         pack, vec = weights[layer]
         x, qkv, soft, rates, attended, middle, active, slope = saved[layer]
         gmiddle, gattended, big, gvec_two = run_feed_backward(
-            upstream, active, slope, middle, attended, pack, vec, F32 if layer == 1 or not folded else BF16
+            layer, upstream, active, slope, middle, attended, pack, vec, F32 if layer == 1 or not folded else BF16
         )
-        upstream, small, gvec_one, cells = run_attention_backward(
-            x, gattended, attended, rates, soft, qkv, gmiddle, pack, vec,
+        upstream, big, gvec_one, cells = run_attention_backward(
+            layer, big, x, gattended, attended, rates, soft, qkv, gmiddle, pack, vec,
             F32 if layer == 1 else BF16, F32 if layer == 1 or not folded else BF16,
+            place.near and layer == 1,
         )
         if layer == 1 or not folded:
-            scattered[layer] = (
-                scatter(big, [ROWS] * 5 + [4 * ROWS]),
-                scatter(small, [ROWS] * 3),
-            )
+            scattered[layer] = scatter(big, [ROWS] * 5 + [4 * ROWS] + [ROWS] * 3)
         vec_parts[layer] = jnp.concatenate([gvec_one, gvec_two], axis=0)
         cell_parts[layer] = cells
-        if layer == 1:
+        if layer == 1 and not place.near:
             upstream = place.back(upstream)
     clips_grad = place.leave(upstream, False)
 
@@ -929,8 +1011,7 @@
         aux = jnp.concatenate([table_rows.reshape(-1), vec_stack.reshape(-1)])
         used = aux.shape[0]
         aux = jnp.pad(aux, (0, PACKS * AUX_ROWS * D - used)).reshape(PACKS, AUX_ROWS, D)
-        big_own, small_own, aux = run_fold_gradients(big, small, aux)
-        scattered[0] = (big_own, small_own)
+        scattered[0], aux = run_fold_gradients(big, aux)
         aux = aux.reshape(-1)[:used]
         table_total = aux[: table_rows.size].reshape(table_rows.shape)
         vec_total = aux[table_rows.size :].reshape(vec_stack.shape)
@@ -945,29 +1026,29 @@
         size = count * D // devices
         return lax.dynamic_slice_in_dim(whole, device * size, size, axis=1)
 
-    def both(which, first, count):
+    def both(first, count):
         parts = []
         for layer in range(LAYERS):
-            value = scattered[layer][which]
+            value = scattered[layer]
             columns = [
                 value[first + i * rows : first + (i + 1) * rows] for i in range(count)
             ]
             parts.append(jnp.concatenate(columns, axis=1))
         return jnp.stack(parts)
 
-    down = jnp.stack([scattered[layer][0][5 * rows : 9 * rows] for layer in range(LAYERS)])
+    down = jnp.stack([scattered[layer][5 * rows : 9 * rows] for layer in range(LAYERS)])
     return (
         clips_out,
         clips_grad,
         own(0, 1),
         own(1, 1),
-        both(1, 0, 3),
+        both(9 * rows, 3),
         own(2, 2),
-        both(0, 0, 1),
+        both(0, 1),
         own(4, 1),
         own(5, 1),
         own(6, 1),
-        both(0, rows, 4),
+        both(rows, 4),
         own(8, 4),
         down,
         own(7, 1),

time: 996 us -> 786 us (0.79)
  waiting for transfers between devices: 225 us -> 37.3 us
  Pallas kernels: 614 us -> 644 us
  local copies, waits for them, and re-layouts: 68.9 us -> 45.7 us
  other arithmetic: 40.5 us -> 19.6 us
    ppermute x4 -> x1, waiting for transfers between devices: 193 us -> 0.01 us  [swap_halves(): return lax.ppermute(part, 'seq', [(0, 1), (1, 0)])]
    pallas_call x6 -> x4, Pallas kernels: 413 us -> 439 us  [the longest x2 230 us: run_block_forward(): pl.pallas_call(functools.partial(block_forward, masked, pushed, layer ==...]
    slice x11 -> x7, local copies, waits for them, and re-layouts: 16.7 us -> 1.23 us  [the longest x1 0.91 us: per_device(): scattered[layer][5 * rows:9 * rows]]
    concatenate x3 -> x0, other arithmetic: 14.3 us -> none  [the longest x1 6.17 us: back(): return jnp.concatenate([arrived, grid[..., :SHIFT_T, :]], axis=3)]
    all_gather x2 -> x1, waiting for transfers between devices: 31.4 us -> 37.3 us  [per_device(): lax.all_gather(jnp.concatenate(local + [vec_rows], axis=0), AXES, axis=0)]
  transfers between devices with their start and end apart: 8 -> 3, of which waited for: 3 -> 1; matrix products, arithmetic and copies ran while one was open for 11% -> 8% of each run, Pallas kernels for 36% -> 32%
where the time goes in v3:
time: 786 us; the launch traced here: 781 us
  Pallas kernels  644 us (82%)
  local copies, waits for them, and re-layouts  45.7 us (6%)
  waiting for transfers between devices  37.3 us (5%)
  other arithmetic  19.6 us (2%)
  matrix products  17.7 us (2%)
  between operations  15.1 us (2%)
    pallas_call x2, Pallas kernels, run_block_forward(): pl.pallas_call(functools.partial(block_forward, masked, pushed, layer ==...  230 us
    pallas_call x2, Pallas kernels, run_attention_backward(): pl.pallas_call(functools.partial(attention_backward, pushed), grid=(windo...  209 us
    pallas_call x2, Pallas kernels, run_feed_backward(): pl.pallas_call(feed_backward, grid=(windows,), in_specs=[grid_spec(grad.s...  106 us
    pallas_call x1, Pallas kernels, run_fold_gradients(): pl.pallas_call(fold_gradients, in_specs=[pl.BlockSpec(memory_space=pltpu....  75.6 us
    all_gather x1, waiting for transfers between devices, per_device(): lax.all_gather(jnp.concatenate(local + [vec_rows], axis=0), AXES, axis=0)  37.3 us
    pallas_call x2, Pallas kernels, run_expand_bias(): pl.pallas_call(expand_bias, out_shape=jax.ShapeDtypeStruct((HEADS, WIN, W...  22.8 us
    dot_general x4, matrix products, dot(): return lax.dot_general(left, right, dims, preferred_element_type=F32)  17.7 us
  transfers between devices with their start and end apart: 3, of which 1 were waited for; matrix products, arithmetic and copies ran while one was open for 8% of the time, Pallas kernels for 32%

profile of v3, /device:TPU:25, one launch (start us, length us, event | category | flops | bytes accessed | tf_op | source)
XLA Modules:
  0.0 780.9 jit_solution(15597438983825885880)
XLA Ops:
  13.9 5.4 fusion.46
  19.3 1.2 collective-permute-start
  21.3 14.1 %gather_fusion = s32[2535]{0:T(1024)S(1)} fusion(s32[153664]{0:T(1024)S(1)} %reshape.268, s32[3072]{0:T(1024)S(1)} %pad_clamp_fusion), kind=kCustom, calls=%fused_computation | custom fusion | bytes 30420 | tf_op jit(solution)/shard_map/jit(_take)/gather | solution.py:949
  35.6 5.0 fusion.8
  41.7 3.8 fusion.5
  46.9 11.5 %shard_map.352.refs_5_ = f32[16,392,392]{2,1,0:T(8,128)} custom-call(f32[128,1352]{1,0:T(8,128)} %get-tuple-element.98.cells_ref), custom_call_target="tpu_custom_call" | custom-call | tf_op jit(solution)/shard_map/pallas_call | solution.py:574
  58.5 11.3 %shard_map.354.refs_5_ = f32[16,392,392]{2,1,0:T(8,128)} custom-call(f32[128,1352]{1,0:T(8,128)} %get-tuple-element.97.cells_ref), custom_call_target="tpu_custom_call" | custom-call | tf_op jit(solution)/shard_map/pallas_call | solution.py:574
  69.9 1.5 select_convert_fusion
  71.5 2.5 fusion.12
  74.0 1.9 fusion.11
  76.1 2.9 fusion.10.grad_ref
  79.0 37.3 %all-gather.3.cloned.1.call-done = bf16[12800,512]{1,0:T(8,128)(2,1)} async-done(((bf16[400,512]{1,0:T(8,128)(2,1)}), bf16[12800,512]{1,0:T(8,128)(2,1)}) %all-gather.3.cloned.1.call-update) | async-done | bytes 13107216 | tf_op jit(solution)/shard_map/all_gather | solution.py:928
  118.9 1.3 concatenate.58.refs_4_.vec_ref
  120.2 114.4 %shard_map.353 = (bf16[8,392,1536]{2,1,0:T(8,128)(2,1)}, bf16[8,16,392,392]{3,2,1,0:T(8,128)(2,1)}, f32[8,16,392]{2,1,0:T(8,128)}, bf16[8,392,512]{2,1,0:T(8,128...) custom-call(bf16[2,14,14,8,512]{4,3,2,1,0:T(8,128)(2,1)} %bitcast.19, ...), custom_call_target="tpu_custom_call" | custom-call | flops 103999995904 | tf_op jit(solution)/shard_map/pallas_call | solution.py:286
  234.6 1.3 concatenate.61.refs_4_.vec_ref
  235.8 116.1 %shard_map.355 = (bf16[8,392,1536]{2,1,0:T(8,128)(2,1)}, bf16[8,16,392,392]{3,2,1,0:T(8,128)(2,1)}, f32[8,16,392]{2,1,0:T(8,128)}, bf16[8,392,512]{2,1,0:T(8,128...) custom-call(f32[2,14,14,8,512]{4,3,2,1,0:T(8,128)} %get-tuple-elemen, ...), custom_call_target="tpu_custom_call" | custom-call | flops 103999995904 | tf_op jit(solution)/shard_map/pallas_call | solution.py:286
  351.9 54.0 %shard_map.356 = (f32[8,392,512]{2,1,0:T(8,128)}, bf16[8,392,512]{2,1,0:T(8,128)(2,1)}, f32[32,192,512]{2,1,0:T(8,128)}, f32[8,512]{1,0:T(8,128)}) custom-call(bf16[2,14,14,8,512]{4,3,2,1,0:T(8,128)(2,1)} %fusion.10.grad_ref, bf16[8,392,2048]{2,1,0:T(8,128)(2,1)} %get-tuple-element.51.act_ref, bf16[8,392,2048]{2,1,0:T(8,128)(2,1)} %get-tuple-element.52.slope_ref, ...), custom_call_target="tpu_custom_call" | custom-call | flops 56000000000 | tf_op jit(solution)/shard_map/pallas_call | solution.py:373
  405.9 109.5 %shard_map.357 = (f32[2,14,14,8,512]{4,3,2,1,0:T(8,128)}, f32[32,192,512]{2,1,0:T(8,128)}, f32[4,512]{1,0:T(4,128)}, f32[128,1352]{1,0:T(8,128)}) custom-call(f32[32,192,512]{2,1,0:T(8,128)} %get-tuple-element.55.whole_ref, f32[2,14,14,8,512]{4,3,2,1,0:T(8,128)} %get-tuple-element.49.refs_0_.x_ref, ...), custom_call_target="tpu_custom_call", output_to_operand_aliasing={{1}: (0, {})} | custom-call | flops 96000000000 | tf_op jit(solution)/shard_map/pallas_call | solution.py:514
  516.7 52.5 %shard_map.358 = (f32[8,392,512]{2,1,0:T(8,128)}, bf16[8,392,512]{2,1,0:T(8,128)(2,1)}, bf16[32,192,512]{2,1,0:T(8,128)(2,1)}, f32[8,512]{1,0:T(8,128)}) custom-call(f32[2,14,14,8,512]{4,3,2,1,0:T(8,128)} %get-tuple-element.61.grad_ref, bf16[8,392,2048]{2,1,0:T(8,128)(2,1)} %get-tuple-element.62.act_ref, bf16[8,392,2048]{2,1,0:T(8,128)(2,1)} %get-tuple-element.63.slope_ref, ...), custom_call_target="tpu_custom_call" | custom-call | flops 56000000000 | tf_op jit(solution)/shard_map/pallas_call | solution.py:373
  569.2 99.4 %shard_map.359 = (bf16[2,14,14,8,512]{4,3,2,1,0:T(8,128)(2,1)}, bf16[32,192,512]{2,1,0:T(8,128)(2,1)}, f32[4,512]{1,0:T(4,128)}, f32[128,1352]{1,0:T(8,128)}) custom-call(bf16[32,192,512]{2,1,0:T(8,128)(2,1)} %get-tuple-element.66.whole_ref, bf16[2,14,14,8,512]{4,3,2,1,0:T(8,128)(2,1)} %bitcast.196, ...), custom_call_target="tpu_custom_call", output_to_operand_aliasing={{1}: (0, {})} | custom-call | flops 96000000000 | tf_op jit(solution)/shard_map/pallas_call | solution.py:514
  671.3 3.7 fusion.4
  678.5 75.6 %shard_map.360 = (f32[192,512]{1,0:T(8,128)}, f32[32,8,512]{2,1,0:T(8,128)}) custom-call(bf16[4,2,2,2,192,512]{5,4,3,2,1,0:T(8,128)(2,1)} %bitcast.157, f32[4,2,2,2,8,512]{5,4,3,2,1,0:T(8,128)} %reshape_reshape.3.refs_1_), custom_call_target="tpu_custom_call" | custom-call | tf_op jit(solution)/shard_map/pallas_call | solution.py:716
  761.0 5.2 fusion
  767.1 2.2 convert_bitcast_fusion
  (173 shorter events, 32.4 us)
Async XLA Ops:
  7.2 109.0 %all-gather.3.cloned.1.call-start = ((), (), s32[]{:S(2)}) async-start(), calls=%async_computation.2 | async-start | bytes 13516800 | tf_op jit(solution)/shard_map/all_gather | solution.py:928
  13.0 0.8 copy-start.2
  13.8 6.7 copy-start
  13.9 7.4 copy-start.8
  13.9 755.4 %reduce-scatter.2.cloned.1.call-start = ((), (), s32[]{:S(2)}) async-start(), calls=%async_computation.1 | async-start | bytes 12976128 | tf_op jit(solution)/shard_map/reduce_scatter | solution.py:986
  19.3 52.2 %collective-permute-start = (bf16[2,4,14,14,512]{4,1,3,2,0:T(4,128)(2,1)}, bf16[2,4,14,14,512]{4,1,3,2,0:T(4,128)(2,1)}, u32[]{:S(2)}, u32[]{:S(2)}) collective-permute-start(bf16[2,4,14,14,512]{4,1,3,2,0:T(4,128)(2,1)} %get-tuple-element.85), channel_id=1, source_target_pairs={{0,1},{1,0},{2,3},{3,2},{4,5},{5,4},{6,7},{7,6},{8,9},{9,8},{10,11... | collective-permute-start | bytes 4816904 | tf_op jit(solution)/shard_map/ppermute | solution.py:798
  21.3 14.2 %copy-start.4 = (f32[2,2535,16]{1,2,0:T(8,128)S(1)}, f32[2,2535,16]{1,2,0:T(8,128)}, u32[]{:S(2)}) copy-start(f32[2,2535,16]{1,2,0:T(8,128)} %param.40) | copy-start | bytes 973444
  35.5 5.1 copy-start.9
  40.5 1.1 copy-start.19
  58.4 11.4 %copy-start.18 = (pred[392]{0:T(512)(128)(4,1)S(1)}, pred[392]{0:T(512)(128)(4,1)}, u32[]{:S(2)}) copy-start(pred[392]{0:T(512)(128)(4,1)} %constant.112.clone) | copy-start | bytes 1180
  58.4 11.4 %copy-start.12 = (s32[392]{0:T(512)S(1)}, s32[392]{0:T(512)}, u32[]{:S(2)}) copy-start(s32[392]{0:T(512)} %constant.158) | copy-start | bytes 4708
  58.4 11.4 %copy-start.13 = (s32[392]{0:T(512)S(1)}, s32[392]{0:T(512)}, u32[]{:S(2)}) copy-start(s32[392]{0:T(512)} %constant.157) | copy-start | bytes 4708
  58.4 11.5 %copy-start.14 = (s32[128]{0:T(128)S(1)}, s32[128]{0:T(128)}, u32[]{:S(2)}) copy-start(s32[128]{0:T(128)} %constant.115.clone) | copy-start | bytes 1540
  58.4 11.5 %copy-start.15 = (pred[128]{0:T(512)(128)(4,1)S(1)}, pred[128]{0:T(512)(128)(4,1)}, u32[]{:S(2)}) copy-start(pred[128]{0:T(512)(128)(4,1)} %constant.117.clone) | copy-start | bytes 388
  58.5 11.5 %copy-start.16 = (pred[128]{0:T(512)(128)(4,1)S(1)}, pred[128]{0:T(512)(128)(4,1)}, u32[]{:S(2)}) copy-start(pred[128]{0:T(512)(128)(4,1)} %constant.116.clone) | copy-start | bytes 388
  58.5 11.5 %copy-start.17 = (f32[128]{0:T(128)S(1)}, f32[128]{0:T(128)}, u32[]{:S(2)}) copy-start(f32[128]{0:T(128)} %constant.118.clone) | copy-start | bytes 1540
  515.4 0.7 copy-start.6
  569.2 99.4 %copy-start.7 = (f32[8,512]{1,0:T(8,128)S(1)}, f32[8,512]{1,0:T(8,128)}, u32[]{:S(2)}) copy-start(f32[8,512]{1,0:T(8,128)} %get-tuple-element.77) | copy-start | bytes 49156
  569.2 100.1 %copy-start.5 = (f32[1,12,512]{2,1,0:T(8,128)S(1)}, f32[1,12,512]{2,1,0:T(8,128)}, u32[]{:S(2)}) copy-start(f32[1,12,512]{2,1,0:T(8,128)} %maximum_bitcast_fusion.5) | copy-start | bytes 73732
  569.2 100.2 %copy-start.1 = (f32[128,1352]{1,0:T(8,128)S(1)}, f32[128,1352]{1,0:T(8,128)}, u32[]{:S(2)}) copy-start(f32[128,1352]{1,0:T(8,128)} %get-tuple-element.75) | copy-start | bytes 2076676
  754.1 6.8 copy-start.3
  754.1 6.9 copy-start.10
  761.0 6.1 slice-start
  761.0 6.1 slice-start.1
  (2 other events, 1.4 us)
Sparse Core Ops, SparseCore 0:
  14.0 102.2 all-gather.2
  515.6 154.6 reduce-scatter.1

commit v4 on v3

--- a/solution.py
+++ b/solution.py
@@ -210,8 +210,8 @@
 
 def gelu_parts(hidden):
     cumulative = 0.5 + 0.5 * lax.erf(hidden * (0.5**0.5))
-    density = jnp.exp(-0.5 * hidden * hidden) * 0.3989422804014327
-    return hidden * cumulative, cumulative + hidden * density
+    decay = jnp.exp2(hidden * hidden * (-0.5 * LOG2E))
+    return hidden * cumulative, cumulative + hidden * decay * 0.3989422804014327
 
 
 def block_forward(masked, pushed, forth, *refs):
@@ -221,8 +221,7 @@
         augq_ref, augk_ref = refs[:2]
         refs = refs[2:]
     qkv_ref, soft_ref, rate_ref, att_ref, mid_ref, act_ref, slope_ref, out_ref = refs[:8]
-    vt_s, ot_s = refs[8:10]
-    push = refs[10:]
+    push = refs[8:]
     if pushed:
         push_begin()
     x = x_ref[0].astype(F32).reshape(WIN, D)
@@ -232,47 +231,73 @@
     qkv_ref[0, :, D : 2 * D] = dot(normed, square(w_ref, ROWS)).astype(BF16)
     values = dot(normed, square(w_ref, 2 * ROWS)) + vec_ref[3:4]
     qkv_ref[0, :, 2 * D :] = values.astype(BF16)
-    vt_s[...] = jnp.transpose(values).astype(BF16)
-
-    def group(g, carry):
-        query4 = qkv_ref[0, :, lane_slice(g)]
-        keys4 = qkv_ref[0, :, lane_slice(g, D)]
+
+    def score(head):
+        first = head // 4 * 128
+        query4 = qkv_ref[0, :, first : first + 128]
+        keys4 = qkv_ref[0, :, D + first : D + first + 128]
+        query4 = jnp.where(head_lanes(head % 4), query4, jnp.zeros_like(query4))
         if masked:
             query4 = jnp.concatenate([query4, augq_ref[0]], axis=1)
-        for which in range(4):
-            head = g * 4 + which
-            keys = jnp.where(head_lanes(which), keys4, jnp.zeros_like(keys4))
-            if masked:
-                keys = jnp.concatenate([keys, augk_ref[0]], axis=1)
-            total = dot(keys, query4, NT) + bias_ref[head]
-            peak = jnp.max(total, axis=0, keepdims=True)
-            soft = jnp.exp2(total - peak).astype(BF16)
-            soft_ref[0, head] = soft
-            rows = pl.ds(pl.multiple_of(head * HD, HD), HD)
-            left = jnp.concatenate([vt_s[rows, :], jnp.ones((16, WIN), BF16)], axis=0)
-            joined = dot(left, soft)
-            rate = 1.0 / joined[HD : HD + 1]
-            rate_ref[0, pl.ds(head, 1), :] = rate
-            ot_s[rows, :] = joined[:HD] * rate
-        return carry
-
-    lax.fori_loop(0, 4, group, 0)
-    attended = jnp.transpose(ot_s[...]).astype(BF16)
-    att_ref[0] = attended
+            keys4 = jnp.concatenate([keys4, augk_ref[0]], axis=1)
+        return dot(query4, keys4, NT)
+
+    parts = [None, None]
+
+    def finish(head, soft):
+        first = head // 4 * 128
+        mine = head_lanes(head % 4)
+        values4 = qkv_ref[0, :, 2 * D + first : 2 * D + first + 128]
+        values4 = jnp.where(mine, values4, jnp.zeros_like(values4))
+        right = jnp.concatenate([values4, jnp.ones((WIN, 128), BF16)], axis=1)
+        joined = dot(soft, right)
+        rate = 1.0 / joined[:, 128:]
+        part = joined[:, :128] * rate
+        parts[0] = part if head % 4 == 0 else parts[0] + part
+        parts[1] = rate if head % 4 == 0 else jnp.where(mine, rate, parts[1])
+        if head % 4 == 3:
+            att_ref[0, :, first : first + 128] = parts[0].astype(BF16)
+            rate_ref[0, :, first : first + 128] = parts[1]
+
+    total = score(0)
+    last = None
+    for head in range(HEADS):
+        following = score(head + 1) if head < HEADS - 1 else None
+        total = total + bias_ref[head]
+        soft = jnp.exp2(total - jnp.max(total, axis=1, keepdims=True)).astype(BF16)
+        soft_ref[0, head] = soft
+        if head > 0:
+            finish(head - 1, last)
+        last = soft
+        total = following
+    finish(HEADS - 1, last)
+    attended = att_ref[0]
     middle = x_ref[0].astype(F32).reshape(WIN, D)
     middle = middle + dot(attended, square(w_ref, 3 * ROWS)) + vec_ref[4:5]
     mid_ref[0] = middle
     normed = (normalize(middle)[0] * vec_ref[5:6] + vec_ref[6:7]).astype(BF16)
     total = middle + vec_ref[7:8]
+
+    def raise_part(part):
+        return dot(normed, square(up_ref, part * ROWS)) + vec_ref[8 + part : 9 + part]
+
+    def lower_part(part, active):
+        return dot(active, down_ref[part * 8 : part * 8 + 8].reshape(D, D))
+
+    hidden = raise_part(0)
+    last = None
     for part in range(4):
+        following = raise_part(part + 1) if part < 3 else None
         lanes = slice(part * D, (part + 1) * D)
-        hidden = dot(normed, square(up_ref, part * ROWS)) + vec_ref[8 + part : 9 + part]
         active, slope = gelu_parts(hidden)
         active = active.astype(BF16)
         act_ref[0, :, lanes] = active
         slope_ref[0, :, lanes] = slope.astype(BF16)
-        down = down_ref[part * 8 : part * 8 + 8].reshape(D, D)
-        total = total + dot(active, down)
+        if part > 0:
+            total = total + lower_part(part - 1, last)
+        last = active
+        hidden = following
+    total = total + lower_part(3, last)
     if pushed:
         push_window(forth, total, out_ref, *push)
     else:
@@ -298,7 +323,7 @@
         out_specs=[
             window_spec(WIN, 3 * D),
             window_spec(HEADS, WIN, WIN),
-            window_spec(HEADS, WIN),
+            window_spec(WIN, D),
             window_spec(WIN, D),
             window_spec(WIN, D),
             window_spec(WIN, FF),
@@ -308,15 +333,14 @@
         out_shape=[
             jax.ShapeDtypeStruct((windows, WIN, 3 * D), BF16),
             jax.ShapeDtypeStruct((windows, HEADS, WIN, WIN), BF16),
-            jax.ShapeDtypeStruct((windows, HEADS, WIN), F32),
+            jax.ShapeDtypeStruct((windows, WIN, D), F32),
             jax.ShapeDtypeStruct((windows, WIN, D), BF16),
             jax.ShapeDtypeStruct((windows, WIN, D), F32),
             jax.ShapeDtypeStruct((windows, WIN, FF), BF16),
             jax.ShapeDtypeStruct((windows, WIN, FF), BF16),
             jax.ShapeDtypeStruct(x.shape, dtype),
         ],
-        scratch_shapes=[pltpu.VMEM((D, WIN), BF16), pltpu.VMEM((D, WIN), F32)]
-        + (push_scratch() if pushed else []),
+        scratch_shapes=push_scratch() if pushed else [],
         cost_estimate=cost(windows, 13),
         compiler_params=params(2 + layer if pushed else None),
     )(x, pack, pack, pack, vec, bias, *extra)
@@ -337,31 +361,57 @@
         pack_ref[...] = jnp.zeros_like(pack_ref)
         gvec_ref[...] = jnp.zeros_like(gvec_ref)
 
-    grad = grad_ref[0].astype(F32).reshape(WIN, D)
-    gvec_ref[3:4] += row_sum(grad)
-    grad_low = grad.astype(BF16)
-    normal, rate = normalize(mid_ref[0])
-    normed = (normal * vec_ref[5:6] + vec_ref[6:7]).astype(BF16)
-    gnormed = jnp.zeros((WIN, D), F32)
+    count = mid_ref.shape[0]
+    each = range(count)
+    grads = [
+        grad_ref[0, :, WW * w : WW * (w + 1)].astype(F32).reshape(WIN, D) for w in each
+    ]
+    gvec_ref[3:4] += sum(row_sum(grad) for grad in grads)
+    lows = [grad.astype(BF16) for grad in grads]
+    normals = [normalize(mid_ref[w]) for w in each]
+    normed = [(normals[w][0] * vec_ref[5:6] + vec_ref[6:7]).astype(BF16) for w in each]
+    gnormed = [jnp.zeros((WIN, D), F32) for w in each]
+
+    def back_part(part):
+        down = down_ref[part * 8 : part * 8 + 8].reshape(D, D)
+        return [dot(lows[w], down, NT) for w in each]
+
+    def finish(part, ghidden):
+        first = ROWS * (1 + part)
+        total = sum(dot(normed[w], ghidden[w], TN) for w in each)
+        pack_ref[:, first : first + ROWS, :] += total.reshape(PACKS, ROWS, D)
+        up = square(up_ref, part * ROWS)
+        for w in each:
+            gnormed[w] = gnormed[w] + dot(ghidden[w], up, NT)
+
+    gactive = back_part(0)
+    last = None
     for part in range(4):
+        following = back_part(part + 1) if part < 3 else None
         lanes = slice(part * D, (part + 1) * D)
-        active = act_ref[0, :, lanes]
-        pack_ref[part * 8 : part * 8 + 8, 80:144, :] += dot(active, grad_low, TN).reshape(8, 64, D)
-        down = down_ref[part * 8 : part * 8 + 8].reshape(D, D)
-        ghidden = dot(grad_low, down, NT) * slope_ref[0, :, lanes].astype(F32)
-        gvec_ref[4 + part : 5 + part] += row_sum(ghidden)
-        ghidden = ghidden.astype(BF16)
-        first = ROWS * (1 + part)
-        pack_ref[:, first : first + ROWS, :] += dot(normed, ghidden, TN).reshape(PACKS, ROWS, D)
-        gnormed = gnormed + dot(ghidden, square(up_ref, part * ROWS), NT)
-    gvec_ref[1:2] += row_sum(gnormed * normal)
-    gvec_ref[2:3] += row_sum(gnormed)
-    gmid = grad + norm_back(normal, rate, gnormed * vec_ref[5:6])
-    gmid_ref[0] = gmid
-    gvec_ref[0:1] += row_sum(gmid)
-    gmid_low = gmid.astype(BF16)
-    pack_ref[:, 0:ROWS, :] += dot(att_ref[0], gmid_low, TN).reshape(PACKS, ROWS, D)
-    gatt_ref[0] = dot(gmid_low, square(in_ref, 3 * ROWS), NT).astype(BF16)
+        ghidden = [gactive[w] * slope_ref[w, :, lanes].astype(F32) for w in each]
+        gvec_ref[4 + part : 5 + part] += sum(row_sum(value) for value in ghidden)
+        ghidden = [value.astype(BF16) for value in ghidden]
+        total = sum(dot(act_ref[w, :, lanes], lows[w], TN) for w in each)
+        pack_ref[part * 8 : part * 8 + 8, 80:144, :] += total.reshape(8, 64, D)
+        if part > 0:
+            finish(part - 1, last)
+        last = ghidden
+        gactive = following
+    finish(3, last)
+    outer = square(in_ref, 3 * ROWS)
+    total = jnp.zeros((D, D), F32)
+    for w in each:
+        normal, rate = normals[w]
+        gvec_ref[1:2] += row_sum(gnormed[w] * normal)
+        gvec_ref[2:3] += row_sum(gnormed[w])
+        gmid = grads[w] + norm_back(normal, rate, gnormed[w] * vec_ref[5:6])
+        gmid_ref[w] = gmid
+        gvec_ref[0:1] += row_sum(gmid)
+        gmid_low = gmid.astype(BF16)
+        total = total + dot(att_ref[w], gmid_low, TN)
+        gatt_ref[w] = dot(gmid_low, outer, NT).astype(BF16)
+    pack_ref[:, 0:ROWS, :] += total.reshape(PACKS, ROWS, D)
 
     @pl.when(pl.program_id(0) == pl.num_programs(0) - 1)
     def _():
@@ -370,23 +420,32 @@
 
 def run_feed_backward(layer, grad, active, slope, middle, attended, pack, vec, dtype):
     windows = middle.shape[0]
+    count = grad.shape[2] // WW
+    row_blocks = grad.shape[1] // WH
+
+    def some(width):
+        return pl.BlockSpec((count, WIN, width), lambda i: (i, 0, 0))
+
+    grid_block = pl.BlockSpec(
+        (1, WH, count * WW, WT, D), lambda i: (i // row_blocks, i % row_blocks, 0, 0, 0)
+    )
     return pl.pallas_call(
         feed_backward,
-        grid=(windows,),
+        grid=(windows // count,),
         in_specs=[
-            grid_spec(grad.shape),
-            window_spec(WIN, FF),
-            window_spec(WIN, FF),
-            window_spec(WIN, D),
-            window_spec(WIN, D),
+            grid_block,
+            some(FF),
+            some(FF),
+            some(D),
+            some(D),
             pack_spec(64, 3 * layer),
             pack_spec(64, 3 * layer + 1),
             pack_spec(64, 3 * layer + 2),
             whole_spec(12, D),
         ],
         out_specs=[
-            window_spec(WIN, D),
-            window_spec(WIN, D),
+            some(D),
+            some(D),
             whole_spec(PACKS, 144, D),
             pl.BlockSpec((8, D), lambda i: (0, 0)),
         ],
@@ -406,7 +465,7 @@
     pushed,
     whole_ref, x_ref, gatt_ref, att_ref, rate_ref, soft_ref, qkv_ref, gmid_ref, in_ref, vec_ref,
     out_ref, result_ref, gvec_ref, table_ref,
-    pack_ref, sum_s, kt_s, qt_s, do_s, gk_s, gv_s, wide_s, *push,
+    pack_ref, sum_s, qt_s, dot_s, gkt_s, gvt_s, gq_s, do_s, wide_s, *push,
 ):
     step = pl.program_id(0)
     if pushed:
@@ -419,11 +478,7 @@
         gvec_ref[...] = jnp.zeros_like(gvec_ref)
 
     lane = lax.broadcasted_iota(jnp.int32, (1, 128), 1)
-    head_row = lax.broadcasted_iota(jnp.int32, (3 * HEADS, D), 0) % HEADS
-    head_col = lax.broadcasted_iota(jnp.int32, (3 * HEADS, D), 1) // HD
-    spread = jnp.where(head_row == head_col, 1.0, 0.0).astype(BF16)
-    rates = jnp.concatenate(split_three(rate_ref[0]), axis=0)
-    scaled = (gatt_ref[0].astype(F32) * dot(rates, spread, TN)).astype(BF16)
+    scaled = (gatt_ref[0].astype(F32) * rate_ref[0]).astype(BF16)
     do_s[...] = scaled
     product = scaled.astype(F32) * att_ref[0].astype(F32)
     gather_row = lax.broadcasted_iota(jnp.int32, (D, 128), 0) // HD
@@ -436,38 +491,48 @@
     inner = dot(high, gather) + dot(low, gather)
     first, second, third = split_three(inner)
     inner = jnp.where(lane < HEADS, first, jnp.where(lane < 2 * HEADS, second, third))
-    kt_s[...] = jnp.transpose(qkv_ref[0, :, D : 2 * D].astype(F32)).astype(BF16)
-
-    def group(g, carry):
-        query4 = qkv_ref[0, :, lane_slice(g)]
-        values4 = qkv_ref[0, :, lane_slice(g, 2 * D)]
-        grad4 = do_s[:, lane_slice(g)]
-        right = jnp.concatenate([grad4, inner], axis=1)
-        zero = jnp.zeros_like(grad4)
-        gvalues = jnp.zeros((WIN, 128), F32)
-        gkeys = jnp.zeros((WIN, 128), F32)
-        for which in range(4):
-            head = g * 4 + which
-            mine = head_lanes(which)
-            minus = jnp.where((lane % HEADS == head) & (lane < 3 * HEADS), -1.0, 0.0)
-            minus = jnp.broadcast_to(minus, (WIN, 128)).astype(BF16)
-            left = jnp.concatenate([jnp.where(mine, values4, zero), minus], axis=1)
-            soft = soft_ref[0, head]
-            gtotal = soft.astype(F32) * dot(left, right, NT)
-            sum_s[head] += gtotal
-            gtotal = gtotal.astype(BF16)
-            gvalues = gvalues + dot(soft, jnp.where(mine, grad4, zero))
-            gkeys = gkeys + dot(gtotal, jnp.where(mine, query4, zero))
-            rows = pl.ds(pl.multiple_of(head * HD, HD), HD)
-            qt_s[rows, :] = dot(kt_s[rows, :], gtotal)
-        gv_s[:, lane_slice(g)] = gvalues.astype(BF16)
-        gk_s[:, lane_slice(g)] = (gkeys * LN2).astype(BF16)
-        return carry
-
-    lax.fori_loop(0, 4, group, 0)
-    gquery = jnp.transpose(qt_s[...]).astype(BF16)
-    gkeys = gk_s[...]
-    gvalues = gv_s[...]
+    qt_s[...] = jnp.transpose(qkv_ref[0, :, 0:D].astype(F32)).astype(BF16)
+    dot_s[...] = jnp.transpose(scaled.astype(F32)).astype(BF16)
+    minus = jnp.broadcast_to(jnp.where(lane < 3 * HEADS, -1.0, 0.0), (WIN, 128)).astype(BF16)
+    zero = jnp.zeros((WIN, 128), BF16)
+
+    def score(head):
+        first = head // 4 * 128
+        grad4 = jnp.where(head_lanes(head % 4), do_s[:, first : first + 128], zero)
+        own = jnp.where((lane % HEADS == head) & (lane < 3 * HEADS), inner, zero)
+        left = jnp.concatenate([grad4, own], axis=1)
+        values4 = qkv_ref[0, :, 2 * D + first : 2 * D + first + 128]
+        return dot(left, jnp.concatenate([values4, minus], axis=1), NT)
+
+    parts = [None]
+
+    def finish(head, soft, gtotal):
+        first = head // 4 * 128
+        rows = slice(head * HD, (head + 1) * HD)
+        gvt_s[rows, :] = dot(dot_s[rows, :], soft)
+        gkt_s[rows, :] = dot(qt_s[rows, :], gtotal)
+        keys4 = qkv_ref[0, :, D + first : D + first + 128]
+        part = dot(gtotal, jnp.where(head_lanes(head % 4), keys4, zero))
+        parts[0] = part if head % 4 == 0 else parts[0] + part
+        if head % 4 == 3:
+            gq_s[:, first : first + 128] = parts[0].astype(BF16)
+
+    slope = score(0)
+    last = None
+    for head in range(HEADS):
+        following = score(head + 1) if head < HEADS - 1 else None
+        soft = soft_ref[0, head]
+        gtotal = soft.astype(F32) * slope
+        sum_s[head] += gtotal
+        gtotal = gtotal.astype(BF16)
+        if head > 0:
+            finish(head - 1, *last)
+        last = (soft, gtotal)
+        slope = following
+    finish(HEADS - 1, *last)
+    gquery = gq_s[...]
+    gkeys = (jnp.transpose(gkt_s[...]) * LN2).astype(BF16)
+    gvalues = jnp.transpose(gvt_s[...]).astype(BF16)
     normal, rate = normalize(x_ref[0].astype(F32).reshape(WIN, D))
     normed = (normal * vec_ref[0:1] + vec_ref[1:2]).astype(BF16)
     pack_ref[:, 0:ROWS, :] += (dot(normed, gquery, TN) * SCALE).reshape(PACKS, ROWS, D)
@@ -519,7 +584,7 @@
             grid_spec(x.shape),
             window_spec(WIN, D),
             window_spec(WIN, D),
-            window_spec(HEADS, WIN),
+            window_spec(WIN, D),
             window_spec(HEADS, WIN, WIN),
             window_spec(WIN, 3 * D),
             window_spec(WIN, D),
@@ -542,8 +607,9 @@
             pltpu.VMEM((PACKS, 48, D), F32),
             pltpu.VMEM((HEADS, WIN, WIN), F32),
             pltpu.VMEM((D, WIN), BF16),
+            pltpu.VMEM((D, WIN), BF16),
             pltpu.VMEM((D, WIN), F32),
-            pltpu.VMEM((WIN, D), BF16),
+            pltpu.VMEM((D, WIN), F32),
             pltpu.VMEM((WIN, D), BF16),
             pltpu.VMEM((WIN, D), BF16),
             pltpu.VMEM((HEADS * WT, (2 * WH - 1) * WW * WT), F32),
@@ -580,14 +646,14 @@
 
 
 AUX_ROWS = 8
-SHARES = ((0, 0, 96, 0), (0, 96, 96, 1), (1, 0, AUX_ROWS, 0))
+SHARES = ((1, 0, AUX_ROWS, 0), (0, 0, 48, 0), (0, 48, 48, 1), (0, 96, 48, 0), (0, 144, 48, 1))
 
 
 def fold_gradients(*refs):
     operands = refs[:2]
     pack_out, aux_out = refs[2:4]
-    buffers = refs[4:13]
-    send_sem, recv_sem, wide_send, wide_recv = refs[13:]
+    buffers = refs[4:19]
+    send_sem, recv_sem, wide_send, wide_recv = refs[19:]
     batch = lax.axis_index("batch")
     y = lax.axis_index("seq")
     z, x, core = batch // 4, (batch // 2) % 2, batch % 2
@@ -742,7 +808,7 @@
     def place(f, r, c):
         return (np.maximum(f, 0) * WH + np.maximum(r, 0)) * WW + np.maximum(c, 0)
 
-    return (place(frame, row, col) * WIN + place(-frame, -row, -col)).reshape(-1)
+    return (place(frame, row, col) * WIN + place(-frame, -row, -col)).reshape(-1)[::-1].copy()
 
 
 def interleave():

time: 786 us -> 693 us (0.88)
  Pallas kernels: 644 us -> 553 us
    pallas_call x2, Pallas kernels: 230 us -> 182 us  [run_block_forward(): pl.pallas_call(functools.partial(block_forward, masked, pushed, layer ==...]
    pallas_call x2, Pallas kernels: 209 us -> 180 us  [run_attention_backward(): pl.pallas_call(functools.partial(attention_backward, pushed), grid=(windo...]
    pallas_call x2, Pallas kernels: 106 us -> 98 us  [run_feed_backward(): pl.pallas_call(feed_backward, grid=(windows // count,), in_specs=[grid_bl...]
  transfers between devices with their start and end apart: 3 -> 3, of which waited for: 1 -> 1; matrix products, arithmetic and copies ran while one was open for 8% -> 9% of each run, Pallas kernels for 32% -> 33%
where the time goes in v4:
time: 693 us; the launch traced here: 689 us
  Pallas kernels  553 us (80%)
  local copies, waits for them, and re-layouts  45.4 us (7%)
  waiting for transfers between devices  37.6 us (5%)
  other arithmetic  19.6 us (3%)
  matrix products  17.7 us (3%)
  between operations  15.1 us (2%)
    pallas_call x2, Pallas kernels, run_block_forward(): pl.pallas_call(functools.partial(block_forward, masked, pushed, layer ==...  182 us
    pallas_call x2, Pallas kernels, run_attention_backward(): pl.pallas_call(functools.partial(attention_backward, pushed), grid=(windo...  180 us
    pallas_call x2, Pallas kernels, run_feed_backward(): pl.pallas_call(feed_backward, grid=(windows // count,), in_specs=[grid_bl...  98 us
    pallas_call x1, Pallas kernels, run_fold_gradients(): pl.pallas_call(fold_gradients, in_specs=[pl.BlockSpec(memory_space=pltpu....  69.6 us
    all_gather x1, waiting for transfers between devices, per_device(): lax.all_gather(jnp.concatenate(local + [vec_rows], axis=0), AXES, axis=0)  37.5 us
    pallas_call x2, Pallas kernels, run_expand_bias(): pl.pallas_call(expand_bias, out_shape=jax.ShapeDtypeStruct((HEADS, WIN, W...  22.9 us
    dot_general x4, matrix products, dot(): return lax.dot_general(left, right, dims, preferred_element_type=F32)  17.7 us
  transfers between devices with their start and end apart: 3, of which 1 were waited for; matrix products, arithmetic and copies ran while one was open for 9% of the time, Pallas kernels for 33%

profile of v4, /device:TPU:25, one launch (start us, length us, event | category | flops | bytes accessed | tf_op | source)
XLA Modules:
  0.0 689.4 jit_solution(9450548400998754139)
XLA Ops:
  13.9 5.4 fusion.46
  19.3 1.2 collective-permute-start
  21.3 13.8 %gather_fusion = s32[2535]{0:T(1024)S(1)} fusion(s32[153664]{0:T(1024)S(1)} %reshape.268, s32[3072]{0:T(1024)S(1)} %pad_clamp_fusion), kind=kCustom, calls=%fused_computation | custom fusion | bytes 30420 | tf_op jit(solution)/shard_map/jit(_take)/gather | solution.py:1015
  35.2 5.0 fusion.8
  41.3 3.8 fusion.5
  46.5 11.6 %shard_map.352.refs_5_ = f32[16,392,392]{2,1,0:T(8,128)} custom-call(f32[128,1352]{1,0:T(8,128)} %get-tuple-element.98.cells_ref), custom_call_target="tpu_custom_call" | custom-call | tf_op jit(solution)/shard_map/pallas_call | solution.py:640
  58.2 11.3 %shard_map.354.refs_5_ = f32[16,392,392]{2,1,0:T(8,128)} custom-call(f32[128,1352]{1,0:T(8,128)} %get-tuple-element.97.cells_ref), custom_call_target="tpu_custom_call" | custom-call | tf_op jit(solution)/shard_map/pallas_call | solution.py:640
  69.6 1.6 select_convert_fusion
  71.2 2.5 fusion.12
  73.7 1.9 fusion.11
  75.8 2.9 fusion.10.grad_ref
  78.7 37.5 %all-gather.3.cloned.1.call-done = bf16[12800,512]{1,0:T(8,128)(2,1)} async-done(((bf16[400,512]{1,0:T(8,128)(2,1)}), bf16[12800,512]{1,0:T(8,128)(2,1)}) %all-gather.3.cloned.1.call-update) | async-done | bytes 13107216 | tf_op jit(solution)/shard_map/all_gather | solution.py:994
  118.9 1.3 concatenate.58.refs_4_.vec_ref
  120.1 91.2 %shard_map.353 = (bf16[8,392,1536]{2,1,0:T(8,128)(2,1)}, bf16[8,16,392,392]{3,2,1,0:T(8,128)(2,1)}, f32[8,392,512]{2,1,0:T(8,128)}, bf16[8,392,512]{2,1,0:T(8,12...) custom-call(bf16[2,14,14,8,512]{4,3,2,1,0:T(8,128)(2,1)} %bitcast.19, ...), custom_call_target="tpu_custom_call" | custom-call | flops 103999995904 | tf_op jit(solution)/shard_map/pallas_call | solution.py:311
  211.3 1.3 concatenate.61.refs_4_.vec_ref
  212.6 91.1 %shard_map.355 = (bf16[8,392,1536]{2,1,0:T(8,128)(2,1)}, bf16[8,16,392,392]{3,2,1,0:T(8,128)(2,1)}, f32[8,392,512]{2,1,0:T(8,128)}, bf16[8,392,512]{2,1,0:T(8,12...) custom-call(f32[2,14,14,8,512]{4,3,2,1,0:T(8,128)} %get-tuple-elemen, ...), custom_call_target="tpu_custom_call" | custom-call | flops 103999995904 | tf_op jit(solution)/shard_map/pallas_call | solution.py:311
  303.7 50.0 %shard_map.356 = (f32[8,392,512]{2,1,0:T(8,128)}, bf16[8,392,512]{2,1,0:T(8,128)(2,1)}, f32[32,192,512]{2,1,0:T(8,128)}, f32[8,512]{1,0:T(8,128)}) custom-call(bf16[2,14,14,8,512]{4,3,2,1,0:T(8,128)(2,1)} %fusion.10.grad_ref, bf16[8,392,2048]{2,1,0:T(8,128)(2,1)} %get-tuple-element.51.act_ref, bf16[8,392,2048]{2,1,0:T(8,128)(2,1)} %get-tuple-element.52.slope_ref, ...), custom_call_target="tpu_custom_call" | custom-call | flops 56000000000 | tf_op jit(solution)/shard_map/pallas_call | solution.py:432
  353.7 95.5 %shard_map.357 = (f32[2,14,14,8,512]{4,3,2,1,0:T(8,128)}, f32[32,192,512]{2,1,0:T(8,128)}, f32[4,512]{1,0:T(4,128)}, f32[128,1352]{1,0:T(8,128)}) custom-call(f32[32,192,512]{2,1,0:T(8,128)} %get-tuple-element.55.whole_ref, f32[2,14,14,8,512]{4,3,2,1,0:T(8,128)} %get-tuple-element.49.refs_0_.x_ref, ...), custom_call_target="tpu_custom_call", output_to_operand_aliasing={{1}: (0, {})} | custom-call | flops 96000000000 | tf_op jit(solution)/shard_map/pallas_call | solution.py:579
  450.5 48.0 %shard_map.358 = (f32[8,392,512]{2,1,0:T(8,128)}, bf16[8,392,512]{2,1,0:T(8,128)(2,1)}, bf16[32,192,512]{2,1,0:T(8,128)(2,1)}, f32[8,512]{1,0:T(8,128)}) custom-call(f32[2,14,14,8,512]{4,3,2,1,0:T(8,128)} %get-tuple-element.61.grad_ref, bf16[8,392,2048]{2,1,0:T(8,128)(2,1)} %get-tuple-element.62.act_ref, bf16[8,392,2048]{2,1,0:T(8,128)(2,1)} %get-tuple-element.63.slope_ref, ...), custom_call_target="tpu_custom_call" | custom-call | flops 56000000000 | tf_op jit(solution)/shard_map/pallas_call | solution.py:432
  498.6 84.5 %shard_map.359 = (bf16[2,14,14,8,512]{4,3,2,1,0:T(8,128)(2,1)}, bf16[32,192,512]{2,1,0:T(8,128)(2,1)}, f32[4,512]{1,0:T(4,128)}, f32[128,1352]{1,0:T(8,128)}) custom-call(bf16[32,192,512]{2,1,0:T(8,128)(2,1)} %get-tuple-element.66.whole_ref, bf16[2,14,14,8,512]{4,3,2,1,0:T(8,128)(2,1)} %bitcast.196, ...), custom_call_target="tpu_custom_call", output_to_operand_aliasing={{1}: (0, {})} | custom-call | flops 96000000000 | tf_op jit(solution)/shard_map/pallas_call | solution.py:579
  585.8 3.7 fusion.4
  592.9 69.6 %shard_map.360 = (f32[192,512]{1,0:T(8,128)}, f32[32,8,512]{2,1,0:T(8,128)}) custom-call(bf16[4,2,2,2,192,512]{5,4,3,2,1,0:T(8,128)(2,1)} %bitcast.157, f32[4,2,2,2,8,512]{5,4,3,2,1,0:T(8,128)} %reshape_reshape.3.refs_1_), custom_call_target="tpu_custom_call" | custom-call | tf_op jit(solution)/shard_map/pallas_call | solution.py:782
  669.5 5.2 fusion
  675.6 2.2 convert_bitcast_fusion
  (173 shorter events, 32.4 us)
Async XLA Ops:
  7.2 109.0 %all-gather.3.cloned.1.call-start = ((), (), s32[]{:S(2)}) async-start(), calls=%async_computation.2 | async-start | bytes 13516800 | tf_op jit(solution)/shard_map/all_gather | solution.py:994
  13.0 0.8 copy-start.2
  13.8 6.7 copy-start
  13.9 7.4 %copy-start.8 = (s32[2535]{0:T(1024)S(1)}, s32[2535]{0:T(1024)}, u32[]{:S(2)}) copy-start(s32[2535]{0:T(1024)} %constant.160) | copy-start | bytes 30424
  13.9 663.9 %reduce-scatter.2.cloned.1.call-start = ((), (), s32[]{:S(2)}) async-start(), calls=%async_computation.1 | async-start | bytes 12976128 | tf_op jit(solution)/shard_map/reduce_scatter | solution.py:1052
  19.3 51.9 %collective-permute-start = (bf16[2,4,14,14,512]{4,1,3,2,0:T(4,128)(2,1)}, bf16[2,4,14,14,512]{4,1,3,2,0:T(4,128)(2,1)}, u32[]{:S(2)}, u32[]{:S(2)}) collective-permute-start(bf16[2,4,14,14,512]{4,1,3,2,0:T(4,128)(2,1)} %get-tuple-element.85), channel_id=1, source_target_pairs={{0,1},{1,0},{2,3},{3,2},{4,5},{5,4},{6,7},{7,6},{8,9},{9,8},{10,11... | collective-permute-start | bytes 4816904 | tf_op jit(solution)/shard_map/ppermute | solution.py:864
  21.3 13.8 %copy-start.4 = (f32[2,2535,16]{1,2,0:T(8,128)S(1)}, f32[2,2535,16]{1,2,0:T(8,128)}, u32[]{:S(2)}) copy-start(f32[2,2535,16]{1,2,0:T(8,128)} %param.40) | copy-start | bytes 973444
  35.1 5.1 copy-start.9
  40.2 1.1 copy-start.19
  58.1 11.4 %copy-start.18 = (pred[392]{0:T(512)(128)(4,1)S(1)}, pred[392]{0:T(512)(128)(4,1)}, u32[]{:S(2)}) copy-start(pred[392]{0:T(512)(128)(4,1)} %constant.112.clone) | copy-start | bytes 1180
  58.1 11.4 %copy-start.12 = (s32[392]{0:T(512)S(1)}, s32[392]{0:T(512)}, u32[]{:S(2)}) copy-start(s32[392]{0:T(512)} %constant.158) | copy-start | bytes 4708
  58.1 11.4 %copy-start.13 = (s32[392]{0:T(512)S(1)}, s32[392]{0:T(512)}, u32[]{:S(2)}) copy-start(s32[392]{0:T(512)} %constant.157) | copy-start | bytes 4708
  58.1 11.5 %copy-start.14 = (s32[128]{0:T(128)S(1)}, s32[128]{0:T(128)}, u32[]{:S(2)}) copy-start(s32[128]{0:T(128)} %constant.115.clone) | copy-start | bytes 1540
  58.1 11.5 %copy-start.15 = (pred[128]{0:T(512)(128)(4,1)S(1)}, pred[128]{0:T(512)(128)(4,1)}, u32[]{:S(2)}) copy-start(pred[128]{0:T(512)(128)(4,1)} %constant.117.clone) | copy-start | bytes 388
  58.1 11.5 %copy-start.16 = (pred[128]{0:T(512)(128)(4,1)S(1)}, pred[128]{0:T(512)(128)(4,1)}, u32[]{:S(2)}) copy-start(pred[128]{0:T(512)(128)(4,1)} %constant.116.clone) | copy-start | bytes 388
  58.2 11.5 %copy-start.17 = (f32[128]{0:T(128)S(1)}, f32[128]{0:T(128)}, u32[]{:S(2)}) copy-start(f32[128]{0:T(128)} %constant.118.clone) | copy-start | bytes 1540
  449.2 0.7 copy-start.6
  498.5 84.5 %copy-start.7 = (f32[8,512]{1,0:T(8,128)S(1)}, f32[8,512]{1,0:T(8,128)}, u32[]{:S(2)}) copy-start(f32[8,512]{1,0:T(8,128)} %get-tuple-element.77) | copy-start | bytes 49156
  498.6 85.2 %copy-start.5 = (f32[1,12,512]{2,1,0:T(8,128)S(1)}, f32[1,12,512]{2,1,0:T(8,128)}, u32[]{:S(2)}) copy-start(f32[1,12,512]{2,1,0:T(8,128)} %maximum_bitcast_fusion.5) | copy-start | bytes 73732
  498.6 85.3 %copy-start.1 = (f32[128,1352]{1,0:T(8,128)S(1)}, f32[128,1352]{1,0:T(8,128)}, u32[]{:S(2)}) copy-start(f32[128,1352]{1,0:T(8,128)} %get-tuple-element.75) | copy-start | bytes 2076676
  662.6 6.8 copy-start.3
  662.6 6.9 %copy-start.10 = (s32[2535]{0:T(1024)S(1)}, s32[2535]{0:T(1024)}, u32[]{:S(2)}) copy-start(s32[2535]{0:T(1024)} %copy-done.9) | copy-start | bytes 30424
  669.5 6.1 slice-start
  669.5 6.1 slice-start.1
  (2 other events, 1.4 us)
Sparse Core Ops, SparseCore 0:
  14.0 102.2 all-gather.2
  449.4 153.7 reduce-scatter.1

commit v5 on v4

--- a/solution.py
+++ b/solution.py
@@ -52,7 +52,7 @@
 
 def cost(windows, microseconds):
     return pl.CostEstimate(
-        flops=int(windows * microseconds * 1e9), bytes_accessed=0, transcendentals=0
+        flops=int(windows * microseconds * 2e8), bytes_accessed=0, transcendentals=0
     )
 
 
@@ -168,14 +168,81 @@
             copy.wait_send()
 
 
-def push_begin():
+def own_place():
+    batch = lax.axis_index("batch")
+    return batch // 4, (batch // 2) % 2, batch % 2, lax.axis_index("seq")
+
+
+def device_at(z, x, core, y):
+    return ((z * 2 + x) * 2 + core, y)
+
+
+def push_begin(carried):
     @pl.when(pl.program_id(0) == 0)
     def _():
         barrier = pltpu.get_barrier_semaphore()
-        pl.semaphore_signal(
-            barrier, inc=1, device_id=neighbour(), device_id_type=pl.DeviceIdType.MESH
+        peers = [neighbour()]
+        if carried:
+            z, x, core, y = own_place()
+            peers += [device_at(lax.rem(z + i, 4), x, core, y) for i in range(1, 4)]
+            peers += [device_at(z, 1 - x, core, y), device_at(z, x, 1 - core, y)]
+        for peer in peers:
+            pl.semaphore_signal(
+                barrier, inc=1, device_id=peer, device_id_type=pl.DeviceIdType.MESH
+            )
+        pl.semaphore_wait(barrier, len(peers))
+
+
+def carry_gather(shard_ref, full_ref, shard_sem, send_sem, recv_sem):
+    step = pl.program_id(0)
+    z, x, core, y = own_place()
+    mine = full_ref.at[z, x, core, y]
+    keep = pltpu.make_async_copy(shard_ref, mine, shard_sem)
+
+    def send(number, source, target, to):
+        return pltpu.make_async_remote_copy(
+            src_ref=source,
+            dst_ref=target,
+            send_sem=send_sem.at[number],
+            recv_sem=recv_sem.at[number],
+            device_id=to,
+            device_id_type=pl.DeviceIdType.MESH,
         )
-        pl.semaphore_wait(barrier, 1)
+
+    pair = full_ref.at[z, x, core]
+    plane = full_ref.at[:, x, core]
+    half = full_ref.at[:, :, core]
+    over_y = send(0, shard_ref, mine, device_at(z, x, core, 1 - y))
+    over_z = [
+        send(i, pair, pair, device_at(lax.rem(z + i, 4), x, core, y)) for i in range(1, 4)
+    ]
+    over_x = send(4, plane, plane, device_at(z, 1 - x, core, y))
+    over_core = send(5, half, half, device_at(z, x, 1 - core, y))
+
+    @pl.when(step == 0)
+    def _():
+        keep.start()
+        over_y.start()
+
+    @pl.when(step == 1)
+    def _():
+        keep.wait()
+        over_y.wait()
+        for copy in over_z:
+            copy.start()
+
+    @pl.when(step == 4)
+    def _():
+        for copy in over_z:
+            copy.wait()
+        over_x.start()
+
+    @pl.when(step == 7)
+    def _():
+        over_x.wait()
+        over_core.start()
+
+    return over_core
 
 
 def push_window(forth, value, out_ref, stage, own_sem, send_sem, recv_sem):
@@ -214,16 +281,22 @@
     return hidden * cumulative, cumulative + hidden * decay * 0.3989422804014327
 
 
-def block_forward(masked, pushed, forth, *refs):
+def block_forward(masked, pushed, forth, carried, *refs):
     x_ref, w_ref, up_ref, down_ref, vec_ref, bias_ref = refs[:6]
     refs = refs[6:]
     if masked:
         augq_ref, augk_ref = refs[:2]
         refs = refs[2:]
+    if carried:
+        shard_ref = refs[0]
+        refs = refs[1:]
     qkv_ref, soft_ref, rate_ref, att_ref, mid_ref, act_ref, slope_ref, out_ref = refs[:8]
     push = refs[8:]
     if pushed:
-        push_begin()
+        push_begin(carried)
+    if carried:
+        last_copy = carry_gather(shard_ref, push[0], *push[5:])
+        push = push[1:5]
     x = x_ref[0].astype(F32).reshape(WIN, D)
     normed = (normalize(x)[0] * vec_ref[0:1] + vec_ref[1:2]).astype(BF16)
     query = (dot(normed, square(w_ref, 0)) + vec_ref[2:3]) * (SCALE * LOG2E)
@@ -300,26 +373,39 @@
     total = total + lower_part(3, last)
     if pushed:
         push_window(forth, total, out_ref, *push)
+        if carried:
+            @pl.when(pl.program_id(0) == pl.num_programs(0) - 1)
+            def _():
+                last_copy.wait()
     else:
         out_ref[0] = total.reshape(WH, WW, WT, D).astype(out_ref.dtype)
 
 
-def run_block_forward(layer, x, pack, vec, bias, aug, dtype, pushed):
+def run_block_forward(layer, x, pack, vec, bias, aug, dtype, pushed, shard):
     windows = x.shape[0] * (x.shape[1] // WH) * (x.shape[2] // WW)
     masked = aug is not None
     extra = list(aug) if masked else []
+    carried = shard is not None
+    space = [pl.BlockSpec(memory_space=pl.ANY)] if carried else []
+    full = [jax.ShapeDtypeStruct((4, 2, 2, 2, 192, D), BF16)] if carried else []
+    semaphores = [
+        pltpu.SemaphoreType.DMA,
+        pltpu.SemaphoreType.DMA((6,)),
+        pltpu.SemaphoreType.DMA((6,)),
+    ]
     return pl.pallas_call(
-        functools.partial(block_forward, masked, pushed, layer == 0),
+        functools.partial(block_forward, masked, pushed, layer == 0, carried),
         grid=(windows,),
         in_specs=[
             grid_spec(x.shape),
-            pack_spec(64, 3 * layer),
-            pack_spec(64, 3 * layer + 1),
-            pack_spec(64, 3 * layer + 2),
+            pack_spec(64, 0),
+            pack_spec(64, 1),
+            pack_spec(64, 2),
             whole_spec(12, D),
             whole_spec(HEADS, WIN, WIN),
         ]
-        + [window_spec(WIN, 128)] * len(extra),
+        + [window_spec(WIN, 128)] * len(extra)
+        + space,
         out_specs=[
             window_spec(WIN, 3 * D),
             window_spec(HEADS, WIN, WIN),
@@ -329,7 +415,8 @@
             window_spec(WIN, FF),
             window_spec(WIN, FF),
             pl.BlockSpec(memory_space=pl.ANY) if pushed else grid_spec(x.shape),
-        ],
+        ]
+        + space,
         out_shape=[
             jax.ShapeDtypeStruct((windows, WIN, 3 * D), BF16),
             jax.ShapeDtypeStruct((windows, HEADS, WIN, WIN), BF16),
@@ -339,11 +426,12 @@
             jax.ShapeDtypeStruct((windows, WIN, FF), BF16),
             jax.ShapeDtypeStruct((windows, WIN, FF), BF16),
             jax.ShapeDtypeStruct(x.shape, dtype),
-        ],
-        scratch_shapes=push_scratch() if pushed else [],
+        ]
+        + full,
+        scratch_shapes=(push_scratch() if pushed else []) + (semaphores if carried else []),
         cost_estimate=cost(windows, 13),
         compiler_params=params(2 + layer if pushed else None),
-    )(x, pack, pack, pack, vec, bias, *extra)
+    )(x, pack, pack, pack, vec, bias, *extra, *([shard] if carried else []))
 
 
 def norm_back(normal, rate, gained):
@@ -369,29 +457,31 @@
     gvec_ref[3:4] += sum(row_sum(grad) for grad in grads)
     lows = [grad.astype(BF16) for grad in grads]
     normals = [normalize(mid_ref[w]) for w in each]
-    normed = [(normals[w][0] * vec_ref[5:6] + vec_ref[6:7]).astype(BF16) for w in each]
-    gnormed = [jnp.zeros((WIN, D), F32) for w in each]
+    gnormed = [jnp.zeros((count * WIN, D), F32)]
+
+    low_all = jnp.concatenate(grads, axis=0).astype(BF16)
+    normed_all = jnp.concatenate(
+        [normals[w][0] * vec_ref[5:6] + vec_ref[6:7] for w in each], axis=0
+    ).astype(BF16)
 
     def back_part(part):
-        down = down_ref[part * 8 : part * 8 + 8].reshape(D, D)
-        return [dot(lows[w], down, NT) for w in each]
+        return dot(low_all, down_ref[part * 8 : part * 8 + 8].reshape(D, D), NT)
 
     def finish(part, ghidden):
         first = ROWS * (1 + part)
-        total = sum(dot(normed[w], ghidden[w], TN) for w in each)
+        total = dot(normed_all, ghidden, TN)
         pack_ref[:, first : first + ROWS, :] += total.reshape(PACKS, ROWS, D)
-        up = square(up_ref, part * ROWS)
-        for w in each:
-            gnormed[w] = gnormed[w] + dot(ghidden[w], up, NT)
+        gnormed[0] = gnormed[0] + dot(ghidden, square(up_ref, part * ROWS), NT)
 
     gactive = back_part(0)
     last = None
     for part in range(4):
         following = back_part(part + 1) if part < 3 else None
         lanes = slice(part * D, (part + 1) * D)
-        ghidden = [gactive[w] * slope_ref[w, :, lanes].astype(F32) for w in each]
-        gvec_ref[4 + part : 5 + part] += sum(row_sum(value) for value in ghidden)
-        ghidden = [value.astype(BF16) for value in ghidden]
+        slopes = [slope_ref[w, :, lanes].astype(F32) for w in each]
+        ghidden = gactive * jnp.concatenate(slopes, axis=0)
+        gvec_ref[4 + part : 5 + part] += row_sum(ghidden)
+        ghidden = ghidden.astype(BF16)
         total = sum(dot(act_ref[w, :, lanes], lows[w], TN) for w in each)
         pack_ref[part * 8 : part * 8 + 8, 80:144, :] += total.reshape(8, 64, D)
         if part > 0:
@@ -399,8 +489,9 @@
         last = ghidden
         gactive = following
     finish(3, last)
-    outer = square(in_ref, 3 * ROWS)
+    outer = square(in_ref, 0)
     total = jnp.zeros((D, D), F32)
+    gnormed = [gnormed[0][WIN * w : WIN * (w + 1)] for w in each]
     for w in each:
         normal, rate = normals[w]
         gvec_ref[1:2] += row_sum(gnormed[w] * normal)
@@ -438,9 +529,9 @@
             some(FF),
             some(D),
             some(D),
-            pack_spec(64, 3 * layer),
-            pack_spec(64, 3 * layer + 1),
-            pack_spec(64, 3 * layer + 2),
+            pack_spec(ROWS, 3),
+            pack_spec(64, 1),
+            pack_spec(64, 2),
             whole_spec(12, D),
         ],
         out_specs=[
@@ -469,7 +560,7 @@
 ):
     step = pl.program_id(0)
     if pushed:
-        push_begin()
+        push_begin(False)
 
     @pl.when(step == 0)
     def _():
@@ -588,7 +679,7 @@
             window_spec(HEADS, WIN, WIN),
             window_spec(WIN, 3 * D),
             window_spec(WIN, D),
-            pack_spec(64, 3 * layer),
+            pack_spec(48, 0),
             whole_spec(12, D),
         ],
         out_specs=[
@@ -741,17 +832,6 @@
                     device(other, x, core, y),
                 )
             )
-    for k, (which, first, size, order) in enumerate(SHARES):
-        for step in range(1, 4):
-            far[3 * k + step - 1].wait()
-        held = buffers[3 * k + 2]
-        total = held[z].astype(F32) + held[4].astype(F32)
-        total = total + held[5].astype(F32) + held[6].astype(F32)
-        if which == 0:
-            pack_out[first : first + size, :] = total
-        else:
-            aux_out[batch * 2 + y] = total
-
     def spread(k, carry):
         other = lax.rem(batch * 2 + y + k, 32)
         pltpu.make_async_remote_copy(
@@ -763,6 +843,17 @@
             device_id_type=pl.DeviceIdType.MESH,
         ).start()
         return carry
+
+    for k, (which, first, size, order) in enumerate(SHARES):
+        for step in range(1, 4):
+            far[3 * k + step - 1].wait()
+        held = buffers[3 * k + 2]
+        total = held[z].astype(F32) + held[4].astype(F32)
+        total = total + held[5].astype(F32) + held[6].astype(F32)
+        if which == 0:
+            pack_out[first : first + size, :] = total
+        else:
+            aux_out[batch * 2 + y] = total
 
     lax.fori_loop(1, 32, spread, 0)
     others = aux_out.at[pl.ds(0, 31)]
@@ -794,6 +885,7 @@
             pltpu.SemaphoreType.DMA,
             pltpu.SemaphoreType.DMA,
         ],
+        cost_estimate=cost(1, 1),
         compiler_params=pltpu.CompilerParams(
             vmem_limit_bytes=61 * 1024 * 1024, collective_id=1, has_side_effects=True
         ),
@@ -991,10 +1083,14 @@
         pack_layer(inner_weight[layer], outer_weight[layer], up_weight[layer], down_weight[layer])
         for layer in range(LAYERS)
     ]
-    full = lax.all_gather(jnp.concatenate(local + [vec_rows], axis=0), AXES, axis=0)
+    folded = lax.axis_size("batch") == 16 and lax.axis_size("seq") == 2
+    shape = place.grid_shape()
+    carried = folded and place.near and shape[0] == 2
+    first_part = [local[0], vec_rows] if carried else local + [vec_rows]
+    full = lax.all_gather(jnp.concatenate(first_part, axis=0), AXES, axis=0)
     vecs = []
     for layer in range(LAYERS):
-        held = full[:, 24 * rows + layer, :width].astype(F32)
+        held = full[:, full.shape[1] - 16 + layer, :width].astype(F32)
         pieces = []
         start = 0
         for vector in vectors:
@@ -1002,23 +1098,23 @@
             pieces.append(held[:, start : start + size].reshape(-1, D))
             start += size
         vecs.append(jnp.concatenate(pieces, axis=0))
-    if rows != ROWS:
-        parts = []
-        for first in (0, 12 * rows):
+    packs = [full, None]
+    if not carried:
+        for layer in range(LAYERS):
+            parts = []
+            first = 12 * rows * layer
             for i in range(8):
                 part = full[:, first + i * rows : first + (i + 1) * rows]
                 parts.append(part.reshape(PACKS, ROWS, D))
             part = full[:, first + 8 * rows : first + 12 * rows]
             parts.append(part.reshape(PACKS, 4 * ROWS, D))
-        full = jnp.concatenate(parts, axis=1)
-    weights = [(full, vec) for vec in vecs]
+            packs[layer] = jnp.concatenate(parts, axis=1)
     taken_rows = jnp.take(offset_index.reshape(-1), offset_places())
     order = jnp.arange(BIAS_ROWS, dtype=jnp.int32)
     chosen = (taken_rows[:, None] == order[None, :]).astype(BF16)
     interleaved = interleave()
     cells_in = bias_cells(bias_table, chosen, interleaved)
     bias = [run_expand_bias(cells_in[layer]) for layer in range(LAYERS)]
-    shape = place.grid_shape()
     aug = place.mask_lanes()
 
     x_zero = place.enter(clips_in, False)
@@ -1026,11 +1122,14 @@
     saved = []
     x = x_zero
     for layer in range(LAYERS):
-        pack, vec = weights[layer]
-        qkv, soft, rates, attended, middle, active, slope, result = run_block_forward(
-            layer, x, pack, vec, bias[layer], aug if layer == 1 else None,
+        outs = run_block_forward(
+            layer, x, packs[layer], vecs[layer], bias[layer], aug if layer == 1 else None,
             F32 if layer == 0 or place.near else BF16, place.near,
+            local[1] if carried and layer == 0 else None,
         )
+        qkv, soft, rates, attended, middle, active, slope, result = outs[:8]
+        if carried and layer == 0:
+            packs[1] = outs[8].reshape(PACKS, 192, D)
         saved.append((x, qkv, soft, rates, attended, middle, active, slope))
         x = place.forth(result) if layer == 0 and not place.near else result
     clips_out = place.leave(x, not place.near).astype(BF16)
@@ -1051,16 +1150,15 @@
             value = jnp.concatenate(parts, axis=1)
         return lax.psum_scatter(value, AXES, scatter_dimension=0, tiled=False)
 
-    folded = lax.axis_size("batch") == 16 and lax.axis_size("seq") == 2
     for layer in reversed(range(LAYERS)):
-        pack, vec = weights[layer]
+        pack, vec = packs[layer], vecs[layer]
         x, qkv, soft, rates, attended, middle, active, slope = saved[layer]
         gmiddle, gattended, big, gvec_two = run_feed_backward(
-            layer, upstream, active, slope, middle, attended, pack, vec, F32 if layer == 1 or not folded else BF16
+            layer, upstream, active, slope, middle, attended, pack, vec, BF16 if folded else F32
         )
         upstream, big, gvec_one, cells = run_attention_backward(
             layer, big, x, gattended, attended, rates, soft, qkv, gmiddle, pack, vec,
-            F32 if layer == 1 else BF16, F32 if layer == 1 or not folded else BF16,
+            F32 if layer == 1 else BF16, BF16 if folded else F32,
             place.near and layer == 1,
         )
         if layer == 1 or not folded:
@@ -1077,6 +1175,7 @@
         aux = jnp.concatenate([table_rows.reshape(-1), vec_stack.reshape(-1)])
         used = aux.shape[0]
         aux = jnp.pad(aux, (0, PACKS * AUX_ROWS * D - used)).reshape(PACKS, AUX_ROWS, D)
+        big, scattered[1] = lax.optimization_barrier((big, scattered[1]))
         scattered[0], aux = run_fold_gradients(big, aux)
         aux = aux.reshape(-1)[:used]
         table_total = aux[: table_rows.size].reshape(table_rows.shape)
@@ -1085,6 +1184,7 @@
         vec_total, table_total = lax.psum((vec_stack, table_rows), AXES)
     table_total = rows_to_table(table_total, chosen)
 
+    scattered = [value.astype(F32) for value in scattered]
     device = lax.axis_index(AXES)
 
     def own(first, count):

time: 693 us -> 684 us (0.987)
  waiting for transfers between devices: 37.6 us -> 9.5 us
  Pallas kernels: 553 us -> 567 us
    all_gather x1, waiting for transfers between devices: 37.5 us -> 9.47 us  [per_device(): full = lax.all_gather(jnp.concatenate(first_part, axis=0), AXES, axis=0)]
    pallas_call x2, Pallas kernels: 182 us -> 200 us  [run_block_forward(): pl.pallas_call(functools.partial(block_forward, masked, pushed, layer ==...]
  transfers between devices with their start and end apart: 3 -> 3, of which waited for: 1 -> 1; matrix products, arithmetic and copies ran while one was open for 9% -> 8% of each run, Pallas kernels for 33% -> 23%
where the time goes in v5:
time: 684 us; the launch traced here: 681 us
  Pallas kernels  567 us (83%)
  local copies, waits for them, and re-layouts  48.6 us (7%)
  other arithmetic  21.9 us (3%)
  matrix products  17.7 us (3%)
  between operations  15 us (2%)
  waiting for transfers between devices  9.5 us (1%)
    pallas_call x2, Pallas kernels, run_block_forward(): pl.pallas_call(functools.partial(block_forward, masked, pushed, layer ==...  200 us
    pallas_call x2, Pallas kernels, run_attention_backward(): pl.pallas_call(functools.partial(attention_backward, pushed), grid=(windo...  178 us
    pallas_call x2, Pallas kernels, run_feed_backward(): pl.pallas_call(feed_backward, grid=(windows // count,), in_specs=[grid_bl...  95.9 us
    pallas_call x1, Pallas kernels, run_fold_gradients(): pl.pallas_call(fold_gradients, in_specs=[pl.BlockSpec(memory_space=pltpu....  69.6 us
    pallas_call x2, Pallas kernels, run_expand_bias(): pl.pallas_call(expand_bias, out_shape=jax.ShapeDtypeStruct((HEADS, WIN, W...  22.9 us
    dot_general x4, matrix products, dot(): return lax.dot_general(left, right, dims, preferred_element_type=F32)  17.7 us
    gather x1, local copies, waits for them, and re-layouts, per_device(): taken_rows = jnp.take(offset_index.reshape(-1), offset_places())  13.8 us
  transfers between devices with their start and end apart: 3, of which 1 were waited for; matrix products, arithmetic and copies ran while one was open for 8% of the time, Pallas kernels for 23%

profile of v5, /device:TPU:25, one launch (start us, length us, event | category | flops | bytes accessed | tf_op | source)
XLA Modules:
  0.0 680.7 jit_solution(3219680777410116546)
XLA Ops:
  10.8 1.3 constant_dynamic-update-slice_fusion.13
  14.6 1.5 bitcast_dynamic-update-slice_fusion
  17.7 5.4 fusion.46
  25.1 13.8 %gather_fusion = s32[2535]{0:T(1024)S(1)} fusion(s32[153664]{0:T(1024)S(1)} %reshape.260, s32[3072]{0:T(1024)S(1)} %pad_clamp_fusion), kind=kCustom, calls=%fused_computation | custom fusion | bytes 30420 | tf_op jit(solution)/shard_map/jit(_take)/gather | solution.py:1112
  39.0 5.0 fusion.8
  45.1 3.8 fusion.5
  50.4 11.6 %shard_map.352.refs_5_ = f32[16,392,392]{2,1,0:T(8,128)} custom-call(f32[128,1352]{1,0:T(8,128)} %get-tuple-element.104.cells_ref), custom_call_target="tpu_custom_call" | custom-call | tf_op jit(solution)/shard_map/pallas_call | solution.py:731
  62.0 11.3 %shard_map.354.refs_5_ = f32[16,392,392]{2,1,0:T(8,128)} custom-call(f32[128,1352]{1,0:T(8,128)} %get-tuple-element.103.cells_ref), custom_call_target="tpu_custom_call" | custom-call | tf_op jit(solution)/shard_map/pallas_call | solution.py:731
  73.4 1.6 select_convert_fusion
  75.0 2.5 fusion.12
  77.5 1.9 fusion.11
  79.6 2.8 fusion.10.grad_ref
  82.5 9.5 %all-gather.3.cloned.1.call-done = bf16[6656,512]{1,0:T(8,128)(2,1)} async-done(((bf16[208,512]{1,0:T(8,128)(2,1)}), bf16[6656,512]{1,0:T(8,128)(2,1)}) %all-gather.3.cloned.1.call-update) | async-done | bytes 6815760 | tf_op jit(solution)/shard_map/all_gather | solution.py:1090
  94.7 1.3 concatenate.61.refs_4_.vec_ref
  96.0 109.6 %shard_map.353 = (bf16[8,392,1536]{2,1,0:T(8,128)(2,1)}, bf16[8,16,392,392]{3,2,1,0:T(8,128)(2,1)}, f32[8,392,512]{2,1,0:T(8,128)}, bf16[8,392,512]{2,1,0:T(8,12...) custom-call(bf16[2,14,14,8,512]{4,3,2,1,0:T(8,128)(2,1)} %bitcast.16, ...), custom_call_target="tpu_custom_call" | custom-call | flops 20800000000 | tf_op jit(solution)/shard_map/pallas_call | solution.py:396
  206.8 90.3 %shard_map.355 = (bf16[8,392,1536]{2,1,0:T(8,128)(2,1)}, bf16[8,16,392,392]{3,2,1,0:T(8,128)(2,1)}, f32[8,392,512]{2,1,0:T(8,128)}, bf16[8,392,512]{2,1,0:T(8,12...) custom-call(f32[2,14,14,8,512]{4,3,2,1,0:T(8,128)} %get-tuple-elemen, ...), custom_call_target="tpu_custom_call" | custom-call | flops 20800000000 | tf_op jit(solution)/shard_map/pallas_call | solution.py:396
  297.1 48.1 %shard_map.356 = (f32[8,392,512]{2,1,0:T(8,128)}, bf16[8,392,512]{2,1,0:T(8,128)(2,1)}, bf16[32,192,512]{2,1,0:T(8,128)(2,1)}, f32[8,512]{1,0:T(8,128)}) custom-call(bf16[2,14,14,8,512]{4,3,2,1,0:T(8,128)(2,1)} %fusion.10.grad_ref, bf16[8,392,2048]{2,1,0:T(8,128)(2,1)} %get-tuple-element.55.act_ref, bf16[8,392,2048]{2,1,0:T(8,128)(2,1)} %get-tuple-element.56.slope_ref, ...), custom_call_target="tpu_custom_call" | custom-call | flops 11200000000 | tf_op jit(solution)/shard_map/pallas_call | solution.py:523
  345.3 94.1 %shard_map.357 = (f32[2,14,14,8,512]{4,3,2,1,0:T(8,128)}, bf16[32,192,512]{2,1,0:T(8,128)(2,1)}, f32[4,512]{1,0:T(4,128)}, f32[128,1352]{1,0:T(8,128)}) custom-call(bf16[32,192,512]{2,1,0:T(8,128)(2,1)} %get-tuple-element.59.whole_ref, f32[2,14,14,8,512]{4,3,2,1,0:T(8,128)} %get-tuple-element.52.refs_0_.x_ref, ...), custom_call_target="tpu_custom_call", output_to_operand_aliasing={{1}: (0, {})} | custom-call | flops 19200000000 | tf_op jit(solution)/shard_map/pallas_call | solution.py:670
  439.4 47.8 %shard_map.358 = (f32[8,392,512]{2,1,0:T(8,128)}, bf16[8,392,512]{2,1,0:T(8,128)(2,1)}, bf16[32,192,512]{2,1,0:T(8,128)(2,1)}, f32[8,512]{1,0:T(8,128)}) custom-call(f32[2,14,14,8,512]{4,3,2,1,0:T(8,128)} %get-tuple-element.65.grad_ref, bf16[8,392,2048]{2,1,0:T(8,128)(2,1)} %get-tuple-element.66.act_ref, bf16[8,392,2048]{2,1,0:T(8,128)(2,1)} %get-tuple-element.67.slope_ref, ...), custom_call_target="tpu_custom_call" | custom-call | flops 11200000000 | tf_op jit(solution)/shard_map/pallas_call | solution.py:523
  487.2 84.3 %shard_map.359 = (bf16[2,14,14,8,512]{4,3,2,1,0:T(8,128)(2,1)}, bf16[32,192,512]{2,1,0:T(8,128)(2,1)}, f32[4,512]{1,0:T(4,128)}, f32[128,1352]{1,0:T(8,128)}) custom-call(bf16[32,192,512]{2,1,0:T(8,128)(2,1)} %get-tuple-element.70.whole_ref, bf16[2,14,14,8,512]{4,3,2,1,0:T(8,128)(2,1)} %bitcast.167, ...), custom_call_target="tpu_custom_call", output_to_operand_aliasing={{1}: (0, {})} | custom-call | flops 19200000000 | tf_op jit(solution)/shard_map/pallas_call | solution.py:670
  574.2 3.7 fusion.4
  581.4 5.0 convert_bitcast_fusion
  586.4 69.6 %shard_map.360 = (f32[192,512]{1,0:T(8,128)}, f32[32,8,512]{2,1,0:T(8,128)}) custom-call(bf16[4,2,2,2,192,512]{5,4,3,2,1,0:T(8,128)(2,1)} %bitcast.164, f32[4,2,2,2,8,512]{5,4,3,2,1,0:T(8,128)} %reshape_reshape.3.refs_1_), custom_call_target="tpu_custom_call" | custom-call | flops 200000000 | tf_op jit(solution)/shard_map/pallas_call | solution.py:873
  663.5 5.2 fusion
  (166 shorter events, 34.8 us)
Async XLA Ops:
  7.2 84.8 %all-gather.3.cloned.1.call-start = ((), (), s32[]{:S(2)}) async-start(), calls=%async_computation.2 | async-start | bytes 7028736 | tf_op jit(solution)/shard_map/all_gather | solution.py:1090
  17.0 0.7 copy-start.4
  17.7 6.7 copy-start.1
  17.7 7.4 %copy-start.7 = (s32[2535]{0:T(1024)S(1)}, s32[2535]{0:T(1024)}, u32[]{:S(2)}) copy-start(s32[2535]{0:T(1024)} %constant.160) | copy-start | bytes 30424
  17.7 568.8 %reduce-scatter.2.cloned.1.call-start = ((), (), s32[]{:S(2)}) async-start(), calls=%async_computation.1 | async-start | bytes 6488064 | tf_op jit(solution)/shard_map/reduce_scatter | solution.py:1151
  23.1 51.9 %collective-permute-start = (bf16[2,4,14,14,512]{4,1,3,2,0:T(4,128)(2,1)}, bf16[2,4,14,14,512]{4,1,3,2,0:T(4,128)(2,1)}, u32[]{:S(2)}, u32[]{:S(2)}) collective-permute-start(bf16[2,4,14,14,512]{4,1,3,2,0:T(4,128)(2,1)} %get-tuple-element.91), channel_id=1, source_target_pairs={{0,1},{1,0},{2,3},{3,2},{4,5},{5,4},{6,7},{7,6},{8,9},{9,8},{10,11... | collective-permute-start | bytes 4816904 | tf_op jit(solution)/shard_map/ppermute | solution.py:956
  25.1 13.8 %copy-start.3 = (f32[2,2535,16]{1,2,0:T(8,128)S(1)}, f32[2,2535,16]{1,2,0:T(8,128)}, u32[]{:S(2)}) copy-start(f32[2,2535,16]{1,2,0:T(8,128)} %param.40) | copy-start | bytes 973444
  38.9 5.1 copy-start.8
  44.0 1.1 copy-start.18
  61.9 11.4 %copy-start.17 = (pred[392]{0:T(512)(128)(4,1)S(1)}, pred[392]{0:T(512)(128)(4,1)}, u32[]{:S(2)}) copy-start(pred[392]{0:T(512)(128)(4,1)} %constant.112.clone) | copy-start | bytes 1180
  61.9 11.4 %copy-start.11 = (s32[392]{0:T(512)S(1)}, s32[392]{0:T(512)}, u32[]{:S(2)}) copy-start(s32[392]{0:T(512)} %constant.158) | copy-start | bytes 4708
  61.9 11.4 %copy-start.12 = (s32[392]{0:T(512)S(1)}, s32[392]{0:T(512)}, u32[]{:S(2)}) copy-start(s32[392]{0:T(512)} %constant.157) | copy-start | bytes 4708
  61.9 11.5 %copy-start.13 = (s32[128]{0:T(128)S(1)}, s32[128]{0:T(128)}, u32[]{:S(2)}) copy-start(s32[128]{0:T(128)} %constant.115.clone) | copy-start | bytes 1540
  62.0 11.5 %copy-start.14 = (pred[128]{0:T(512)(128)(4,1)S(1)}, pred[128]{0:T(512)(128)(4,1)}, u32[]{:S(2)}) copy-start(pred[128]{0:T(512)(128)(4,1)} %constant.117.clone) | copy-start | bytes 388
  62.0 11.5 %copy-start.15 = (pred[128]{0:T(512)(128)(4,1)S(1)}, pred[128]{0:T(512)(128)(4,1)}, u32[]{:S(2)}) copy-start(pred[128]{0:T(512)(128)(4,1)} %constant.116.clone) | copy-start | bytes 388
  62.0 11.5 %copy-start.16 = (f32[128]{0:T(128)S(1)}, f32[128]{0:T(128)}, u32[]{:S(2)}) copy-start(f32[128]{0:T(128)} %constant.118.clone) | copy-start | bytes 1540
  439.4 47.8 %copy-start.5 = (f32[8,512]{1,0:T(8,128)S(1)}, f32[8,512]{1,0:T(8,128)}, u32[]{:S(2)}) copy-start(f32[8,512]{1,0:T(8,128)} %get-tuple-element.85) | copy-start | bytes 49156
  439.4 47.8 %copy-start.10 = (f32[4,512]{1,0:T(4,128)S(1)}, f32[4,512]{1,0:T(4,128)}, u32[]{:S(2)}) copy-start(f32[4,512]{1,0:T(4,128)} %get-tuple-element.84) | copy-start | bytes 24580
  487.2 84.3 %copy-start.6 = (f32[8,512]{1,0:T(8,128)S(1)}, f32[8,512]{1,0:T(8,128)}, u32[]{:S(2)}) copy-start(f32[8,512]{1,0:T(8,128)} %get-tuple-element.83) | copy-start | bytes 49156
  487.2 85.1 %copy-start.2 = (f32[128,1352]{1,0:T(8,128)S(1)}, f32[128,1352]{1,0:T(8,128)}, u32[]{:S(2)}) copy-start(f32[128,1352]{1,0:T(8,128)} %get-tuple-element.81) | copy-start | bytes 2076676
  573.5 0.7 copy-start.19
  586.4 70.9 %copy-start = (bf16[1,192,512]{2,1,0:T(8,128)(2,1)S(1)}, bf16[1,192,512]{2,1,0:T(8,128)(2,1)}, u32[]{:S(2)}) copy-start(bf16[1,192,512]{2,1,0:T(8,128)(2,1)} %reduce-scatter.2.cloned.1.call-done) | copy-start | bytes 589828
  656.0 7.4 %copy-start.9 = (s32[2535]{0:T(1024)S(1)}, s32[2535]{0:T(1024)}, u32[]{:S(2)}) copy-start(s32[2535]{0:T(1024)} %copy-done.8) | copy-start | bytes 30424
Sparse Core Ops, SparseCore 0:
  17.8 74.1 all-gather.2
  439.5 114.1 reduce-scatter.1

commit v6 on v5

--- a/solution.py
+++ b/solution.py
@@ -209,15 +209,19 @@
             device_id_type=pl.DeviceIdType.MESH,
         )
 
-    pair = full_ref.at[z, x, core]
-    plane = full_ref.at[:, x, core]
+    top, bottom = pl.ds(0, 96), pl.ds(96, 96)
+    top_pair = full_ref.at[z, x, core, :, top, :]
+    low_pair = full_ref.at[z, x, core, :, bottom, :]
+    top_line = full_ref.at[:, x, core, :, top, :]
+    low_both = full_ref.at[z, :, core, :, bottom, :]
     half = full_ref.at[:, :, core]
     over_y = send(0, shard_ref, mine, device_at(z, x, core, 1 - y))
-    over_z = [
-        send(i, pair, pair, device_at(lax.rem(z + i, 4), x, core, y)) for i in range(1, 4)
-    ]
-    over_x = send(4, plane, plane, device_at(z, 1 - x, core, y))
-    over_core = send(5, half, half, device_at(z, x, 1 - core, y))
+    levels = [device_at(lax.rem(z + i, 4), x, core, y) for i in range(1, 4)]
+    top_z = [send(1 + i, top_pair, top_pair, to) for i, to in enumerate(levels)]
+    low_x = send(4, low_pair, low_pair, device_at(z, 1 - x, core, y))
+    top_x = send(5, top_line, top_line, device_at(z, 1 - x, core, y))
+    low_z = [send(6 + i, low_both, low_both, to) for i, to in enumerate(levels)]
+    over_core = send(9, half, half, device_at(z, x, 1 - core, y))
 
     @pl.when(step == 0)
     def _():
@@ -228,18 +232,24 @@
     def _():
         keep.wait()
         over_y.wait()
-        for copy in over_z:
+        low_x.start()
+        for copy in top_z:
             copy.start()
 
-    @pl.when(step == 4)
+    @pl.when(step == 3)
     def _():
-        for copy in over_z:
+        low_x.wait()
+        for copy in low_z:
+            copy.start()
+        for copy in top_z:
             copy.wait()
-        over_x.start()
-
-    @pl.when(step == 7)
+        top_x.start()
+
+    @pl.when(step == 6)
     def _():
-        over_x.wait()
+        for copy in low_z:
+            copy.wait()
+        top_x.wait()
         over_core.start()
 
     return over_core
@@ -390,8 +400,8 @@
     full = [jax.ShapeDtypeStruct((4, 2, 2, 2, 192, D), BF16)] if carried else []
     semaphores = [
         pltpu.SemaphoreType.DMA,
-        pltpu.SemaphoreType.DMA((6,)),
-        pltpu.SemaphoreType.DMA((6,)),
+        pltpu.SemaphoreType.DMA((10,)),
+        pltpu.SemaphoreType.DMA((10,)),
     ]
     return pl.pallas_call(
         functools.partial(block_forward, masked, pushed, layer == 0, carried),

time: 684 us -> 676 us (0.988)
  Pallas kernels: 567 us -> 558 us
    pallas_call x2, Pallas kernels: 200 us -> 192 us  [run_block_forward(): pl.pallas_call(functools.partial(block_forward, masked, pushed, layer ==...]
where the time goes in v6:
time: 676 us; the launch traced here: 672 us
  Pallas kernels  558 us (83%)
  local copies, waits for them, and re-layouts  48.6 us (7%)
  other arithmetic  21.9 us (3%)
  matrix products  17.7 us (3%)
  between operations  15 us (2%)
  waiting for transfers between devices  9.5 us (1%)
    pallas_call x2, Pallas kernels, run_block_forward(): pl.pallas_call(functools.partial(block_forward, masked, pushed, layer ==...  192 us
    pallas_call x2, Pallas kernels, run_attention_backward(): pl.pallas_call(functools.partial(attention_backward, pushed), grid=(windo...  179 us
    pallas_call x2, Pallas kernels, run_feed_backward(): pl.pallas_call(feed_backward, grid=(windows // count,), in_specs=[grid_bl...  95.9 us
    pallas_call x1, Pallas kernels, run_fold_gradients(): pl.pallas_call(fold_gradients, in_specs=[pl.BlockSpec(memory_space=pltpu....  68.9 us
    pallas_call x2, Pallas kernels, run_expand_bias(): pl.pallas_call(expand_bias, out_shape=jax.ShapeDtypeStruct((HEADS, WIN, W...  22.9 us
    dot_general x4, matrix products, dot(): return lax.dot_general(left, right, dims, preferred_element_type=F32)  17.7 us
    gather x1, local copies, waits for them, and re-layouts, per_device(): taken_rows = jnp.take(offset_index.reshape(-1), offset_places())  13.8 us
  transfers between devices with their start and end apart: 3, of which 1 were waited for; matrix products, arithmetic and copies ran while one was open for 8% of the time, Pallas kernels for 23%

profile of v6, /device:TPU:25, one launch (start us, length us, event | category | flops | bytes accessed | tf_op | source)
XLA Modules:
  0.0 672.3 jit_solution(5466908566034264397)
XLA Ops:
  10.8 1.3 constant_dynamic-update-slice_fusion.13
  14.6 1.5 bitcast_dynamic-update-slice_fusion
  17.7 5.4 fusion.46
  25.1 13.8 %gather_fusion = s32[2535]{0:T(1024)S(1)} fusion(s32[153664]{0:T(1024)S(1)} %reshape.260, s32[3072]{0:T(1024)S(1)} %pad_clamp_fusion), kind=kCustom, calls=%fused_computation | custom fusion | bytes 30420 | tf_op jit(solution)/shard_map/jit(_take)/gather | solution.py:1122
  39.0 5.0 fusion.8
  45.1 3.8 fusion.5
  50.4 11.6 %shard_map.352.refs_5_ = f32[16,392,392]{2,1,0:T(8,128)} custom-call(f32[128,1352]{1,0:T(8,128)} %get-tuple-element.104.cells_ref), custom_call_target="tpu_custom_call" | custom-call | tf_op jit(solution)/shard_map/pallas_call | solution.py:741
  62.0 11.3 %shard_map.354.refs_5_ = f32[16,392,392]{2,1,0:T(8,128)} custom-call(f32[128,1352]{1,0:T(8,128)} %get-tuple-element.103.cells_ref), custom_call_target="tpu_custom_call" | custom-call | tf_op jit(solution)/shard_map/pallas_call | solution.py:741
  73.4 1.6 select_convert_fusion
  75.0 2.5 fusion.12
  77.5 1.9 fusion.11
  79.6 2.8 fusion.10.grad_ref
  82.5 9.5 %all-gather.3.cloned.1.call-done = bf16[6656,512]{1,0:T(8,128)(2,1)} async-done(((bf16[208,512]{1,0:T(8,128)(2,1)}), bf16[6656,512]{1,0:T(8,128)(2,1)}) %all-gather.3.cloned.1.call-update) | async-done | bytes 6815760 | tf_op jit(solution)/shard_map/all_gather | solution.py:1100
  94.7 1.3 concatenate.61.refs_4_.vec_ref
  96.0 101.0 %shard_map.353 = (bf16[8,392,1536]{2,1,0:T(8,128)(2,1)}, bf16[8,16,392,392]{3,2,1,0:T(8,128)(2,1)}, f32[8,392,512]{2,1,0:T(8,128)}, bf16[8,392,512]{2,1,0:T(8,12...) custom-call(bf16[2,14,14,8,512]{4,3,2,1,0:T(8,128)(2,1)} %bitcast.16, ...), custom_call_target="tpu_custom_call" | custom-call | flops 20800000000 | tf_op jit(solution)/shard_map/pallas_call | solution.py:406
  198.2 90.7 %shard_map.355 = (bf16[8,392,1536]{2,1,0:T(8,128)(2,1)}, bf16[8,16,392,392]{3,2,1,0:T(8,128)(2,1)}, f32[8,392,512]{2,1,0:T(8,128)}, bf16[8,392,512]{2,1,0:T(8,12...) custom-call(f32[2,14,14,8,512]{4,3,2,1,0:T(8,128)} %get-tuple-elemen, ...), custom_call_target="tpu_custom_call" | custom-call | flops 20800000000 | tf_op jit(solution)/shard_map/pallas_call | solution.py:406
  288.9 48.1 %shard_map.356 = (f32[8,392,512]{2,1,0:T(8,128)}, bf16[8,392,512]{2,1,0:T(8,128)(2,1)}, bf16[32,192,512]{2,1,0:T(8,128)(2,1)}, f32[8,512]{1,0:T(8,128)}) custom-call(bf16[2,14,14,8,512]{4,3,2,1,0:T(8,128)(2,1)} %fusion.10.grad_ref, bf16[8,392,2048]{2,1,0:T(8,128)(2,1)} %get-tuple-element.55.act_ref, bf16[8,392,2048]{2,1,0:T(8,128)(2,1)} %get-tuple-element.56.slope_ref, ...), custom_call_target="tpu_custom_call" | custom-call | flops 11200000000 | tf_op jit(solution)/shard_map/pallas_call | solution.py:533
  337.1 94.5 %shard_map.357 = (f32[2,14,14,8,512]{4,3,2,1,0:T(8,128)}, bf16[32,192,512]{2,1,0:T(8,128)(2,1)}, f32[4,512]{1,0:T(4,128)}, f32[128,1352]{1,0:T(8,128)}) custom-call(bf16[32,192,512]{2,1,0:T(8,128)(2,1)} %get-tuple-element.59.whole_ref, f32[2,14,14,8,512]{4,3,2,1,0:T(8,128)} %get-tuple-element.52.refs_0_.x_ref, ...), custom_call_target="tpu_custom_call", output_to_operand_aliasing={{1}: (0, {})} | custom-call | flops 19200000000 | tf_op jit(solution)/shard_map/pallas_call | solution.py:680
  431.6 47.8 %shard_map.358 = (f32[8,392,512]{2,1,0:T(8,128)}, bf16[8,392,512]{2,1,0:T(8,128)(2,1)}, bf16[32,192,512]{2,1,0:T(8,128)(2,1)}, f32[8,512]{1,0:T(8,128)}) custom-call(f32[2,14,14,8,512]{4,3,2,1,0:T(8,128)} %get-tuple-element.65.grad_ref, bf16[8,392,2048]{2,1,0:T(8,128)(2,1)} %get-tuple-element.66.act_ref, bf16[8,392,2048]{2,1,0:T(8,128)(2,1)} %get-tuple-element.67.slope_ref, ...), custom_call_target="tpu_custom_call" | custom-call | flops 11200000000 | tf_op jit(solution)/shard_map/pallas_call | solution.py:533
  479.5 84.4 %shard_map.359 = (bf16[2,14,14,8,512]{4,3,2,1,0:T(8,128)(2,1)}, bf16[32,192,512]{2,1,0:T(8,128)(2,1)}, f32[4,512]{1,0:T(4,128)}, f32[128,1352]{1,0:T(8,128)}) custom-call(bf16[32,192,512]{2,1,0:T(8,128)(2,1)} %get-tuple-element.70.whole_ref, bf16[2,14,14,8,512]{4,3,2,1,0:T(8,128)(2,1)} %bitcast.167, ...), custom_call_target="tpu_custom_call", output_to_operand_aliasing={{1}: (0, {})} | custom-call | flops 19200000000 | tf_op jit(solution)/shard_map/pallas_call | solution.py:680
  566.5 3.7 fusion.4
  573.7 5.0 convert_bitcast_fusion
  578.8 68.9 %shard_map.360 = (f32[192,512]{1,0:T(8,128)}, f32[32,8,512]{2,1,0:T(8,128)}) custom-call(bf16[4,2,2,2,192,512]{5,4,3,2,1,0:T(8,128)(2,1)} %bitcast.164, f32[4,2,2,2,8,512]{5,4,3,2,1,0:T(8,128)} %reshape_reshape.3.refs_1_), custom_call_target="tpu_custom_call" | custom-call | flops 200000000 | tf_op jit(solution)/shard_map/pallas_call | solution.py:883
  655.1 5.2 fusion
  (166 shorter events, 34.8 us)
Async XLA Ops:
  7.2 84.8 %all-gather.3.cloned.1.call-start = ((), (), s32[]{:S(2)}) async-start(), calls=%async_computation.2 | async-start | bytes 7028736 | tf_op jit(solution)/shard_map/all_gather | solution.py:1100
  17.0 0.7 copy-start.4
  17.7 6.7 copy-start.1
  17.7 7.4 %copy-start.7 = (s32[2535]{0:T(1024)S(1)}, s32[2535]{0:T(1024)}, u32[]{:S(2)}) copy-start(s32[2535]{0:T(1024)} %constant.160) | copy-start | bytes 30424
  17.7 561.1 %reduce-scatter.2.cloned.1.call-start = ((), (), s32[]{:S(2)}) async-start(), calls=%async_computation.1 | async-start | bytes 6488064 | tf_op jit(solution)/shard_map/reduce_scatter | solution.py:1161
  23.1 51.9 %collective-permute-start = (bf16[2,4,14,14,512]{4,1,3,2,0:T(4,128)(2,1)}, bf16[2,4,14,14,512]{4,1,3,2,0:T(4,128)(2,1)}, u32[]{:S(2)}, u32[]{:S(2)}) collective-permute-start(bf16[2,4,14,14,512]{4,1,3,2,0:T(4,128)(2,1)} %get-tuple-element.91), channel_id=1, source_target_pairs={{0,1},{1,0},{2,3},{3,2},{4,5},{5,4},{6,7},{7,6},{8,9},{9,8},{10,11... | collective-permute-start | bytes 4816904 | tf_op jit(solution)/shard_map/ppermute | solution.py:966
  25.1 13.8 %copy-start.3 = (f32[2,2535,16]{1,2,0:T(8,128)S(1)}, f32[2,2535,16]{1,2,0:T(8,128)}, u32[]{:S(2)}) copy-start(f32[2,2535,16]{1,2,0:T(8,128)} %param.40) | copy-start | bytes 973444
  38.9 5.1 copy-start.8
  44.0 1.1 copy-start.18
  61.9 11.4 %copy-start.17 = (pred[392]{0:T(512)(128)(4,1)S(1)}, pred[392]{0:T(512)(128)(4,1)}, u32[]{:S(2)}) copy-start(pred[392]{0:T(512)(128)(4,1)} %constant.112.clone) | copy-start | bytes 1180
  61.9 11.4 %copy-start.11 = (s32[392]{0:T(512)S(1)}, s32[392]{0:T(512)}, u32[]{:S(2)}) copy-start(s32[392]{0:T(512)} %constant.158) | copy-start | bytes 4708
  61.9 11.4 %copy-start.12 = (s32[392]{0:T(512)S(1)}, s32[392]{0:T(512)}, u32[]{:S(2)}) copy-start(s32[392]{0:T(512)} %constant.157) | copy-start | bytes 4708
  61.9 11.5 %copy-start.13 = (s32[128]{0:T(128)S(1)}, s32[128]{0:T(128)}, u32[]{:S(2)}) copy-start(s32[128]{0:T(128)} %constant.115.clone) | copy-start | bytes 1540
  62.0 11.5 %copy-start.14 = (pred[128]{0:T(512)(128)(4,1)S(1)}, pred[128]{0:T(512)(128)(4,1)}, u32[]{:S(2)}) copy-start(pred[128]{0:T(512)(128)(4,1)} %constant.117.clone) | copy-start | bytes 388
  62.0 11.5 %copy-start.15 = (pred[128]{0:T(512)(128)(4,1)S(1)}, pred[128]{0:T(512)(128)(4,1)}, u32[]{:S(2)}) copy-start(pred[128]{0:T(512)(128)(4,1)} %constant.116.clone) | copy-start | bytes 388
  62.0 11.5 %copy-start.16 = (f32[128]{0:T(128)S(1)}, f32[128]{0:T(128)}, u32[]{:S(2)}) copy-start(f32[128]{0:T(128)} %constant.118.clone) | copy-start | bytes 1540
  431.6 47.8 %copy-start.5 = (f32[8,512]{1,0:T(8,128)S(1)}, f32[8,512]{1,0:T(8,128)}, u32[]{:S(2)}) copy-start(f32[8,512]{1,0:T(8,128)} %get-tuple-element.85) | copy-start | bytes 49156
  431.6 47.8 %copy-start.10 = (f32[4,512]{1,0:T(4,128)S(1)}, f32[4,512]{1,0:T(4,128)}, u32[]{:S(2)}) copy-start(f32[4,512]{1,0:T(4,128)} %get-tuple-element.84) | copy-start | bytes 24580
  479.4 84.4 %copy-start.6 = (f32[8,512]{1,0:T(8,128)S(1)}, f32[8,512]{1,0:T(8,128)}, u32[]{:S(2)}) copy-start(f32[8,512]{1,0:T(8,128)} %get-tuple-element.83) | copy-start | bytes 49156
  479.4 85.1 %copy-start.2 = (f32[128,1352]{1,0:T(8,128)S(1)}, f32[128,1352]{1,0:T(8,128)}, u32[]{:S(2)}) copy-start(f32[128,1352]{1,0:T(8,128)} %get-tuple-element.81) | copy-start | bytes 2076676
  565.8 0.7 copy-start.19
  578.8 70.2 %copy-start = (bf16[1,192,512]{2,1,0:T(8,128)(2,1)S(1)}, bf16[1,192,512]{2,1,0:T(8,128)(2,1)}, u32[]{:S(2)}) copy-start(bf16[1,192,512]{2,1,0:T(8,128)(2,1)} %reduce-scatter.2.cloned.1.call-done) | copy-start | bytes 589828
  647.6 7.4 %copy-start.9 = (s32[2535]{0:T(1024)S(1)}, s32[2535]{0:T(1024)}, u32[]{:S(2)}) copy-start(s32[2535]{0:T(1024)} %copy-done.8) | copy-start | bytes 30424
Sparse Core Ops, SparseCore 0:
  17.8 74.1 all-gather.2
  431.7 113.1 reduce-scatter.1
